TPU v7x, 32 devices: a whole 2x2x4 slice. The times are simulated.
32 devices in a mesh: dp: 8 (over y, x, core), tensor: 4 (over z).
Axes of the slice: x: 2, y: 2, z: 4, core: 2. Of those that a mesh axis runs over, the one named last changes fastest.
Arguments:
- tokens: bfloat16 [8192, 3072], P('dp', 'tensor'), may hold values from -6 to 6
- cotangent: bfloat16 [8192, 3072], P('dp', 'tensor'), may hold values from -24 to 24
- codes: int32 [8192, 12288], P('dp', 'tensor'), may hold values from -127 to 127
- row_scale: float32 [8192], P('dp'), may hold values from 0.004 to 0.04
- probe: bfloat16 [3072, 12288], P('dp', 'tensor'), may hold values from -6 to 6
- down_weight: bfloat16 [12288, 3072], P(('tensor', 'dp')), may hold values from -0.0546875 to 0.0546875
Outputs:
- diag_estimate: float32 [3072, 12288], P('dp', 'tensor')
All inputs are finite; a program needn't handle non-finite values.
Results may differ from a plain program's by a relative error of at most 0.003.
Values may be sent and summed in bfloat16 or wider, within the bound.
No kernel may reach another device: no remote copies, remote signals or barrier semaphores. Data moves between devices by JAX's collectives and lax.ppermute only.
A program may use at most 192 MiB of HBM per device.

v0:
```python
import math

import jax
import jax.numpy as jnp
from jax import lax
from jax.sharding import PartitionSpec as P

inv_root = 1.0 / math.sqrt(2.0 * math.pi)


def shards(tokens, cotangent, codes, row_scale, probe, down_weight):
    tok_full, cot_full = (
        lax.all_gather(tokens, "tensor", axis=1, tiled=True),
        lax.all_gather(cotangent, "tensor", axis=1, tiled=True),
    )
    tok_rows = tokens.shape[0]
    token_total = tok_rows * lax.axis_size("dp")
    active = codes.astype(jnp.float32) * row_scale[:, None]
    density = jnp.exp(-0.5 * active * active) * inv_root
    curvature = density * (2.0 - active * active)
    columns = tok_full
    tangent = jnp.dot(
        columns, lax.all_gather(probe, "dp", axis=0, tiled=True), preferred_element_type=jnp.float32
    )
    backward = lax.dot_general(
        cot_full,
        lax.all_gather(down_weight, "dp", axis=0, tiled=True),
        (((1,), (1,)), ((), ())),
        preferred_element_type=jnp.float32,
    )
    mixed_term = (backward * curvature * tangent).astype(jnp.bfloat16)
    columns = tok_full
    hessian = lax.psum_scatter(
        lax.dot_general(
            columns, mixed_term, (((0,), (0,)), ((), ())), preferred_element_type=jnp.float32
        ),
        "dp",
        scatter_dimension=0,
        tiled=True,
    )
    return probe.astype(jnp.float32) * hessian * (1.0 / token_total)


def solution(mesh):
    placed = (
        P("dp", "tensor"),
        P("dp", "tensor"),
        P("dp", "tensor"),
        P("dp"),
        P("dp", "tensor"),
        P(("tensor", "dp"), None),
    )
    return jax.shard_map(
        shards, mesh=mesh, in_specs=placed, out_specs=P("dp", "tensor"), check_vma=False
    )
```

profile of v0, /device:TPU:0, one launch (start us, length us, event | category | flops | bytes accessed | tf_op | source)
XLA Modules:
  0.0 744.4 jit_solution(16177659318637663670)
XLA Ops:
  6.5 0.0 all-gather.5.cloned.1.call-start
  6.5 0.7 all-gather.5.cloned.1.call-update
  7.3 0.0 all-gather.7.cloned.1.call-start
  7.3 0.7 all-gather.7.cloned.1.call-update
  8.0 0.0 all-gather.9.cloned.1.call-start
  8.1 0.7 all-gather.9.cloned.1.call-update
  8.7 0.0 all-gather.11.cloned.1.call-start
  8.8 0.5 all-gather.11.cloned.1.call-update
  9.3 0.0 copy-start.2
  9.3 0.0 reduce-scatter.2.cloned.1.call-start
  9.4 117.6 %all-gather.5.cloned.1.call-done = bf16[1024,3072]{1,0:T(8,128)(2,1)} async-done(((bf16[1024,768]{1,0:T(8,128)(2,1)}), bf16[1024,3072]{1,0:T(8,128)(2,1)}) %all-gather.5.cloned.1.call-update) | async-done | bytes 6291472 | tf_op jit(solution)/shard_map/all_gather | solution.py:14
  127.0 98.8 %all-gather.7.cloned.1.call-done = bf16[3072,3072]{1,0:T(8,128)(2,1)} async-done(((bf16[384,3072]{1,0:T(8,128)(2,1)}), bf16[3072,3072]{1,0:T(8,128)(2,1)}) %all-gather.7.cloned.1.call-update) | async-done | bytes 18874384 | tf_op jit(solution)/shard_map/all_gather | solution.py:27
  225.8 26.2 %fusion.9 = f32[1024,3072]{1,0:T(8,128)} fusion(bf16[1024,3072]{1,0:T(8,128)(2,1)} %all-gather.5.cloned.1.call-done, bf16[3072,3072]{1,0:T(8,128)(2,1)} %all-gather.7.cloned.1.call-done), kind=kOutput, calls=%fused_computation.12 | convolution fusion | flops 19327352832 | bytes 37748736 | tf_op jit(solution)/shard_map/dot_general | solution.py:25
  252.1 90.7 %all-gather.9.cloned.1.call-done = bf16[1024,3072]{1,0:T(8,128)(2,1)} async-done(((bf16[1024,768]{1,0:T(8,128)(2,1)}), bf16[1024,3072]{1,0:T(8,128)(2,1)}) %all-gather.9.cloned.1.call-update) | async-done | bytes 6291472 | tf_op jit(solution)/shard_map/all_gather | solution.py:13
  342.8 98.7 %all-gather.11.cloned.1.call-done = bf16[3072,3072]{1,0:T(8,128)(2,1)} async-done(((bf16[384,3072]{1,0:T(8,128)(2,1)}), bf16[3072,3072]{1,0:T(8,128)(2,1)}) %all-gather.11.cloned.1.call-update) | async-done | bytes 18874384 | tf_op jit(solution)/shard_map/all_gather | solution.py:23
  441.5 0.0 copy-done.2
  441.5 32.7 %fusion.5.clone.4 = bf16[1024,3072]{1,0:T(8,128)(2,1)} fusion(f32[1024,3072]{1,0:T(8,128)} %fusion.9, s32[1024,3072]{1,0:T(8,128)} %param.8, bf16[1024,3072]{1,0:T(8,128)(2,1)} %all-gather.9.cloned.1.call-done, bf16[3072,3072]{1,0:T(8,128)(2,1)} %all-gather.11.cloned.1.call-done, f32[1024]{0:T(1024)S(1)} %copy-done.2), kind=kOutput, calls=%fused_computation.7.clone.clone.clone.1 | convolution fusion | flops 19361955840 | bytes 56627200 | tf_op jit(solution)/shard_map/dot_general | solution.py:22
  474.2 26.4 %convolution_bitcast_fusion = f32[3072,3072]{0,1:T(8,128)} fusion(bf16[1024,3072]{1,0:T(8,128)(2,1)S(1)} %copy-done.1, bf16[1024,3072]{1,0:T(8,128)(2,1)} %fusion.5.clone.4), kind=kOutput, calls=%fused_computation | convolution fusion | flops 19327352832 | bytes 50331648 | tf_op jit(solution)/shard_map/dot_general | solution.py:34
  500.6 0.0 reduce-scatter.2.cloned.1.call-update
  500.6 1.6 copy-done
  502.2 2.4 copy.7
  504.7 221.4 %reduce-scatter.2.cloned.1.call-done = f32[384,3072]{0,1:T(8,128)} async-done(((f32[3072,3072]{0,1:T(8,128)}), f32[384,3072]{0,1:T(8,128)}) %reduce-scatter.2.cloned.1.call-update) | async-done | bytes 4718608 | tf_op jit(solution)/shard_map/reduce_scatter | solution.py:33
  726.1 5.7 multiply_multiply_fusion.1
  731.8 6.0 copy.8
  (3 shorter events, 0.0 us)
Async XLA Ops:
  6.5 120.5 %all-gather.5.cloned.1.call-start = ((), (), s32[]{:S(2)}) async-start(), calls=%async_computation.1 | async-start | bytes 7864320 | tf_op jit(solution)/shard_map/all_gather | solution.py:14
  7.3 218.6 %all-gather.7.cloned.1.call-start = ((), (), s32[]{:S(2)}) async-start(), calls=%async_computation.2 | async-start | bytes 21233664 | tf_op jit(solution)/shard_map/all_gather | solution.py:27
  8.0 334.8 %all-gather.9.cloned.1.call-start = ((), (), s32[]{:S(2)}) async-start(), calls=%async_computation.3 | async-start | bytes 7864320 | tf_op jit(solution)/shard_map/all_gather | solution.py:13
  8.7 432.8 %all-gather.11.cloned.1.call-start = ((), (), s32[]{:S(2)}) async-start(), calls=%async_computation.4 | async-start | bytes 21233664 | tf_op jit(solution)/shard_map/all_gather | solution.py:23
  9.3 432.2 %copy-start.2 = (f32[1024]{0:T(1024)S(1)}, f32[1024]{0:T(1024)}, u32[]{:S(2)}) copy-start(f32[1024]{0:T(1024)} %param.9) | copy-start | bytes 12292
  9.3 716.8 %reduce-scatter.2.cloned.1.call-start = ((), (), s32[]{:S(2)}) async-start(), calls=%async_computation.5 | async-start | bytes 42467328 | tf_op jit(solution)/shard_map/reduce_scatter | solution.py:33
  441.5 32.7 %copy-start.1 = (bf16[1024,3072]{1,0:T(8,128)(2,1)S(1)}, bf16[1024,3072]{1,0:T(8,128)(2,1)}, u32[]{:S(2)}) copy-start(bf16[1024,3072]{1,0:T(8,128)(2,1)} %all-gather.9.cloned.1.call-done) | copy-start | bytes 18874372
  500.6 1.7 copy-start
Sparse Core Ops, SparseCore 0:
  8.9 118.0 all-gather.4
  128.9 96.9 all-gather.6
  227.4 115.3 all-gather.8
  344.5 96.9 all-gather.10
  500.7 225.3 reduce-scatter.1
where the time goes:
time: 745 us; the launch traced here: 744 us
  waiting for transfers between devices  630 us (85%)
  matrix products  85.3 us (11%)
  between operations  13.2 us (2%)
  local copies, waits for them, and re-layouts  10.1 us (1%)
    reduce_scatter x1, waiting for transfers between devices, shards(): lax.psum_scatter(lax.dot_general(columns, mixed_term, (((0,), (0,)), ((),...  221 us
    all_gather x1, waiting for transfers between devices, shards(): lax.all_gather(cotangent, 'tensor', axis=1, tiled=True)  118 us
    all_gather x1, waiting for transfers between devices, shards(): lax.all_gather(down_weight, 'dp', axis=0, tiled=True)  98.8 us
    all_gather x1, waiting for transfers between devices, shards(): lax.all_gather(probe, 'dp', axis=0, tiled=True)  98.7 us
    all_gather x1, waiting for transfers between devices, shards(): lax.all_gather(tokens, 'tensor', axis=1, tiled=True)  90.7 us
    dot_general x1, matrix products, shards(): jnp.dot(columns, lax.all_gather(probe, 'dp', axis=0, tiled=True), preferr...  32.7 us
    dot_general x1, matrix products, shards(): lax.dot_general(columns, mixed_term, (((0,), (0,)), ((), ())), preferred_...  26.4 us
    dot_general x1, matrix products, shards(): lax.dot_general(cot_full, lax.all_gather(down_weight, 'dp', axis=0, tiled...  26.2 us
  transfers between devices with their start and end apart: 5, of which 5 were waited for; matrix products, arithmetic and copies ran while one was open for 4% of the time, Pallas kernels for 0%

commit v1 on v0

v1 whole, which is shorter than its diff:
```python
import math

import jax
import jax.numpy as jnp
from jax import lax
from jax.sharding import PartitionSpec as P

inv_root = 1.0 / math.sqrt(2.0 * math.pi)
chunks = 4
f32 = jnp.float32
bf16 = jnp.bfloat16


def folded(n):
    return [0] + list(range(1, n, 2)) + list(range(n - 2 + n % 2, 0, -2)) if n > 1 else [0]


def shift(n, stride, total, by):
    pairs = []
    for i in range(total):
        digit = (i // stride) % n
        pairs.append((i, i + (((digit + by) % n) - digit) * stride))
    return pairs


def ring_gather(block, order, starts):
    n = len(order)
    pairs = [(order[i], order[(i + 1) % n]) for i in range(n)]
    full = jnp.zeros((block.shape[0], block.shape[1] * n), block.dtype)
    held = block
    full = lax.dynamic_update_slice(full, held, (0, starts[0]))
    for step in range(1, n):
        held = lax.ppermute(held, "tensor", pairs)
        full = lax.dynamic_update_slice(full, held, (0, starts[step]))
    return full


def reduce_over(parts, dim, n, stride, total, digit):
    own = lax.dynamic_index_in_dim(parts, digit, dim, keepdims=True)
    for by in range(1, n):
        send = lax.dynamic_index_in_dim(parts, lax.rem(digit + by, n), dim, keepdims=True).astype(bf16)
        own = own + lax.ppermute(send, "dp", shift(n, stride, total, by)).astype(f32)
    return own


def shards(tokens, cotangent, codes, row_scale, probe, down_weight):
    dp, tp = lax.axis_size("dp"), lax.axis_size("tensor")
    cores, xs = 2, 2
    ys = dp // (cores * xs)
    me = lax.axis_index("dp")
    core, x, y = lax.rem(me, cores), lax.rem(lax.div(me, cores), xs), lax.div(me, cores * xs)
    tok_rows = tokens.shape[0]
    rows, hidden = probe.shape
    order = folded(tp)
    width = tokens.shape[1]
    table = [[width * order[(order.index(i) - s) % tp] for s in range(tp)] for i in range(tp)]
    starts = lax.dynamic_index_in_dim(
        jnp.array(table, jnp.int32), lax.axis_index("tensor"), 0, keepdims=False
    )
    wide = hidden // chunks

    cot_full = ring_gather(cotangent, order, starts)
    tok_full = ring_gather(tokens, order, starts)
    down_full = lax.all_gather(down_weight, "dp", axis=0, tiled=True)
    active = codes.astype(f32) * row_scale[:, None]
    curvature = jnp.exp(-0.5 * active * active) * inv_root * (2.0 - active * active)
    backward = lax.dot_general(
        cot_full, down_full, (((1,), (1,)), ((), ())), preferred_element_type=f32
    )
    bent = backward * curvature

    by_core = tok_full.reshape(tok_rows, ys * xs, cores, rows)
    mine = lax.dynamic_index_in_dim(by_core, core, 2, keepdims=False).reshape(tok_rows, -1)
    other = lax.dynamic_index_in_dim(by_core, 1 - core, 2, keepdims=False).reshape(tok_rows, -1)

    pieces = []
    for j in range(chunks):
        cut = slice(j * wide, (j + 1) * wide)
        probe_full = lax.all_gather(probe[:, cut], "dp", axis=0, tiled=True)
        tangent = jnp.dot(tok_full, probe_full, preferred_element_type=f32)
        mixed = (bent[:, cut] * tangent).astype(bf16)
        away = lax.dot_general(other, mixed, (((0,), (0,)), ((), ())), preferred_element_type=f32)
        came = lax.ppermute(away.astype(bf16), "dp", shift(cores, 1, dp, 1))
        kept = lax.dot_general(mine, mixed, (((0,), (0,)), ((), ())), preferred_element_type=f32)
        chip = (kept + came.astype(f32)).reshape(ys, xs, rows, wide)
        half = wide // 2
        first, second = chip[..., :half], chip[..., half:]
        first = reduce_over(first, 1, xs, cores, dp, x)
        first = reduce_over(first, 0, ys, cores * xs, dp, y)
        second = reduce_over(second, 0, ys, cores * xs, dp, y)
        second = reduce_over(second, 1, xs, cores, dp, x)
        pieces += [first.reshape(rows, half), second.reshape(rows, half)]
    hessian = jnp.concatenate(pieces, axis=1)
    return probe.astype(f32) * hessian * (1.0 / (tok_rows * dp))


def solution(mesh):
    placed = (
        P("dp", "tensor"),
        P("dp", "tensor"),
        P("dp", "tensor"),
        P("dp"),
        P("dp", "tensor"),
        P(("tensor", "dp"), None),
    )
    return jax.shard_map(
        shards, mesh=mesh, in_specs=placed, out_specs=P("dp", "tensor"), check_vma=False
    )
```

time: 745 us -> 447 us (0.60)
  waiting for transfers between devices: 630 us -> 178 us
  local copies, waits for them, and re-layouts: 10.1 us -> 91.1 us
  starting transfers between devices: 0.15 us -> 32.3 us
  matrix products: 85.3 us -> 113 us
  between operations: 13.2 us -> 21.2 us
    all_gather x4 -> x5, waiting for transfers between devices: 406 us -> 0.01 us  [the longest x4 0.01 us: shards(): probe_full = lax.all_gather(probe[:, cut], 'dp', axis=0, tiled=True)]
    reduce_scatter x1 -> x0, waiting for transfers between devices: 221 us -> none  [shards(): lax.psum_scatter(lax.dot_general(columns, mixed_term, (((0,), (0,)), ((),...]
    ppermute x0 -> x26, waiting for transfers between devices: none -> 176 us  [the longest x6 129 us: ring_gather(): held = lax.ppermute(held, 'tensor', pairs)]
    dynamic_update_slice x0 -> x8, local copies, waits for them, and re-layouts: none -> 68.4 us  [the longest x6 51.4 us: ring_gather(): full = lax.dynamic_update_slice(full, held, (0, starts[step]))]
    ppermute x0 -> x26, starting transfers between devices: none -> 32.2 us  [the longest x16 20.9 us: reduce_over(): lax.ppermute(send, 'dp', shift(n, stride, total, by)).astype(f32)]
    dot_general x3 -> x13, matrix products: 85.3 us -> 113 us  [the longest x4 45.7 us: shards(): tangent = jnp.dot(tok_full, probe_full, preferred_element_type=f32)]
  transfers between devices with their start and end apart: 5 -> 31, of which waited for: 5 -> 13; matrix products, arithmetic and copies ran while one was open for 4% -> 41% of each run, Pallas kernels for 0% -> 0%
where the time goes in v1:
time: 447 us; the launch traced here: 441 us
  waiting for transfers between devices  178 us (40%)
  matrix products  113 us (25%)
  local copies, waits for them, and re-layouts  91.1 us (20%)
  starting transfers between devices  32.3 us (7%)
  between operations  21.2 us (5%)
  other arithmetic  4.81 us (1%)
    ppermute x6, waiting for transfers between devices, ring_gather(): held = lax.ppermute(held, 'tensor', pairs)  129 us
    dynamic_update_slice x6, local copies, waits for them, and re-layouts, ring_gather(): full = lax.dynamic_update_slice(full, held, (0, starts[step]))  51.4 us
    ppermute x16, waiting for transfers between devices, reduce_over(): lax.ppermute(send, 'dp', shift(n, stride, total, by)).astype(f32)  47.6 us
    dot_general x4, matrix products, shards(): tangent = jnp.dot(tok_full, probe_full, preferred_element_type=f32)  45.7 us
    dot_general x1, matrix products, shards(): lax.dot_general(cot_full, down_full, (((1,), (1,)), ((), ())), preferred_...  31.7 us
    dot_general x4, matrix products, shards(): lax.dot_general(other, mixed, (((0,), (0,)), ((), ())), preferred_element...  23.3 us
    ppermute x16, starting transfers between devices, reduce_over(): lax.ppermute(send, 'dp', shift(n, stride, total, by)).astype(f32)  20.9 us
    dynamic_update_slice x2, local copies, waits for them, and re-layouts, ring_gather(): full = lax.dynamic_update_slice(full, held, (0, starts[0]))  17 us
  transfers between devices with their start and end apart: 31, of which 13 were waited for; matrix products, arithmetic and copies ran while one was open for 41% of the time, Pallas kernels for 0%

profile of v1, /device:TPU:0, one launch (start us, length us, event | category | flops | bytes accessed | tf_op | source)
XLA Modules:
  0.0 440.5 jit_solution(16190941481231905520)
XLA Ops:
  19.9 32.0 %collective-permute-done = bf16[1024,768]{0,1:T(8,128)(2,1)} collective-permute-done((bf16[1024,768]{0,1:T(8,128)(2,1)S(1)}, bf16[1024,768]{0,1:T(8,128)(2,1)}, u32[]{:S(2)}, u32[]{:S(2)}) %collective-permute-start) | collective-permute-done | bytes 1572896 | tf_op jit(solution)/shard_map/ppermute | solution.py:33
  52.9 32.6 %collective-permute-done.3 = bf16[1024,768]{0,1:T(8,128)(2,1)S(1)} collective-permute-done((bf16[1024,768]{0,1:T(8,128)(2,1)S(1)}, bf16[1024,768]{0,1:T(8,128)(2,1)S(1)}, u32[]{:S(2)}, u32[]{:S(2)}) %collective-permute-start.3) | collective-permute-done | bytes 1572896 | tf_op jit(solution)/shard_map/ppermute | solution.py:33
  87.8 31.5 %collective-permute-done.1 = bf16[1024,768]{0,1:T(8,128)(2,1)} collective-permute-done((bf16[1024,768]{0,1:T(8,128)(2,1)}, bf16[1024,768]{0,1:T(8,128)(2,1)}, u32[]{:S(2)}, u32[]{:S(2)}) %collective-permute-start.1) | collective-permute-done | bytes 1572896 | tf_op jit(solution)/shard_map/ppermute | solution.py:33
  120.5 32.6 %collective-permute-done.4 = bf16[1024,768]{0,1:T(8,128)(2,1)} collective-permute-done((bf16[1024,768]{0,1:T(8,128)(2,1)S(1)}, bf16[1024,768]{0,1:T(8,128)(2,1)}, u32[]{:S(2)}, u32[]{:S(2)}) %collective-permute-start.4) | collective-permute-done | bytes 1572896 | tf_op jit(solution)/shard_map/ppermute | solution.py:33
  164.6 8.4 %dynamic_update_slice.24 = bf16[1024,3072]{0,1:T(8,128)(2,1)} dynamic-update-slice(bf16[1024,3072]{0,1:T(8,128)(2,1)} %broadcast.8.clone, bf16[1024,768]{0,1:T(8,128)(2,1)S(1)} %copy.8, s32[]{:T(128)} %constant.114.clone.1, s32[]{:T(128)S(6)} %select_n.72) | dynamic-update-slice | bytes 3145732 | tf_op jit(solution)/shard_map/dynamic_update_slice | solution.py:31
  176.4 8.6 %dynamic_update_slice.28 = bf16[1024,3072]{0,1:T(8,128)(2,1)} dynamic-update-slice(bf16[1024,3072]{0,1:T(8,128)(2,1)} %broadcast.8.clone.1, bf16[1024,768]{0,1:T(8,128)(2,1)S(1)} %copy.10, s32[]{:T(128)} %constant.114.clone.1, s32[]{:T(128)S(6)} %select_n.72) | dynamic-update-slice | bytes 3145732 | tf_op jit(solution)/shard_map/dynamic_update_slice | solution.py:31
  186.7 8.8 %dynamic_update_slice.25 = bf16[1024,3072]{0,1:T(8,128)(2,1)} dynamic-update-slice(bf16[1024,3072]{0,1:T(8,128)(2,1)} %dynamic_update_slice.24, bf16[1024,768]{0,1:T(8,128)(2,1)} %collective-permute-done, s32[]{:T(128)} %constant.114.clone.1, s32[]{:T(128)S(6)} %select_n.73) | dynamic-update-slice | bytes 3145732 | tf_op jit(solution)/shard_map/dynamic_update_slice | solution.py:34
  195.6 8.4 %dynamic_update_slice.29 = bf16[1024,3072]{0,1:T(8,128)(2,1)} dynamic-update-slice(bf16[1024,3072]{0,1:T(8,128)(2,1)} %dynamic_update_slice.28, bf16[1024,768]{0,1:T(8,128)(2,1)S(1)} %copy-done.5, s32[]{:T(128)} %constant.114.clone.1, s32[]{:T(128)S(6)} %select_n.73) | dynamic-update-slice | bytes 3145732 | tf_op jit(solution)/shard_map/dynamic_update_slice | solution.py:34
  204.0 8.3 %dynamic_update_slice.26 = bf16[1024,3072]{0,1:T(8,128)(2,1)} dynamic-update-slice(bf16[1024,3072]{0,1:T(8,128)(2,1)} %dynamic_update_slice.25, bf16[1024,768]{0,1:T(8,128)(2,1)} %collective-permute-done.1, s32[]{:T(128)} %constant.114.clone.1, s32[]{:T(128)S(6)} %select_n.74) | dynamic-update-slice | bytes 3145732 | tf_op jit(solution)/shard_map/dynamic_update_slice | solution.py:34
  212.3 8.3 %dynamic_update_slice.30 = bf16[1024,3072]{0,1:T(8,128)(2,1)} dynamic-update-slice(bf16[1024,3072]{0,1:T(8,128)(2,1)} %dynamic_update_slice.29, bf16[1024,768]{0,1:T(8,128)(2,1)} %collective-permute-done.4, s32[]{:T(128)} %constant.114.clone.1, s32[]{:T(128)S(6)} %select_n.74) | dynamic-update-slice | bytes 3145732 | tf_op jit(solution)/shard_map/dynamic_update_slice | solution.py:34
  220.6 8.8 %dynamic_update_slice.27 = bf16[1024,3072]{0,1:T(8,128)(2,1)} dynamic-update-slice(bf16[1024,3072]{0,1:T(8,128)(2,1)} %dynamic_update_slice.26, bf16[1024,768]{0,1:T(8,128)(2,1)} %collective-permute-done.2, s32[]{:T(128)} %constant.114.clone.1, s32[]{:T(128)S(6)} %select_n.75) | dynamic-update-slice | bytes 3145732 | tf_op jit(solution)/shard_map/dynamic_update_slice | solution.py:34
  229.4 5.6 %constant_dynamic-slice_fusion.1 = (bf16[1024,4,1,384]{0,3,2,1:T(8,128)(2,1)S(1)}, bf16[1024,4,1,384]{0,3,2,1:T(8,128)(2,1)}) fusion(bf16[1024,4,2,384]{0,3,2,1:T(8,128)(2,1)} %bitcast.53, s32[]{:T(128)S(6)} %select_n.76, s32[]{:T(128)S(6)} %select_n.77), kind=kLoop, calls=%fused_computation.55 | loop fusion | bytes 12582920 | tf_op jit(solution)/shard_map/jit(dynamic_index_in_dim)/dynamic_slice | solution.py:73
  234.9 8.8 %dynamic_update_slice.31 = bf16[1024,3072]{0,1:T(8,128)(2,1)} dynamic-update-slice(bf16[1024,3072]{0,1:T(8,128)(2,1)} %dynamic_update_slice.30, bf16[1024,768]{0,1:T(8,128)(2,1)} %collective-permute-done.5, s32[]{:T(128)} %constant.114.clone.1, s32[]{:T(128)S(6)} %select_n.75) | dynamic-update-slice | bytes 3145732 | tf_op jit(solution)/shard_map/dynamic_update_slice | solution.py:34
  243.7 9.8 %fusion.16 = f32[1024,768]{1,0:T(8,128)} fusion(bf16[1024,3072]{0,1:T(8,128)(2,1)} %dynamic_update_slice.27, bf16[3072,768]{1,0:T(8,128)(2,1)} %all-gather.12.cloned.1.call-done), kind=kOutput, calls=%fused_computation.65 | convolution fusion | flops 4831838208 | bytes 14155776 | tf_op jit(solution)/shard_map/dot_general | solution.py:80
  253.5 9.8 %fusion.15 = f32[1024,768]{1,0:T(8,128)} fusion(bf16[1024,3072]{0,1:T(8,128)(2,1)} %dynamic_update_slice.27, bf16[3072,768]{1,0:T(8,128)(2,1)} %all-gather.10.cloned.1.call-done), kind=kOutput, calls=%fused_computation.64 | convolution fusion | flops 4831838208 | bytes 14155776 | tf_op jit(solution)/shard_map/dot_general | solution.py:80
  263.3 9.9 %fusion.14 = f32[1024,768]{1,0:T(8,128)} fusion(bf16[1024,3072]{0,1:T(8,128)(2,1)} %dynamic_update_slice.27, bf16[3072,768]{1,0:T(8,128)(2,1)} %all-gather.8.cloned.1.call-done), kind=kOutput, calls=%fused_computation.63 | convolution fusion | flops 4831838208 | bytes 14155776 | tf_op jit(solution)/shard_map/dot_general | solution.py:80
  273.2 31.7 %fusion.3 = f32[1024,3072]{1,0:T(8,128)} fusion(s32[1024,3072]{1,0:T(8,128)} %param.9, bf16[1024,3072]{0,1:T(8,128)(2,1)} %dynamic_update_slice.31, bf16[3072,3072]{1,0:T(8,128)(2,1)} %all-gather.6.cloned.1.call-done, f32[1024]{0:T(1024)S(1)} %copy-done.6), kind=kOutput, calls=%fused_computation.4 | convolution fusion | flops 19355664384 | bytes 50335744 | tf_op jit(solution)/shard_map/dot_general | solution.py:67
  304.9 16.2 %fusion.4 = (bf16[1024,768]{1,0:T(8,128)(2,1)}, bf16[1024,768]{1,0:T(8,128)(2,1)}, bf16[1024,768]{1,0:T(8,128)(2,1)}, bf16[1024,768]{1,0:T(8,128)(2,1)S(1)}) fusion(f32[1024,3072]{1,0:T(8,128)} %fusion.3, f32[1024,768]{1,0:T(8,128)} %fusion.16, f32[1024,768]{1,0:T(8,128)} %fusion.15, f32[1024,768]{1,0:T(8,128)} %fusion.14, ...), kind=kOutput, calls=%fused_computation.15 | convolution fusion | flops 4838129664 | bytes 39321600 | tf_op jit(solution)/shard_map/dot_general | solution.py:80
  325.0 5.1 %convolution_convert_fusion.2 = bf16[1536,768]{1,0:T(8,128)(2,1)S(1)} fusion(bf16[1024,1536]{0,1:T(8,128)(2,1)} %bitcast.62, bf16[1024,768]{1,0:T(8,128)(2,1)} %get-tuple-element.7), kind=kOutput, calls=%fused_computation.12 | convolution fusion | flops 2417098752 | bytes 7077888 | tf_op jit(solution)/shard_map/dot_general | solution.py:82
  333.7 11.5 %convolution_convert_fusion = bf16[1536,768]{1,0:T(8,128)(2,1)S(1)} fusion(bf16[1024,1536]{0,1:T(8,128)(2,1)S(1)} %bitcast.65, bf16[1024,768]{1,0:T(8,128)(2,1)S(1)} %copy-done.7), kind=kOutput, calls=%fused_computation.10 | convolution fusion | flops 2417098752 | bytes 7077888 | tf_op jit(solution)/shard_map/dot_general | solution.py:82
  368.7 10.7 %collective-permute-done.12 = bf16[2,1,384,384]{3,2,1,0:T(8,128)(2,1)S(1)} collective-permute-done((bf16[2,1,384,384]{3,2,1,0:T(8,128)(2,1)S(1)}, bf16[2,1,384,384]{3,2,1,0:T(8,128)(2,1)S(1)}, u32[]{:S(2)}, u32[]{:S(2)}) %collective-permute-start.12) | collective-permute-done | bytes 589856 | tf_op jit(solution)/shard_map/ppermute | solution.py:42
  383.8 8.2 %collective-permute-done.17 = bf16[2,1,384,384]{3,2,1,0:T(8,128)(2,1)S(1)} collective-permute-done((bf16[2,1,384,384]{3,2,1,0:T(8,128)(2,1)S(1)}, bf16[2,1,384,384]{3,2,1,0:T(8,128)(2,1)S(1)}, u32[]{:S(2)}, u32[]{:S(2)}) %collective-permute-start.17) | collective-permute-done | bytes 589856 | tf_op jit(solution)/shard_map/ppermute | solution.py:42
  395.6 9.0 %collective-permute-done.22 = bf16[2,1,384,384]{3,2,1,0:T(8,128)(2,1)S(1)} collective-permute-done((bf16[2,1,384,384]{3,2,1,0:T(8,128)(2,1)S(1)}, bf16[2,1,384,384]{3,2,1,0:T(8,128)(2,1)S(1)}, u32[]{:S(2)}, u32[]{:S(2)}) %collective-permute-start.22) | collective-permute-done | bytes 589856 | tf_op jit(solution)/shard_map/ppermute | solution.py:42
  419.7 5.7 %collective-permute-done.18 = bf16[1,1,384,384]{3,2,1,0:T(8,128)(2,1)S(1)} collective-permute-done((bf16[1,1,384,384]{3,2,1,0:T(8,128)(2,1)S(1)}, bf16[1,1,384,384]{3,2,1,0:T(8,128)(2,1)S(1)}, u32[]{:S(2)}, u32[]{:S(2)}) %collective-permute-start.18) | collective-permute-done | bytes 294944 | tf_op jit(solution)/shard_map/ppermute | solution.py:42
  (137 shorter events, 89.1 us)
Async XLA Ops:
  6.5 237.2 %all-gather.12.cloned.1.call-start = ((), (), s32[]{:S(2)}) async-start(), calls=%async_computation.3 | async-start | bytes 5308416 | tf_op jit(solution)/shard_map/all_gather | solution.py:79
  9.6 243.9 %all-gather.10.cloned.1.call-start = ((), (), s32[]{:S(2)}) async-start(), calls=%async_computation.2 | async-start | bytes 5308416 | tf_op jit(solution)/shard_map/all_gather | solution.py:79
  10.3 252.9 %all-gather.8.cloned.1.call-start = ((), (), s32[]{:S(2)}) async-start(), calls=%async_computation.1 | async-start | bytes 5308416 | tf_op jit(solution)/shard_map/all_gather | solution.py:79
  11.1 262.1 %all-gather.6.cloned.1.call-start = ((), (), s32[]{:S(2)}) async-start(), calls=%async_computation | async-start | bytes 21233664 | tf_op jit(solution)/shard_map/all_gather | solution.py:64
  11.7 293.3 %all-gather.14.cloned.1.call-start = ((), (), s32[]{:S(2)}) async-start(), calls=%async_computation.4 | async-start | bytes 5308416 | tf_op jit(solution)/shard_map/all_gather | solution.py:79
  12.5 39.4 %collective-permute-start = (bf16[1024,768]{0,1:T(8,128)(2,1)S(1)}, bf16[1024,768]{0,1:T(8,128)(2,1)}, u32[]{:S(2)}, u32[]{:S(2)}) collective-permute-start(bf16[1024,768]{0,1:T(8,128)(2,1)S(1)} %copy.8), channel_id=1, source_target_pairs={{0,1},{1,3},{3,2},{2,0},{4,5},{5,7},{7,6},{6,4},{8,9},{9,11},{11,1... | collective-permute-start | bytes 4718600 | tf_op jit(solution)/shard_map/ppermute | solution.py:33
  17.3 68.2 %collective-permute-start.3 = (bf16[1024,768]{0,1:T(8,128)(2,1)S(1)}, bf16[1024,768]{0,1:T(8,128)(2,1)S(1)}, u32[]{:S(2)}, u32[]{:S(2)}) collective-permute-start(bf16[1024,768]{0,1:T(8,128)(2,1)S(1)} %copy.10), channel_id=1, source_target_pairs={{0,1},{1,3},{3,2},{2,0},{4,5},{5,7},{7,6},{6,4},{8,9},{9,11},{11,1... | collective-permute-start | bytes 4718600 | tf_op jit(solution)/shard_map/ppermute | solution.py:33
  51.9 67.4 %collective-permute-start.1 = (bf16[1024,768]{0,1:T(8,128)(2,1)}, bf16[1024,768]{0,1:T(8,128)(2,1)}, u32[]{:S(2)}, u32[]{:S(2)}) collective-permute-start(bf16[1024,768]{0,1:T(8,128)(2,1)} %collective-permute-done), channel_id=1, source_target_pairs={{0,1},{1,3},{3,2},{2,0},{4,5},{5,7},{7,6},{6,4},{8,9},{9,11},{11,1... | collective-permute-start | bytes 4718600 | tf_op jit(solution)/shard_map/ppermute | solution.py:33
  86.6 66.4 %collective-permute-start.4 = (bf16[1024,768]{0,1:T(8,128)(2,1)S(1)}, bf16[1024,768]{0,1:T(8,128)(2,1)}, u32[]{:S(2)}, u32[]{:S(2)}) collective-permute-start(bf16[1024,768]{0,1:T(8,128)(2,1)S(1)} %collective-permute-done.3), channel_id=1, source_target_pairs={{0,1},{1,3},{3,2},{2,0},{4,5},{5,7},{7,6},{6,4},{8,9},{9,11},{11,1... | collective-permute-start | bytes 4718600 | tf_op jit(solution)/shard_map/ppermute | solution.py:33
  119.3 101.3 %collective-permute-start.2 = (bf16[1024,768]{0,1:T(8,128)(2,1)}, bf16[1024,768]{0,1:T(8,128)(2,1)}, u32[]{:S(2)}, u32[]{:S(2)}) collective-permute-start(bf16[1024,768]{0,1:T(8,128)(2,1)} %collective-permute-done.1), channel_id=1, source_target_pairs={{0,1},{1,3},{3,2},{2,0},{4,5},{5,7},{7,6},{6,4},{8,9},{9,11},{11,1... | collective-permute-start | bytes 4718600 | tf_op jit(solution)/shard_map/ppermute | solution.py:33
  153.0 81.9 %collective-permute-start.5 = (bf16[1024,768]{0,1:T(8,128)(2,1)}, bf16[1024,768]{0,1:T(8,128)(2,1)}, u32[]{:S(2)}, u32[]{:S(2)}) collective-permute-start(bf16[1024,768]{0,1:T(8,128)(2,1)} %collective-permute-done.4), channel_id=1, source_target_pairs={{0,1},{1,3},{3,2},{2,0},{4,5},{5,7},{7,6},{6,4},{8,9},{9,11},{11,1... | collective-permute-start | bytes 4718600 | tf_op jit(solution)/shard_map/ppermute | solution.py:33
  325.0 20.7 %collective-permute-start.6 = (bf16[1536,768]{1,0:T(8,128)(2,1)}, bf16[1536,768]{1,0:T(8,128)(2,1)}, u32[]{:S(2)}, u32[]{:S(2)}) collective-permute-start(bf16[1536,768]{1,0:T(8,128)(2,1)} %convolution_convert_fusion.3), channel_id=1, source_target_pairs={{0,4},{4,0},{8,12},{12,8},{16,20},{20,16},{24,28},{28,24},{1,5},{5... | collective-permute-start | bytes 7077896 | tf_op jit(solution)/shard_map/ppermute | solution.py:83
  330.2 23.8 %collective-permute-start.11 = (bf16[1536,768]{1,0:T(8,128)(2,1)S(1)}, bf16[1536,768]{1,0:T(8,128)(2,1)S(1)}, u32[]{:S(2)}, u32[]{:S(2)}) collective-permute-start(bf16[1536,768]{1,0:T(8,128)(2,1)S(1)} %convolution_convert_fusion.2), channel_id=1, source_target_pairs={{0,4},{4,0},{8,12},{12,8},{16,20},{20,16},{24,28},{28,24},{1,5},{5... | collective-permute-start | bytes 7077896 | tf_op jit(solution)/shard_map/ppermute | solution.py:83
  333.5 24.1 %collective-permute-start.16 = (bf16[1536,768]{1,0:T(8,128)(2,1)S(1)}, bf16[1536,768]{1,0:T(8,128)(2,1)S(1)}, u32[]{:S(2)}, u32[]{:S(2)}) collective-permute-start(bf16[1536,768]{1,0:T(8,128)(2,1)S(1)} %convolution_convert_fusion.1), channel_id=1, source_target_pairs={{0,4},{4,0},{8,12},{12,8},{16,20},{20,16},{24,28},{28,24},{1,5},{5... | collective-permute-start | bytes 7077896 | tf_op jit(solution)/shard_map/ppermute | solution.py:83
  352.2 29.1 %collective-permute-start.9 = (bf16[1,2,384,384]{3,2,1,0:T(8,128)(2,1)S(1)}, bf16[1,2,384,384]{3,2,1,0:T(8,128)(2,1)S(1)}, u32[]{:S(2)}, u32[]{:S(2)}) collective-permute-start(bf16[1,2,384,384]{3,2,1,0:T(8,128)(2,1)S(1)} %dynamic-slice_convert_fusion.6), channel_id=1, source_target_pairs={{0,16},{4,20},{8,24},{12,28},{16,0},{20,4},{24,8},{28,12},{1,17},{... | collective-permute-start | bytes 1769480 | tf_op jit(solution)/shard_map/ppermute | solution.py:42
  357.0 22.4 %collective-permute-start.12 = (bf16[2,1,384,384]{3,2,1,0:T(8,128)(2,1)S(1)}, bf16[2,1,384,384]{3,2,1,0:T(8,128)(2,1)S(1)}, u32[]{:S(2)}, u32[]{:S(2)}) collective-permute-start(bf16[2,1,384,384]{3,2,1,0:T(8,128)(2,1)S(1)} %dynamic-slice_convert_fusion.5), channel_id=1, source_target_pairs={{0,8},{4,12},{8,0},{12,4},{16,24},{20,28},{24,16},{28,20},{1,9},{5... | collective-permute-start | bytes 1769480 | tf_op jit(solution)/shard_map/ppermute | solution.py:42
  357.7 25.5 %collective-permute-start.14 = (bf16[1,2,384,384]{3,2,1,0:T(8,128)(2,1)S(1)}, bf16[1,2,384,384]{3,2,1,0:T(8,128)(2,1)S(1)}, u32[]{:S(2)}, u32[]{:S(2)}) collective-permute-start(bf16[1,2,384,384]{3,2,1,0:T(8,128)(2,1)S(1)} %dynamic-slice_convert_fusion.4), channel_id=1, source_target_pairs={{0,16},{4,20},{8,24},{12,28},{16,0},{20,4},{24,8},{28,12},{1,17},{... | collective-permute-start | bytes 1769480 | tf_op jit(solution)/shard_map/ppermute | solution.py:42
  361.1 30.9 %collective-permute-start.17 = (bf16[2,1,384,384]{3,2,1,0:T(8,128)(2,1)S(1)}, bf16[2,1,384,384]{3,2,1,0:T(8,128)(2,1)S(1)}, u32[]{:S(2)}, u32[]{:S(2)}) collective-permute-start(bf16[2,1,384,384]{3,2,1,0:T(8,128)(2,1)S(1)} %dynamic-slice_convert_fusion.3), channel_id=1, source_target_pairs={{0,8},{4,12},{8,0},{12,4},{16,24},{20,28},{24,16},{28,20},{1,9},{5... | collective-permute-start | bytes 1769480 | tf_op jit(solution)/shard_map/ppermute | solution.py:42
  366.7 27.0 %collective-permute-start.19 = (bf16[1,2,384,384]{3,2,1,0:T(8,128)(2,1)S(1)}, bf16[1,2,384,384]{3,2,1,0:T(8,128)(2,1)S(1)}, u32[]{:S(2)}, u32[]{:S(2)}) collective-permute-start(bf16[1,2,384,384]{3,2,1,0:T(8,128)(2,1)S(1)} %dynamic-slice_convert_fusion.2), channel_id=1, source_target_pairs={{0,16},{4,20},{8,24},{12,28},{16,0},{20,4},{24,8},{28,12},{1,17},{... | collective-permute-start | bytes 1769480 | tf_op jit(solution)/shard_map/ppermute | solution.py:42
  379.4 25.3 %collective-permute-start.22 = (bf16[2,1,384,384]{3,2,1,0:T(8,128)(2,1)S(1)}, bf16[2,1,384,384]{3,2,1,0:T(8,128)(2,1)S(1)}, u32[]{:S(2)}, u32[]{:S(2)}) collective-permute-start(bf16[2,1,384,384]{3,2,1,0:T(8,128)(2,1)S(1)} %dynamic-slice_convert_fusion.1), channel_id=1, source_target_pairs={{0,8},{4,12},{8,0},{12,4},{16,24},{20,28},{24,16},{28,20},{1,9},{5... | collective-permute-start | bytes 1769480 | tf_op jit(solution)/shard_map/ppermute | solution.py:42
  381.2 25.1 %collective-permute-start.24 = (bf16[1,2,384,384]{3,2,1,0:T(8,128)(2,1)S(1)}, bf16[1,2,384,384]{3,2,1,0:T(8,128)(2,1)S(1)}, u32[]{:S(2)}, u32[]{:S(2)}) collective-permute-start(bf16[1,2,384,384]{3,2,1,0:T(8,128)(2,1)S(1)} %dynamic-slice_convert_fusion), channel_id=1, source_target_pairs={{0,16},{4,20},{8,24},{12,28},{16,0},{20,4},{24,8},{28,12},{1,17},{... | collective-permute-start | bytes 1769480 | tf_op jit(solution)/shard_map/ppermute | solution.py:42
  383.2 29.5 %collective-permute-start.8 = (bf16[1,1,384,384]{3,2,1,0:T(8,128)(2,1)S(1)}, bf16[1,1,384,384]{3,2,1,0:T(8,128)(2,1)S(1)}, u32[]{:S(2)}, u32[]{:S(2)}) collective-permute-start(bf16[1,1,384,384]{3,2,1,0:T(8,128)(2,1)S(1)} %dynamic-slice_convert_fusion.15), channel_id=1, source_target_pairs={{0,16},{4,20},{8,24},{12,28},{16,0},{20,4},{24,8},{28,12},{1,17},{... | collective-permute-start | bytes 884744 | tf_op jit(solution)/shard_map/ppermute | solution.py:42
  392.0 21.2 %collective-permute-start.10 = (bf16[1,1,384,384]{3,2,1,0:T(8,128)(2,1)S(1)}, bf16[1,1,384,384]{3,2,1,0:T(8,128)(2,1)S(1)}, u32[]{:S(2)}, u32[]{:S(2)}) collective-permute-start(bf16[1,1,384,384]{3,2,1,0:T(8,128)(2,1)S(1)} %dynamic-slice_convert_fusion.14), channel_id=1, source_target_pairs={{0,8},{4,12},{8,0},{12,4},{16,24},{20,28},{24,16},{28,20},{1,9},{5... | collective-permute-start | bytes 884744 | tf_op jit(solution)/shard_map/ppermute | solution.py:42
  393.7 25.3 %collective-permute-start.13 = (bf16[1,1,384,384]{3,2,1,0:T(8,128)(2,1)S(1)}, bf16[1,1,384,384]{3,2,1,0:T(8,128)(2,1)S(1)}, u32[]{:S(2)}, u32[]{:S(2)}) collective-permute-start(bf16[1,1,384,384]{3,2,1,0:T(8,128)(2,1)S(1)} %dynamic-slice_convert_fusion.13), channel_id=1, source_target_pairs={{0,16},{4,20},{8,24},{12,28},{16,0},{20,4},{24,8},{28,12},{1,17},{... | collective-permute-start | bytes 884744 | tf_op jit(solution)/shard_map/ppermute | solution.py:42
  (21 other events, 204.7 us)
Sparse Core Ops, SparseCore 0:
  9.7 41.6 all-gather.11
  53.2 38.9 all-gather.9
  94.1 38.9 all-gather.7
  134.8 98.7 all-gather.5
  235.3 38.9 all-gather.13

commit v2 on v1

v2 whole, which is shorter than its diff:
```python
import functools
import math

import jax
import jax.numpy as jnp
from jax import lax
from jax.experimental import pallas as pl
from jax.experimental.pallas import tpu as pltpu
from jax.sharding import PartitionSpec as P

inv_root = 1.0 / math.sqrt(2.0 * math.pi)
sixths = (1, 2, 2, 1)
f32 = jnp.float32
bf16 = jnp.bfloat16
vmem = 56 * 1024 * 1024


def folded(n):
    return [0] + list(range(1, n, 2)) + list(range(n - 2 + n % 2, 0, -2)) if n > 1 else [0]


def shift(n, stride, total, by):
    pairs = []
    for i in range(total):
        digit = (i // stride) % n
        pairs.append((i, i + (((digit + by) % n) - digit) * stride))
    return pairs


def params():
    return pltpu.CompilerParams(vmem_limit_bytes=vmem)


def cost(flops, nbytes):
    return pl.CostEstimate(flops=int(flops), bytes_accessed=int(nbytes), transcendentals=0)


def place_body(count, by_column, width, at, *refs):
    pieces, out, sems = refs[:count], refs[-2], refs[-1]
    copies = []
    for i in range(count):
        if by_column:
            where = out.at[:, pl.ds(pl.multiple_of(at[i] * width, 128), width)]
        else:
            where = out.at[at[i]]
        copies.append(pltpu.make_async_copy(pieces[i], where, sems.at[i]))
    for c in copies:
        c.start()
    for c in copies:
        c.wait()


def place_rows(pieces, at, slots):
    shape = pieces[0].shape
    count = len(pieces)
    total = slots * shape[0] * shape[1] * 2
    out = pl.pallas_call(
        functools.partial(place_body, count, False, shape[0]),
        grid_spec=pltpu.PrefetchScalarGridSpec(
            num_scalar_prefetch=1,
            grid=(1,),
            in_specs=[pl.BlockSpec(memory_space=pl.ANY)] * count,
            out_specs=pl.BlockSpec(memory_space=pl.ANY),
            scratch_shapes=[pltpu.SemaphoreType.DMA((count,))],
        ),
        out_shape=jax.ShapeDtypeStruct((slots,) + shape, pieces[0].dtype),
        compiler_params=params(),
        cost_estimate=cost(0, 2 * total),
        name="place_rows",
    )(at, *pieces)
    return out.reshape(slots * shape[0], shape[1])


def split_body(count, half, core, aliased, at, *refs):
    pieces = refs[:count]
    mine, other, sems = refs[-3], refs[-2], refs[-1]
    own = core[0]
    copies = []
    for i in range(count):
        into = pl.ds(pl.multiple_of(at[i] * half, 128), half)
        for k, (out, which) in enumerate(((mine, own), (other, 1 - own))):
            source = pieces[i].at[:, pl.ds(pl.multiple_of(which * half, 128), half)]
            copies.append(pltpu.make_async_copy(source, out.at[:, into], sems.at[2 * i + k]))
    for c in copies:
        c.start()
    for c in copies:
        c.wait()


def split_cores(pieces, at, core, slots, before=None):
    count = len(pieces)
    tok, wide = pieces[0].shape
    half = wide // 2
    shape = jax.ShapeDtypeStruct((tok, slots * half), pieces[0].dtype)

    def body(core_ref, at_ref, *refs):
        split_body(count, half, core_ref, before, at_ref, *refs)

    extra = list(before) if before else []
    return pl.pallas_call(
        body,
        grid_spec=pltpu.PrefetchScalarGridSpec(
            num_scalar_prefetch=2,
            grid=(1,),
            in_specs=[pl.BlockSpec(memory_space=pl.ANY)] * (count + len(extra)),
            out_specs=[pl.BlockSpec(memory_space=pl.ANY)] * 2,
            scratch_shapes=[pltpu.SemaphoreType.DMA((2 * count,))],
        ),
        out_shape=[shape, shape],
        input_output_aliases={2 + count: 0, 3 + count: 1} if extra else {},
        compiler_params=params(),
        cost_estimate=cost(0, 4 * count * tok * wide),
        name="split_cores",
    )(core.reshape(1), at, *pieces, *extra)


def split_plain(pieces, at, core):
    tok, wide = pieces[0].shape
    full = jnp.zeros((tok, wide * len(pieces)), pieces[0].dtype)
    for i, piece in enumerate(pieces):
        full = lax.dynamic_update_slice(full, piece, (0, at[i] * wide))
    full = full.reshape(tok, len(pieces), 2, wide // 2)
    return [
        lax.dynamic_index_in_dim(full, which, 2, keepdims=False).reshape(tok, -1)
        for which in (core, 1 - core)
    ]


def whole(shape):
    return pl.BlockSpec(shape, lambda *_: (0,) * len(shape))


def bent_body(count, width, at, scale, codes, down, *refs):
    shards, out = refs[:count], refs[count]
    total = None
    for s in range(count):
        cols = pl.ds(pl.multiple_of(at[s] * width, 128), width)
        term = lax.dot_general(
            shards[s][...], down[:, cols], (((1,), (1,)), ((), ())), preferred_element_type=f32
        )
        total = term if total is None else total + term
    active = codes[...].astype(f32) * scale[...]
    square = active * active
    out[...] = total * (jnp.exp(-0.5 * square) * inv_root * (2.0 - square))


def bent_of(shards, at, row_scale, codes, down_full):
    count = len(shards)
    tok, width = shards[0].shape
    hidden, feats = down_full.shape
    tile = 512
    return pl.pallas_call(
        functools.partial(bent_body, count, width),
        grid_spec=pltpu.PrefetchScalarGridSpec(
            num_scalar_prefetch=1,
            grid=(hidden // tile,),
            in_specs=[
                whole((tok, 1)),
                pl.BlockSpec((tok, tile), lambda j, at: (0, j)),
                pl.BlockSpec((tile, feats), lambda j, at: (j, 0)),
            ]
            + [whole((tok, width))] * count,
            out_specs=pl.BlockSpec((tok, tile), lambda j, at: (0, j)),
        ),
        out_shape=jax.ShapeDtypeStruct((tok, hidden), f32),
        compiler_params=params(),
        cost_estimate=cost(2 * tok * feats * hidden, hidden * (2 * feats + 8 * tok)),
        name="bent",
    )(at, row_scale[:, None], codes, down_full, *shards)


def partial_body(count, width, at, probe, *refs):
    shards, out = refs[:count], refs[count]
    total = None
    for s in range(count):
        rows = pl.ds(pl.multiple_of(at[s] * width, 128), width)
        term = jnp.dot(shards[s][...], probe[rows, :], preferred_element_type=f32)
        total = term if total is None else total + term
    out[...] = total


def partial_tangent(shards, at, probe_full):
    count = len(shards)
    tok, width = shards[0].shape
    feats, hidden = probe_full.shape
    tile = 512
    return pl.pallas_call(
        functools.partial(partial_body, count, width),
        grid_spec=pltpu.PrefetchScalarGridSpec(
            num_scalar_prefetch=1,
            grid=(hidden // tile,),
            in_specs=[pl.BlockSpec((feats, tile), lambda j, at: (0, j))]
            + [whole((tok, width))] * count,
            out_specs=pl.BlockSpec((tok, tile), lambda j, at: (0, j)),
        ),
        out_shape=jax.ShapeDtypeStruct((tok, hidden), f32),
        compiler_params=params(),
        cost_estimate=cost(2 * tok * count * width * hidden, hidden * (2 * feats + 4 * tok)),
        name="partial_tangent",
    )(at, probe_full, *shards)


def mixed_body(at, shard, probe, begun, bent, out):
    tangent = begun[...] + jnp.dot(shard[...], probe[...], preferred_element_type=f32)
    out[...] = (bent[...] * tangent).astype(bf16)


def mixed_of(shard, at, probe_full, begun, bent, first, wide):
    tok, width = shard.shape
    tile = wide // 2
    base = first // tile
    last = at.shape[0] - 1
    return pl.pallas_call(
        mixed_body,
        grid_spec=pltpu.PrefetchScalarGridSpec(
            num_scalar_prefetch=1,
            grid=(2,),
            in_specs=[
                whole((tok, width)),
                pl.BlockSpec((width, tile), lambda j, at: (at[last], base + j)),
                pl.BlockSpec((tok, tile), lambda j, at: (0, base + j)),
                pl.BlockSpec((tok, tile), lambda j, at: (0, base + j)),
            ],
            out_specs=pl.BlockSpec((tok, tile), lambda j, at: (0, j)),
        ),
        out_shape=jax.ShapeDtypeStruct((tok, wide), bf16),
        compiler_params=params(),
        cost_estimate=cost(2 * tok * width * wide, wide * (2 * width + 10 * tok)),
        name="mixed",
    )(at, shard, probe_full, begun, bent)


def ring_gather(block, order):
    n = len(order)
    pairs = [(order[i], order[(i + 1) % n]) for i in range(n)]
    held = [block]
    for _ in range(1, n):
        held.append(lax.ppermute(held[-1], "tensor", pairs))
    return held


def plane_gather(block, cores, xs, ys, core, x, y):
    dp = cores * xs * ys
    rows = block.shape[0] // 2

    def chip(a, by):
        return lax.ppermute(a, "dp", shift(xs, cores, dp, by))

    def up(a, by):
        return lax.ppermute(a, "dp", shift(ys, cores * xs, dp, by))

    top, low = block[:rows], block[rows:]
    held = [(top, 0, 0, 0), (low, 1, 0, 0)]
    for i in range(1, xs):
        across = chip(top, i)
        held += [(across, 0, i, 0), (chip(low, i), 1, i, 0)]
        held += [(up(across, k), 0, i, k) for k in range(1, ys)]
    for k in range(1, ys):
        above = up(low, k)
        held += [(above, 1, 0, k), (up(top, k), 0, 0, k)]
        held += [(chip(above, i), 1, i, k) for i in range(1, xs)]
    pieces, at = [], []
    for by in range(cores):
        for piece, half, i, k in held:
            pieces.append(lax.ppermute(piece, "dp", shift(cores, 1, dp, by)) if by else piece)
            there = (lax.rem(y + ys - k, ys) * xs + lax.rem(x + xs - i, xs)) * cores
            at.append((there + lax.rem(core + cores - by, cores)) * 2 + half)
    return place_rows(pieces, jnp.stack(at), 2 * dp)


def reduce_over(parts, dim, n, stride, total, digit):
    own = lax.dynamic_index_in_dim(parts, digit, dim, keepdims=True)
    for by in range(1, n):
        send = lax.dynamic_index_in_dim(parts, lax.rem(digit + by, n), dim, keepdims=True)
        own = own + lax.ppermute(send.astype(bf16), "dp", shift(n, stride, total, by)).astype(f32)
    return own


def shards(tokens, cotangent, codes, row_scale, probe, down_weight):
    dp, tp = lax.axis_size("dp"), lax.axis_size("tensor")
    cores, xs = 2, 2
    ys = dp // (cores * xs)
    me = lax.axis_index("dp")
    core, x, y = lax.rem(me, cores), lax.rem(lax.div(me, cores), xs), lax.div(me, cores * xs)
    tok_rows = tokens.shape[0]
    rows, hidden = probe.shape
    order = folded(tp)
    table = [[order[(order.index(i) - s) % tp] for s in range(tp)] for i in range(tp)]
    at = lax.dynamic_index_in_dim(
        jnp.array(table, jnp.int32), lax.axis_index("tensor"), 0, keepdims=False
    )

    cot = ring_gather(cotangent, order)
    tok = ring_gather(tokens, order)
    down_full = lax.all_gather(down_weight, "dp", axis=0, tiled=True)
    probe_full = plane_gather(probe, cores, xs, ys, core, x, y)

    bent = bent_of(cot, at, row_scale, codes, down_full)
    begun = partial_tangent(tok[:-1], at, probe_full)
    if rows % 128:
        mine, other = split_plain(tok, at, core)
    else:
        early = split_cores(tok[:-1], at[:-1], core, tp)
        mine, other = split_cores(tok[-1:], at[-1:], core, tp, early)

    pieces = []
    first = 0
    for part in sixths:
        wide = hidden * part // sum(sixths)
        mixed = mixed_of(tok[-1], at, probe_full, begun, bent, first, wide)
        first += wide
        away = lax.dot_general(other, mixed, (((0,), (0,)), ((), ())), preferred_element_type=f32)
        came = lax.ppermute(away.astype(bf16), "dp", shift(cores, 1, dp, 1))
        kept = lax.dot_general(mine, mixed, (((0,), (0,)), ((), ())), preferred_element_type=f32)
        both = (kept + came.astype(f32)).reshape(ys, xs, rows, wide)
        half = wide // 2
        left, right = both[..., :half], both[..., half:]
        left = reduce_over(left, 1, xs, cores, dp, x)
        left = reduce_over(left, 0, ys, cores * xs, dp, y)
        right = reduce_over(right, 0, ys, cores * xs, dp, y)
        right = reduce_over(right, 1, xs, cores, dp, x)
        pieces += [left.reshape(rows, half), right.reshape(rows, half)]
    hessian = jnp.concatenate(pieces, axis=1)
    return probe.astype(f32) * hessian * (1.0 / (tok_rows * dp))


def solution(mesh):
    placed = (
        P("dp", "tensor"),
        P("dp", "tensor"),
        P("dp", "tensor"),
        P("dp"),
        P("dp", "tensor"),
        P(("tensor", "dp"), None),
    )
    return jax.shard_map(
        shards, mesh=mesh, in_specs=placed, out_specs=P("dp", "tensor"), check_vma=False
    )
```

time: 447 us -> 1170 us (2.62)
  Pallas kernels: 0 us -> 844 us
  local copies, waits for them, and re-layouts: 91.1 us -> 10.4 us
  matrix products: 113 us -> 37.4 us
  waiting for transfers between devices: 178 us -> 223 us
    pallas_call x0 -> x9, Pallas kernels: none -> 844 us  [the longest x1 574 us: place_rows(): pl.pallas_call(functools.partial(place_body, count, False, shape[0]), gri...]
    dot_general x5 -> x0, matrix products: 77.4 us -> none  [the longest x4 45.7 us: shards(): tangent = jnp.dot(tok_full, probe_full, preferred_element_type=f32)]
    dynamic_update_slice x8 -> x0, local copies, waits for them, and re-layouts: 68.4 us -> none  [the longest x6 51.4 us: ring_gather(): full = lax.dynamic_update_slice(full, held, (0, starts[step]))]
    ppermute x22 -> x36, waiting for transfers between devices: 176 us -> 222 us  [the longest x3 77.4 us: up(): return lax.ppermute(a, 'dp', shift(ys, cores * xs, dp, by))]
    ppermute x22 -> x36, starting transfers between devices: 31 us -> 39.2 us  [the longest x16 21.1 us: reduce_over(): lax.ppermute(send.astype(bf16), 'dp', shift(n, stride, total, by))]
  transfers between devices with their start and end apart: 31 -> 41, of which waited for: 13 -> 16; matrix products, arithmetic and copies ran while one was open for 41% -> 3% of each run, Pallas kernels for 0% -> 68%
where the time goes in v2:
time: 1170 us
  Pallas kernels  844 us (72%)
  waiting for transfers between devices  223 us (19%)
  starting transfers between devices  40.3 us (3%)
  matrix products  37.4 us (3%)
  between operations  14 us (1%)
    pallas_call x1, Pallas kernels, place_rows(): pl.pallas_call(functools.partial(place_body, count, False, shape[0]), gri...  574 us
    pallas_call x2, Pallas kernels, split_cores(): pl.pallas_call(body, grid_spec=pltpu.PrefetchScalarGridSpec(num_scalar_pr...  194 us
    ppermute x3, waiting for transfers between devices, up(): return lax.ppermute(a, 'dp', shift(ys, cores * xs, dp, by))  77.4 us
    ppermute x16, waiting for transfers between devices, reduce_over(): lax.ppermute(send.astype(bf16), 'dp', shift(n, stride, total, by))  64.6 us
    ppermute x3, waiting for transfers between devices, chip(): return lax.ppermute(a, 'dp', shift(xs, cores, dp, by))  51.6 us
    pallas_call x1, Pallas kernels, bent_of(): pl.pallas_call(functools.partial(bent_body, count, width), grid_spec=pltp...  29.5 us
    ppermute x6, waiting for transfers between devices, ring_gather(): held.append(lax.ppermute(held[-1], 'tensor', pairs))  28.5 us
    pallas_call x4, Pallas kernels, mixed_of(): pl.pallas_call(mixed_body, grid_spec=pltpu.PrefetchScalarGridSpec(num_sca...  25.1 us
  transfers between devices with their start and end apart: 41, of which 16 were waited for; matrix products, arithmetic and copies ran while one was open for 3% of the time, Pallas kernels for 68%

profile of v2, /device:TPU:0, one launch (start us, length us, event | category | flops | bytes accessed | tf_op | source)
XLA Modules:
  0.0 1173.4 jit_solution(12779031724979020253)
XLA Ops:
  15.1 38.0 %collective-permute-done.6.refs_5_ = bf16[192,3072]{1,0:T(8,128)(2,1)S(1)} collective-permute-done((bf16[192,3072]{1,0:T(8,128)(2,1)S(1)}, bf16[192,3072]{1,0:T(8,128)(2,1)S(1)}, u32[]{:S(2)}, u32[]{:S(2)}) %collective-permute-start.6) | collective-permute-done | bytes 1179680 | tf_op jit(solution)/shard_map/ppermute | solution.py:250
  58.4 37.1 %collective-permute-done.7.refs_6_ = bf16[192,3072]{1,0:T(8,128)(2,1)S(1)} collective-permute-done((bf16[192,3072]{1,0:T(8,128)(2,1)S(1)}, bf16[192,3072]{1,0:T(8,128)(2,1)S(1)}, u32[]{:S(2)}, u32[]{:S(2)}) %collective-permute-start.7) | collective-permute-done | bytes 1179680 | tf_op jit(solution)/shard_map/ppermute | solution.py:250
  101.4 47.6 %collective-permute-done.8.refs_7_ = bf16[192,3072]{1,0:T(8,128)(2,1)} collective-permute-done((bf16[192,3072]{1,0:T(8,128)(2,1)S(1)}, bf16[192,3072]{1,0:T(8,128)(2,1)}, u32[]{:S(2)}, u32[]{:S(2)}) %collective-permute-start.8) | collective-permute-done | bytes 1179680 | tf_op jit(solution)/shard_map/ppermute | solution.py:247
  158.9 28.5 %collective-permute-done.1.refs_2_ = bf16[1024,768]{1,0:T(8,128)(2,1)} collective-permute-done((bf16[1024,768]{1,0:T(8,128)(2,1)S(1)}, bf16[1024,768]{1,0:T(8,128)(2,1)}, u32[]{:S(2)}, u32[]{:S(2)}) %collective-permute-start.1) | collective-permute-done | bytes 1572896 | tf_op jit(solution)/shard_map/ppermute | solution.py:238
  188.7 144.8 %split_cores.2 = (bf16[1024,1536]{1,0:T(8,128)(2,1)}, bf16[1024,1536]{1,0:T(8,128)(2,1)}) custom-call(s32[1]{0:T(128)} %bitcast.core_ref, s32[3]{0:T(128)} %slice_bitcast_fusion.at_ref, bf16[1024,768]{1,0:T(8,128)(2,1)} %refs_0_.4, bf16[1024,768]{1,0:T(8,128)(2,1)} %copy-done.10, bf16[1024,768]{1,0:T(8,128)(2,1)} %collective-permute-done.1.refs_2_), custom_call_target="tpu_custom_call" | custom-call | bytes 9437184 | tf_op jit(solution)/shard_map/split_cores/pallas_call | solution.py:100
  333.5 573.7 %place_rows.1 = bf16[16,192,3072]{2,1,0:T(8,128)(2,1)} custom-call(s32[16]{0:T(128)} %stack.67.at, bf16[192,3072]{1,0:T(8,128)(2,1)} %copy-done.4, bf16[192,3072]{1,0:T(8,128)(2,1)} %copy-done.3, bf16[192,3072]{1,0:T(8,128)(2,1)} %collective-permute-done.3.refs_2_, bf16[192,3072]{1,0:T(8,128)(2,1)} %copy-done.13, ...), custom_call_target="tpu_custom_call" | custom-call | bytes 37748736 | tf_op jit(solution)/shard_map/place_rows/pallas_call | solution.py:57
  907.2 21.1 %partial_tangent.1.begun = f32[1024,3072]{1,0:T(8,128)} custom-call(s32[4]{0:T(128)} %get-tuple-element.23.at, bf16[3072,3072]{1,0:T(8,128)(2,1)} %bitcast.60, bf16[1024,768]{1,0:T(8,128)(2,1)} %refs_0_.4, bf16[1024,768]{1,0:T(8,128)(2,1)} %copy-done.10, bf16[1024,768]{1,0:T(8,128)(2,1)} %collective-permute-done.1.refs_2_), custom_call_target="tpu_custom_call" | custom-call | flops 14495514624 | bytes 31457280 | tf_op jit(solution)/shard_map/partial_tangent/pallas_call | solution.py:187
  929.4 49.4 %split_cores.3 = (bf16[1024,1536]{1,0:T(8,128)(2,1)}, bf16[1024,1536]{1,0:T(8,128)(2,1)}) custom-call(s32[1]{0:T(128)} %bitcast.core_ref, s32[1]{0:T(128)} %bitcast.1.at_ref, bf16[1024,768]{1,0:T(8,128)(2,1)} %copy-done, bf16[1024,1536]{1,0:T(8,128)(2,1)} %get-tuple-element.9.refs_1_, ...), custom_call_target="tpu_custom_call", output_to_operand_aliasing={{0}: (3, {}), {1}: (4, {})} | custom-call | bytes 3145728 | tf_op jit(solution)/shard_map/split_cores/pallas_call | solution.py:100
  978.9 29.5 %bent.1 = f32[1024,3072]{1,0:T(8,128)} custom-call(s32[4]{0:T(128)} %get-tuple-element.23.at, f32[1024,1]{1,0:T(8,128)} %copy.10.scale, s32[1024,3072]{1,0:T(8,128)} %codes.1, bf16[3072,3072]{1,0:T(8,128)(2,1)} %all-gather.2.cloned.1.call-done.down, bf16[1024,768]{1,0:T(8,128)(2,1)} %refs_0_.5, bf16[1024,768]{1,0:T(8,128)(2,1)} %collective-permute-done.17.refs_1_, ...), custom_call_target="tpu_custom_call" | custom-call | flops 19327352832 | bytes 44040192 | tf_op jit(solution)/shard_map/bent/pallas_call | solution.py:152
  1008.4 5.5 mixed.4
  1013.9 4.2 convolution_convert_fusion.3
  1018.1 5.3 mixed.7
  1028.1 7.2 mixed.6
  1035.3 6.5 convolution_convert_fusion
  1041.8 7.2 mixed.5
  1049.0 6.6 convolution_convert_fusion.1
  1074.7 5.4 collective-permute-done.21
  1086.2 4.3 collective-permute-done.22
  1092.1 5.5 convert_add_fusion
  1107.5 11.7 %collective-permute-done.31 = bf16[2,1,384,512]{3,2,1,0:T(8,128)(2,1)S(1)} collective-permute-done((bf16[2,1,384,512]{3,2,1,0:T(8,128)(2,1)S(1)}, bf16[2,1,384,512]{3,2,1,0:T(8,128)(2,1)S(1)}, u32[]{:S(2)}, u32[]{:S(2)}) %collective-permute-start.31) | collective-permute-done | bytes 786464 | tf_op jit(solution)/shard_map/ppermute | solution.py:275
  1121.0 11.1 collective-permute-done.26
  1133.8 9.7 collective-permute-done.28
  1146.0 9.7 collective-permute-done.27
  1157.3 6.1 collective-permute-done.34
  (165 shorter events, 83.8 us)
Async XLA Ops:
  6.5 972.3 %all-gather.2.cloned.1.call-start = ((), (), s32[]{:S(2)}) async-start(), calls=%async_computation | async-start | bytes 21233664 | tf_op jit(solution)/shard_map/all_gather | solution.py:295
  8.9 44.2 %collective-permute-start.6 = (bf16[192,3072]{1,0:T(8,128)(2,1)S(1)}, bf16[192,3072]{1,0:T(8,128)(2,1)S(1)}, u32[]{:S(2)}, u32[]{:S(2)}) collective-permute-start(bf16[192,3072]{1,0:T(8,128)(2,1)S(1)} %get-tuple-element.21.refs_1_), channel_id=1, source_target_pairs={{0,16},{4,20},{8,24},{12,28},{16,0},{20,4},{24,8},{28,12},{1,17},{... | collective-permute-start | bytes 3538952 | tf_op jit(solution)/shard_map/ppermute | solution.py:250
  11.5 44.4 %collective-permute-start.4 = (bf16[192,3072]{1,0:T(8,128)(2,1)S(1)}, bf16[192,3072]{1,0:T(8,128)(2,1)S(1)}, u32[]{:S(2)}, u32[]{:S(2)}) collective-permute-start(bf16[192,3072]{1,0:T(8,128)(2,1)S(1)} %get-tuple-element.21.refs_1_), channel_id=1, source_target_pairs={{0,8},{4,12},{8,0},{12,4},{16,24},{20,28},{24,16},{28,20},{1,9},{5... | collective-permute-start | bytes 3538952 | tf_op jit(solution)/shard_map/ppermute | solution.py:247
  13.0 45.4 %collective-permute-start.9 = (bf16[192,3072]{1,0:T(8,128)(2,1)S(1)}, bf16[192,3072]{1,0:T(8,128)(2,1)S(1)}, u32[]{:S(2)}, u32[]{:S(2)}) collective-permute-start(bf16[192,3072]{1,0:T(8,128)(2,1)S(1)} %get-tuple-element.22.refs_0_), channel_id=1, source_target_pairs={{0,4},{4,0},{8,12},{12,8},{16,20},{20,16},{24,28},{28,24},{1,5},{5... | collective-permute-start | bytes 3538952 | tf_op jit(solution)/shard_map/ppermute | solution.py:265
  13.0 82.5 %collective-permute-start.7 = (bf16[192,3072]{1,0:T(8,128)(2,1)S(1)}, bf16[192,3072]{1,0:T(8,128)(2,1)S(1)}, u32[]{:S(2)}, u32[]{:S(2)}) collective-permute-start(bf16[192,3072]{1,0:T(8,128)(2,1)S(1)} %get-tuple-element.22.refs_0_), channel_id=1, source_target_pairs={{0,16},{4,20},{8,24},{12,28},{16,0},{20,4},{24,8},{28,12},{1,17},{... | collective-permute-start | bytes 3538952 | tf_op jit(solution)/shard_map/ppermute | solution.py:250
  13.5 85.8 %collective-permute-start.17 = (bf16[1024,768]{1,0:T(8,128)(2,1)S(1)}, bf16[1024,768]{1,0:T(8,128)(2,1)}, u32[]{:S(2)}, u32[]{:S(2)}) collective-permute-start(bf16[1024,768]{1,0:T(8,128)(2,1)S(1)} %copy-done.22), channel_id=1, source_target_pairs={{0,1},{1,3},{3,2},{2,0},{4,5},{5,7},{7,6},{6,4},{8,9},{9,11},{11,1... | collective-permute-start | bytes 4718600 | tf_op jit(solution)/shard_map/ppermute | solution.py:238
  53.1 46.8 %collective-permute-start = (bf16[1024,768]{1,0:T(8,128)(2,1)S(1)}, bf16[1024,768]{1,0:T(8,128)(2,1)S(1)}, u32[]{:S(2)}, u32[]{:S(2)}) collective-permute-start(bf16[1024,768]{1,0:T(8,128)(2,1)S(1)} %copy-done.9), channel_id=1, source_target_pairs={{0,1},{1,3},{3,2},{2,0},{4,5},{5,7},{7,6},{6,4},{8,9},{9,11},{11,1... | collective-permute-start | bytes 4718600 | tf_op jit(solution)/shard_map/ppermute | solution.py:238
  55.9 43.5 %collective-permute-start.3 = (bf16[192,3072]{1,0:T(8,128)(2,1)S(1)}, bf16[192,3072]{1,0:T(8,128)(2,1)}, u32[]{:S(2)}, u32[]{:S(2)}) collective-permute-start(bf16[192,3072]{1,0:T(8,128)(2,1)S(1)} %get-tuple-element.22.refs_0_), channel_id=1, source_target_pairs={{0,8},{4,12},{8,0},{12,4},{16,24},{20,28},{24,16},{28,20},{1,9},{5... | collective-permute-start | bytes 3538952 | tf_op jit(solution)/shard_map/ppermute | solution.py:247
  58.4 41.5 %collective-permute-start.14 = (bf16[192,3072]{1,0:T(8,128)(2,1)S(1)}, bf16[192,3072]{1,0:T(8,128)(2,1)S(1)}, u32[]{:S(2)}, u32[]{:S(2)}) collective-permute-start(bf16[192,3072]{1,0:T(8,128)(2,1)S(1)} %collective-permute-done.6.refs_5_), channel_id=1, source_target_pairs={{0,4},{4,0},{8,12},{12,8},{16,20},{20,16},{24,28},{28,24},{1,5},{5... | collective-permute-start | bytes 3538952 | tf_op jit(solution)/shard_map/ppermute | solution.py:265
  95.5 53.6 %collective-permute-start.8 = (bf16[192,3072]{1,0:T(8,128)(2,1)S(1)}, bf16[192,3072]{1,0:T(8,128)(2,1)}, u32[]{:S(2)}, u32[]{:S(2)}) collective-permute-start(bf16[192,3072]{1,0:T(8,128)(2,1)S(1)} %collective-permute-done.6.refs_5_), channel_id=1, source_target_pairs={{0,8},{4,12},{8,0},{12,4},{16,24},{20,28},{24,16},{28,20},{1,9},{5... | collective-permute-start | bytes 3538952 | tf_op jit(solution)/shard_map/ppermute | solution.py:247
  99.3 51.2 %collective-permute-start.12 = (bf16[192,3072]{1,0:T(8,128)(2,1)S(1)}, bf16[192,3072]{1,0:T(8,128)(2,1)S(1)}, u32[]{:S(2)}, u32[]{:S(2)}) collective-permute-start(bf16[192,3072]{1,0:T(8,128)(2,1)S(1)} %collective-permute-done.4.refs_3_), channel_id=1, source_target_pairs={{0,4},{4,0},{8,12},{12,8},{16,20},{20,16},{24,28},{28,24},{1,5},{5... | collective-permute-start | bytes 3538952 | tf_op jit(solution)/shard_map/ppermute | solution.py:265
  99.3 51.3 %collective-permute-start.15 = (bf16[192,3072]{1,0:T(8,128)(2,1)S(1)}, bf16[192,3072]{1,0:T(8,128)(2,1)S(1)}, u32[]{:S(2)}, u32[]{:S(2)}) collective-permute-start(bf16[192,3072]{1,0:T(8,128)(2,1)S(1)} %collective-permute-done.7.refs_6_), channel_id=1, source_target_pairs={{0,4},{4,0},{8,12},{12,8},{16,20},{20,16},{24,28},{28,24},{1,5},{5... | collective-permute-start | bytes 3538952 | tf_op jit(solution)/shard_map/ppermute | solution.py:265
  99.9 54.1 %collective-permute-start.5 = (bf16[192,3072]{1,0:T(8,128)(2,1)}, bf16[192,3072]{1,0:T(8,128)(2,1)}, u32[]{:S(2)}, u32[]{:S(2)}) collective-permute-start(bf16[192,3072]{1,0:T(8,128)(2,1)} %collective-permute-done.3.refs_2_), channel_id=1, source_target_pairs={{0,16},{4,20},{8,24},{12,28},{16,0},{20,4},{24,8},{28,12},{1,17},{... | collective-permute-start | bytes 3538952 | tf_op jit(solution)/shard_map/ppermute | solution.py:250
  99.9 57.7 %collective-permute-start.18 = (bf16[1024,768]{1,0:T(8,128)(2,1)}, bf16[1024,768]{1,0:T(8,128)(2,1)}, u32[]{:S(2)}, u32[]{:S(2)}) collective-permute-start(bf16[1024,768]{1,0:T(8,128)(2,1)} %collective-permute-done.17.refs_1_), channel_id=1, source_target_pairs={{0,1},{1,3},{3,2},{2,0},{4,5},{5,7},{7,6},{6,4},{8,9},{9,11},{11,1... | collective-permute-start | bytes 4718600 | tf_op jit(solution)/shard_map/ppermute | solution.py:238
  150.5 182.9 %collective-permute-start.11 = (bf16[192,3072]{1,0:T(8,128)(2,1)}, bf16[192,3072]{1,0:T(8,128)(2,1)}, u32[]{:S(2)}, u32[]{:S(2)}) collective-permute-start(bf16[192,3072]{1,0:T(8,128)(2,1)} %collective-permute-done.3.refs_2_), channel_id=1, source_target_pairs={{0,4},{4,0},{8,12},{12,8},{16,20},{20,16},{24,28},{28,24},{1,5},{5... | collective-permute-start | bytes 3538952 | tf_op jit(solution)/shard_map/ppermute | solution.py:265
  150.7 182.8 %collective-permute-start.16 = (bf16[192,3072]{1,0:T(8,128)(2,1)}, bf16[192,3072]{1,0:T(8,128)(2,1)}, u32[]{:S(2)}, u32[]{:S(2)}) collective-permute-start(bf16[192,3072]{1,0:T(8,128)(2,1)} %collective-permute-done.8.refs_7_), channel_id=1, source_target_pairs={{0,4},{4,0},{8,12},{12,8},{16,20},{20,16},{24,28},{28,24},{1,5},{5... | collective-permute-start | bytes 3538952 | tf_op jit(solution)/shard_map/ppermute | solution.py:265
  154.0 179.5 %collective-permute-start.13 = (bf16[192,3072]{1,0:T(8,128)(2,1)}, bf16[192,3072]{1,0:T(8,128)(2,1)}, u32[]{:S(2)}, u32[]{:S(2)}) collective-permute-start(bf16[192,3072]{1,0:T(8,128)(2,1)} %collective-permute-done.5.refs_4_), channel_id=1, source_target_pairs={{0,4},{4,0},{8,12},{12,8},{16,20},{20,16},{24,28},{28,24},{1,5},{5... | collective-permute-start | bytes 3538952 | tf_op jit(solution)/shard_map/ppermute | solution.py:265
  157.6 821.3 %collective-permute-start.19 = (bf16[1024,768]{1,0:T(8,128)(2,1)}, bf16[1024,768]{1,0:T(8,128)(2,1)}, u32[]{:S(2)}, u32[]{:S(2)}) collective-permute-start(bf16[1024,768]{1,0:T(8,128)(2,1)} %collective-permute-done.18.refs_2_), channel_id=1, source_target_pairs={{0,1},{1,3},{3,2},{2,0},{4,5},{5,7},{7,6},{6,4},{8,9},{9,11},{11,1... | collective-permute-start | bytes 4718600 | tf_op jit(solution)/shard_map/ppermute | solution.py:238
  187.4 740.9 %collective-permute-start.2 = (bf16[1024,768]{1,0:T(8,128)(2,1)}, bf16[1024,768]{1,0:T(8,128)(2,1)S(1)}, u32[]{:S(2)}, u32[]{:S(2)}) collective-permute-start(bf16[1024,768]{1,0:T(8,128)(2,1)} %collective-permute-done.1.refs_2_), channel_id=1, source_target_pairs={{0,1},{1,3},{3,2},{2,0},{4,5},{5,7},{7,6},{6,4},{8,9},{9,11},{11,1... | collective-permute-start | bytes 4718600 | tf_op jit(solution)/shard_map/ppermute | solution.py:238
  1041.8 50.3 %collective-permute-start.30 = (bf16[1536,1024]{1,0:T(8,128)(2,1)}, bf16[1536,1024]{1,0:T(8,128)(2,1)}, u32[]{:S(2)}, u32[]{:S(2)}) collective-permute-start(bf16[1536,1024]{1,0:T(8,128)(2,1)} %convolution_convert_fusion), channel_id=1, source_target_pairs={{0,4},{4,0},{8,12},{12,8},{16,20},{20,16},{24,28},{28,24},{1,5},{5... | collective-permute-start | bytes 9437192 | tf_op jit(solution)/shard_map/ppermute | solution.py:313
  1055.6 43.7 %collective-permute-start.25 = (bf16[1536,1024]{1,0:T(8,128)(2,1)}, bf16[1536,1024]{1,0:T(8,128)(2,1)S(1)}, u32[]{:S(2)}, u32[]{:S(2)}) collective-permute-start(bf16[1536,1024]{1,0:T(8,128)(2,1)} %convolution_convert_fusion.1), channel_id=1, source_target_pairs={{0,4},{4,0},{8,12},{12,8},{16,20},{20,16},{24,28},{28,24},{1,5},{5... | collective-permute-start | bytes 9437192 | tf_op jit(solution)/shard_map/ppermute | solution.py:313
  1074.3 89.3 %collective-permute-start.37 = (bf16[1,1,384,256]{3,2,1,0:T(8,128)(2,1)S(1)}, bf16[1,1,384,256]{3,2,1,0:T(8,128)(2,1)S(1)}, u32[]{:S(2)}, u32[]{:S(2)}) collective-permute-start(bf16[1,1,384,256]{3,2,1,0:T(8,128)(2,1)S(1)} %dynamic-slice_convert_fusion.13), channel_id=1, source_target_pairs={{0,16},{4,20},{8,24},{12,28},{16,0},{20,4},{24,8},{28,12},{1,17},{... | collective-permute-start | bytes 589832 | tf_op jit(solution)/shard_map/ppermute | solution.py:275
  1080.0 83.6 %collective-permute-start.39 = (bf16[1,1,384,256]{3,2,1,0:T(8,128)(2,1)S(1)}, bf16[1,1,384,256]{3,2,1,0:T(8,128)(2,1)S(1)}, u32[]{:S(2)}, u32[]{:S(2)}) collective-permute-start(bf16[1,1,384,256]{3,2,1,0:T(8,128)(2,1)S(1)} %dynamic-slice_convert_fusion.12), channel_id=1, source_target_pairs={{0,8},{4,12},{8,0},{12,4},{16,24},{20,28},{24,16},{28,20},{1,9},{5... | collective-permute-start | bytes 589832 | tf_op jit(solution)/shard_map/ppermute | solution.py:275
  1106.0 39.1 %collective-permute-start.33 = (bf16[1,2,384,512]{3,2,1,0:T(8,128)(2,1)S(1)}, bf16[1,2,384,512]{3,2,1,0:T(8,128)(2,1)S(1)}, u32[]{:S(2)}, u32[]{:S(2)}) collective-permute-start(bf16[1,2,384,512]{3,2,1,0:T(8,128)(2,1)S(1)} %dynamic-slice_convert_fusion), channel_id=1, source_target_pairs={{0,16},{4,20},{8,24},{12,28},{16,0},{20,4},{24,8},{28,12},{1,17},{... | collective-permute-start | bytes 2359304 | tf_op jit(solution)/shard_map/ppermute | solution.py:275
  (40 other events, 1502.8 us)
Sparse Core Ops, SparseCore 0:
  9.2 158.5 all-gather.1

commit v3 on v1

v3 whole, which is shorter than its diff:
```python
import functools
import math

import jax
import jax.numpy as jnp
from jax import lax
from jax.experimental import pallas as pl
from jax.experimental.pallas import tpu as pltpu
from jax.sharding import PartitionSpec as P

inv_root = 1.0 / math.sqrt(2.0 * math.pi)
sixths = (1, 2, 2, 1)
f32 = jnp.float32
bf16 = jnp.bfloat16
vmem = 56 * 1024 * 1024


def folded(n):
    return [0] + list(range(1, n, 2)) + list(range(n - 2 + n % 2, 0, -2)) if n > 1 else [0]


def shift(n, stride, total, by):
    pairs = []
    for i in range(total):
        digit = (i // stride) % n
        pairs.append((i, i + (((digit + by) % n) - digit) * stride))
    return pairs


light = pl.CostEstimate(flops=0, bytes_accessed=1024, transcendentals=0)


def params():
    return pltpu.CompilerParams(vmem_limit_bytes=vmem)


def split_body(count, half, core, at, *refs):
    pieces = refs[:count]
    outs, held, sems = refs[-4:-2], refs[-2], refs[-1]
    copies = []
    for i in range(count):
        rows = pl.ds(pl.multiple_of(at[i] * half, half), half)
        for k, which in enumerate((core[0], 1 - core[0])):
            slot = 2 * i + k
            cols = pl.ds(pl.multiple_of(which * half, 128), half)
            held[slot] = pieces[i][:, cols].T
            copies.append(pltpu.make_async_copy(held.at[slot], outs[k].at[rows], sems.at[slot]))
            copies[-1].start()
    for c in copies:
        c.wait()


def split_cores(pieces, at, core, slots, before=()):
    count = len(pieces)
    tok, wide = pieces[0].shape
    half = wide // 2
    shape = jax.ShapeDtypeStruct((slots * half, tok), bf16)
    return pl.pallas_call(
        functools.partial(split_body, count, half),
        grid_spec=pltpu.PrefetchScalarGridSpec(
            num_scalar_prefetch=2,
            grid=(1,),
            in_specs=[whole((tok, wide))] * count
            + [pl.BlockSpec(memory_space=pl.ANY)] * len(before),
            out_specs=[pl.BlockSpec(memory_space=pl.ANY)] * 2,
            scratch_shapes=[
                pltpu.VMEM((2 * count, half, tok), bf16),
                pltpu.SemaphoreType.DMA((2 * count,)),
            ],
        ),
        out_shape=[shape, shape],
        input_output_aliases={2 + count: 0, 3 + count: 1} if before else {},
        compiler_params=params(),
        cost_estimate=light,
        name="split_cores",
    )(core.reshape(1), at, *pieces, *before)


def split_plain(pieces, at, core):
    tok, wide = pieces[0].shape
    full = jnp.zeros((tok, wide * len(pieces)), pieces[0].dtype)
    for i, piece in enumerate(pieces):
        full = lax.dynamic_update_slice(full, piece, (0, at[i] * wide))
    full = full.reshape(tok, len(pieces), 2, wide // 2)
    return [
        lax.dynamic_index_in_dim(full, which, 2, keepdims=False).reshape(tok, -1).T
        for which in (core, 1 - core)
    ]


def whole(shape):
    return pl.BlockSpec(shape, lambda *_: (0,) * len(shape))


def bent_body(count, parts, width, at, scale, codes, down, *refs):
    shards, out = refs[: count * parts], refs[count * parts]
    for h in range(parts):
        tall = shards[h].shape[0]
        total = None
        for s in range(count):
            cols = pl.ds(pl.multiple_of(at[s] * width, 128), width)
            term = lax.dot_general(
                shards[s * parts + h][...],
                down[:, cols],
                (((1,), (1,)), ((), ())),
                preferred_element_type=f32,
            )
            total = term if total is None else total + term
        rows = pl.ds(h * tall, tall)
        active = codes[rows, :].astype(f32) * scale[rows, :]
        square = active * active
        out[rows, :] = total * (jnp.exp(-0.5 * square) * inv_root * (2.0 - square))


def bent_of(shards, at, row_scale, codes, down_full, first, wide):
    count, parts = len(shards), len(shards[0])
    tall, width = shards[0][0].shape
    tok = tall * parts
    feats = down_full.shape[1]
    tile = math.gcd(wide, math.gcd(first, 512))
    base = first // tile
    return pl.pallas_call(
        functools.partial(bent_body, count, parts, width),
        grid_spec=pltpu.PrefetchScalarGridSpec(
            num_scalar_prefetch=1,
            grid=(wide // tile,),
            in_specs=[
                whole((tok, 1)),
                pl.BlockSpec((tok, tile), lambda j, at: (0, base + j)),
                pl.BlockSpec((tile, feats), lambda j, at: (base + j, 0)),
            ]
            + [whole((tall, width))] * (count * parts),
            out_specs=pl.BlockSpec((tok, tile), lambda j, at: (0, j)),
        ),
        out_shape=jax.ShapeDtypeStruct((tok, wide), f32),
        compiler_params=params(),
        cost_estimate=light,
        name="bent",
    )(at, row_scale[:, None], codes, down_full, *[p for piece in shards for p in piece])


def partial_body(count, parts, width, spots, plan, arrays, tile, at, slots, *refs):
    pieces, refs = refs[:arrays], refs[arrays:]
    shards = refs[: count * parts]
    out, last, held, sems = refs[count * parts :]
    step = pl.program_id(0)

    @pl.when(step == 0)
    def _():
        copies = []
        for i, (which, first, size) in enumerate(plan):
            into = held.at[pl.ds(pl.multiple_of(slots[i] * spots, spots), size)]
            source = pieces[which].at[pl.ds(first, size)]
            copies.append(pltpu.make_async_copy(source, into, sems.at[i]))
        for c in copies:
            c.start()
        for c in copies:
            c.wait()

    cols = pl.ds(pl.multiple_of(step * tile, tile), tile)
    for h in range(parts):
        tall = shards[h].shape[0]
        total = None
        for s in range(count):
            rows = pl.ds(pl.multiple_of(at[s] * width, width), width)
            term = jnp.dot(
                shards[s * parts + h][...], held[rows, cols], preferred_element_type=f32
            )
            total = term if total is None else total + term
        out[pl.ds(h * tall, tall), :] = total
    last[...] = held[pl.ds(pl.multiple_of(at[count] * width, width), width), cols]


def partial_tangent(shards, at, pieces, slots, spots, feats):
    count, parts = len(shards), len(shards[0])
    tall, width = shards[0][0].shape
    tok = tall * parts
    hidden = pieces[0][0].shape[1]
    tile = 512
    arrays, plan = [], []
    for piece, first, size in pieces:
        which = [i for i, a in enumerate(arrays) if a is piece]
        if not which:
            arrays.append(piece)
        plan.append((which[0] if which else len(arrays) - 1, first, size))
    return pl.pallas_call(
        functools.partial(
            partial_body, count, parts, width, spots, plan, len(arrays), tile
        ),
        grid_spec=pltpu.PrefetchScalarGridSpec(
            num_scalar_prefetch=2,
            grid=(hidden // tile,),
            in_specs=[pl.BlockSpec(memory_space=pl.ANY)] * len(arrays)
            + [whole((tall, width))] * (count * parts),
            out_specs=[
                pl.BlockSpec((tok, tile), lambda j, *_: (0, j)),
                pl.BlockSpec((width, tile), lambda j, *_: (0, j)),
            ],
            scratch_shapes=[
                pltpu.VMEM((feats, hidden), bf16),
                pltpu.SemaphoreType.DMA((len(pieces),)),
            ],
        ),
        out_shape=[
            jax.ShapeDtypeStruct((tok, hidden), f32),
            jax.ShapeDtypeStruct((width, hidden), bf16),
        ],
        compiler_params=params(),
        cost_estimate=light,
        name="partial_tangent",
    )(at, slots, *arrays, *[p for piece in shards for p in piece])


def front_body(shard, probe, begun, bent, other, mixed, away):
    tangent = begun[...] + jnp.dot(shard[...], probe[...], preferred_element_type=f32)
    mixed[...] = (bent[...] * tangent).astype(bf16)
    away[...] = jnp.dot(other[...], mixed[...], preferred_element_type=f32).astype(bf16)


def front_of(shard, last, begun, bent, other, first):
    tok, width = shard.shape
    wide = bent.shape[1]
    half = other.shape[0]
    tile = math.gcd(wide, math.gcd(first, 256))
    base = first // tile
    return pl.pallas_call(
        front_body,
        grid=(wide // tile,),
        in_specs=[
            whole((tok, width)),
            pl.BlockSpec((width, tile), lambda j: (0, base + j)),
            pl.BlockSpec((tok, tile), lambda j: (0, base + j)),
            pl.BlockSpec((tok, tile), lambda j: (0, j)),
            whole(other.shape),
        ],
        out_specs=[
            pl.BlockSpec((tok, tile), lambda j: (0, j)),
            pl.BlockSpec((half, tile), lambda j: (0, j)),
        ],
        out_shape=[
            jax.ShapeDtypeStruct((tok, wide), bf16),
            jax.ShapeDtypeStruct((half, wide), bf16),
        ],
        compiler_params=params(),
        cost_estimate=light,
        name="front",
    )(shard, last, begun, bent, other)


def back_body(xs, ys, rows, steps, me, mine, mixed, came, keep_x, keep_y, to_x, to_y):
    x, y = me[0], me[1]

    def block(at_y, at_x):
        part = pl.ds(pl.multiple_of((at_y * xs + at_x) * rows, rows), rows)
        total = jnp.dot(mine[part, :], mixed[...], preferred_element_type=f32)
        return total + came[part, :].astype(f32)

    @pl.when(pl.program_id(0) < steps)
    def _():
        for k in range(ys):
            for i in range(1, xs):
                to_x[k, i - 1] = block(k, lax.rem(x + i, xs)).astype(bf16)
            keep_x[k, 0] = block(k, x)

    @pl.when(pl.program_id(0) >= steps)
    def _():
        for i in range(xs):
            for k in range(1, ys):
                to_y[k - 1, i] = block(lax.rem(y + k, ys), i).astype(bf16)
            keep_y[0, i] = block(y, i)


def back_of(mine, mixed, came, x, y, xs, ys, rows):
    tok, wide = mixed.shape
    side = wide // 2
    tile = math.gcd(side, 256)
    steps = side // tile

    def left(j, me):
        return (0, 0, 0, jnp.minimum(j, steps - 1))

    def right(j, me):
        return (0, 0, 0, jnp.maximum(j - steps, 0))

    shapes = [(ys, 1, rows), (1, xs, rows), (ys, xs - 1, rows), (ys - 1, xs, rows)]
    kinds = [f32, f32, bf16, bf16]
    return pl.pallas_call(
        functools.partial(back_body, xs, ys, rows, steps),
        grid_spec=pltpu.PrefetchScalarGridSpec(
            num_scalar_prefetch=1,
            grid=(2 * steps,),
            in_specs=[
                whole(mine.shape),
                pl.BlockSpec((tok, tile), lambda j, me: (0, j)),
                pl.BlockSpec((mine.shape[0], tile), lambda j, me: (0, j)),
            ],
            out_specs=[
                pl.BlockSpec(shape + (tile,), where)
                for shape, where in zip(shapes, (left, right, left, right))
            ],
        ),
        out_shape=[
            jax.ShapeDtypeStruct(shape + (side,), kind) for shape, kind in zip(shapes, kinds)
        ],
        compiler_params=params(),
        cost_estimate=light,
        name="back",
    )(jnp.stack([x, y]), mine, mixed, came)


def after(ready, *values):
    out = lax.optimization_barrier((ready, *values))
    return out[0], (out[1] if len(values) == 1 else list(out[1:]))


def ring_step(block, order):
    n = len(order)
    pairs = [(order[i], order[(i + 1) % n]) for i in range(n)]
    return lax.ppermute(block, "tensor", pairs)


def swapped(block, dp, cores):
    return lax.ppermute(block, "dp", shift(cores, 1, dp, 1))


def parted(parts, dim, n, digit):
    own = lax.dynamic_index_in_dim(parts, digit, dim, keepdims=True)
    sends = [
        lax.dynamic_index_in_dim(parts, lax.rem(digit + by, n), dim, keepdims=True).astype(bf16)
        for by in range(1, n)
    ]
    return own, sends


def sent(sends, n, stride, total):
    return [
        lax.ppermute(send, "dp", shift(n, stride, total, by + 1)) for by, send in enumerate(sends)
    ]


def summed(own, received):
    for r in received:
        own = own + r.astype(f32)
    return own


def shards(tokens, cotangent, codes, row_scale, probe, down_weight):
    dp, tp = lax.axis_size("dp"), lax.axis_size("tensor")
    cores, xs = 2, 2
    ys = dp // (cores * xs)
    me = lax.axis_index("dp")
    core, x, y = lax.rem(me, cores), lax.rem(lax.div(me, cores), xs), lax.div(me, cores * xs)
    tok_rows = tokens.shape[0]
    rows, hidden = probe.shape
    order = folded(tp)
    table = [[order[(order.index(i) - s) % tp] for s in range(tp)] for i in range(tp)]
    at = lax.dynamic_index_in_dim(
        jnp.array(table, jnp.int32), lax.axis_index("tensor"), 0, keepdims=False
    )

    edges = [hidden * sum(sixths[:j]) // sum(sixths) for j in range(len(sixths) + 1)]
    x_way, y_way = (xs, cores), (ys, cores * xs)

    def over(block, way, by):
        return lax.ppermute(block, "dp", shift(way[0], way[1], dp, by))

    cot, tok = [cotangent], [tokens]
    for s in range(1, tp):
        cot.append(ring_step(cot[-1], order))
        tok.append(ring_step(tok[-1], order))
        if s == 1:
            across = [over(probe, x_way, i) for i in range(1, xs)]
            above = [over(probe, y_way, k) for k in range(1, ys)]
            far = []
            for i in range(1, xs):
                for k in range(1, ys):
                    far.append(over(across[i - 1][: rows // 2], y_way, k))
                    far.append(over(above[k - 1][rows // 2 :], x_way, i))
            near = [(p, swapped(p, dp, cores)) for p in (probe, *across, *above)]
        if s < tp - 1:
            cot[s], tok[s] = lax.optimization_barrier((cot[s], tok[s]))
    far = [(p, swapped(p, dp, cores)) for p in far]
    down_full = lax.all_gather(down_weight, "dp", axis=0, tiled=True)

    pieces, slots = [], []

    def hold(pair, half, i, k):
        chip = (lax.rem(y + ys - k, ys) * xs + lax.rem(x + xs - i, xs)) * cores
        for piece, whose in zip(pair, (core, 1 - core)):
            pieces.append((piece, 0, piece.shape[0]))
            slots.append((chip + whose) * 2 + half)

    spots = [(0, 0)] + [(i, 0) for i in range(1, xs)] + [(0, k) for k in range(1, ys)]
    for pair, (i, k) in zip(near, spots):
        hold(pair, 0, i, k)
    spots = [(half, i, k) for i in range(1, xs) for k in range(1, ys) for half in range(2)]
    for pair, spot in zip(far, spots):
        hold(pair, *spot)
    begun, last = partial_tangent(
        [[t] for t in tok[:-1]], at, pieces, jnp.stack(slots), rows // 2, rows * dp
    )
    begun, cot[-1] = after(begun, cot[-1])
    plain = rows % 128 != 0
    if not plain:
        early = list(split_cores(tok[:-1], at[:-1], core, tp))
        early[0], cot[-1] = after(early[0], cot[-1])
    bent = [
        bent_of(
            [[c] for c in cot], at, row_scale, codes, down_full, edges[j], edges[j + 1] - edges[j]
        )
        for j in range(len(sixths))
    ]
    *bent, tok[-1] = lax.optimization_barrier((*bent, tok[-1]))
    if plain:
        mine, other = split_plain(tok, at, core)
    else:
        mine, other = split_cores(tok[-1:], at[-1:], core, tp, early)

    count = len(sixths)
    out = {}

    def finish(j, keeps, arrived):
        middle = (edges[j] + edges[j + 1]) // 2
        for k, (a, b) in enumerate(((edges[j], middle), (middle, edges[j + 1]))):
            hessian = summed(keeps[k], arrived[k]).reshape(rows, b - a)
            out[2 * j + k] = probe[:, a:b].astype(f32) * hessian * (1.0 / (tok_rows * dp))

    def front(j):
        return front_of(tok[-1], last, begun, bent[j], other, edges[j])

    fronts = {0: front(0)}
    came = {0: swapped(fronts[0][1], dp, cores)}
    mixed = fronts[0][0]
    if count > 1:
        mixed, bent[1] = lax.optimization_barrier((mixed, bent[1]))
        following, away = front(1)
        mixed, following, away, came[0] = lax.optimization_barrier(
            (mixed, following, away, came[0])
        )
        came[1] = swapped(away, dp, cores)
    behind = None
    for j in range(count):
        keep_x, keep_y, to_x, to_y = back_of(mine, mixed, came[j], x, y, xs, ys, rows)
        if behind is not None:
            keeps, arrived = behind
            to_x, to_y, arrived = lax.optimization_barrier((to_x, to_y, arrived))
            finish(j - 1, keeps, arrived)
        ahead = j + 2 < count
        if ahead:
            to_x, to_y, bent[j + 2] = lax.optimization_barrier((to_x, to_y, bent[j + 2]))
        from_x = [over(to_x[:, i - 1 : i], x_way, i) for i in range(1, xs)]
        from_y = [over(to_y[k - 1 : k], y_way, k) for k in range(1, ys)]
        if ahead:
            beyond, away = front(j + 2)
            from_x, from_y, away = lax.optimization_barrier((from_x, from_y, away))
            came[j + 2] = swapped(away, dp, cores)
        left, left_sends = parted(summed(keep_x, from_x), 0, ys, y)
        right, right_sends = parted(summed(keep_y, from_y), 1, xs, x)
        if j + 1 < count:
            left_sends, right_sends, mixed = lax.optimization_barrier(
                (left_sends, right_sends, following)
            )
        if ahead:
            following = beyond
        behind = (left, right), (sent(left_sends, *y_way, dp), sent(right_sends, *x_way, dp))
    finish(count - 1, *behind)
    return jnp.concatenate([out[j] for j in range(2 * count)], axis=1)


def solution(mesh):
    placed = (
        P("dp", "tensor"),
        P("dp", "tensor"),
        P("dp", "tensor"),
        P("dp"),
        P("dp", "tensor"),
        P(("tensor", "dp"), None),
    )
    return jax.shard_map(
        shards, mesh=mesh, in_specs=placed, out_specs=P("dp", "tensor"), check_vma=False
    )
```

time: 447 us -> 407 us (0.911); the launches traced: 441 us -> 406 us
  Pallas kernels: 0 us -> 161 us
  matrix products: 113 us -> 0 us
  local copies, waits for them, and re-layouts: 91.1 us -> 18.5 us
  waiting for transfers between devices: 178 us -> 166 us
  other arithmetic: 4.81 us -> 12.9 us
  between operations: 21.2 us -> 13.9 us
    pallas_call x0 -> x15, Pallas kernels: none -> 161 us  [the longest x4 48.9 us: bent_of(): pl.pallas_call(functools.partial(bent_body, count, parts, width), grid_sp...]
    dot_general x13 -> x0, matrix products: 113 us -> none  [the longest x4 45.7 us: shards(): tangent = jnp.dot(tok_full, probe_full, preferred_element_type=f32)]
    dynamic_update_slice x8 -> x0, local copies, waits for them, and re-layouts: 68.4 us -> none  [the longest x6 51.4 us: ring_gather(): full = lax.dynamic_update_slice(full, held, (0, starts[step]))]
    ppermute x26 -> x35, waiting for transfers between devices: 176 us -> 165 us  [the longest x12 97 us: over(): return lax.ppermute(block, 'dp', shift(way[0], way[1], dp, by))]
    another operation x2 -> x1, local copies, waits for them, and re-layouts: 6.95 us -> 0.67 us  [shards(): jnp.stack(slots)]
    dynamic_slice x2 -> x0, local copies, waits for them, and re-layouts: 6.26 us -> none  [the longest x1 5.57 us: shards(): lax.dynamic_index_in_dim(by_core, core, 2, keepdims=False)]
    unnamed x30 -> x58, local copies, waits for them, and re-layouts: 3.66 us -> 9.84 us
    unnamed x7, other arithmetic: 0.53 us -> 6.41 us
  transfers between devices with their start and end apart: 31 -> 36, of which waited for: 13 -> 11; matrix products, arithmetic and copies ran while one was open for 41% -> 5% of each run, Pallas kernels for 0% -> 37%
where the time goes in v3:
time: 407 us; the launch traced here: 406 us
  waiting for transfers between devices  166 us (41%)
  Pallas kernels  161 us (40%)
  starting transfers between devices  34.2 us (8%)
  local copies, waits for them, and re-layouts  18.5 us (5%)
  between operations  13.9 us (3%)
  other arithmetic  12.9 us (3%)
    ppermute x12, waiting for transfers between devices, over(): return lax.ppermute(block, 'dp', shift(way[0], way[1], dp, by))  97 us
    ppermute x6, waiting for transfers between devices, ring_step(): return lax.ppermute(block, 'tensor', pairs)  64.8 us
    pallas_call x4, Pallas kernels, bent_of(): pl.pallas_call(functools.partial(bent_body, count, parts, width), grid_sp...  48.9 us
    pallas_call x4, Pallas kernels, front_of(): pl.pallas_call(front_body, grid=(wide // tile,), in_specs=[whole((tok, wi...  44.3 us
    pallas_call x4, Pallas kernels, back_of(): pl.pallas_call(functools.partial(back_body, xs, ys, rows, steps), grid_sp...  31.5 us
    pallas_call x1, Pallas kernels, partial_tangent(): pl.pallas_call(functools.partial(partial_body, count, parts, width, spots...  27.1 us
    ppermute x12, starting transfers between devices, over(): return lax.ppermute(block, 'dp', shift(way[0], way[1], dp, by))  14 us
    ppermute x8, starting transfers between devices, sent(): lax.ppermute(send, 'dp', shift(n, stride, total, by + 1))  10.5 us
  transfers between devices with their start and end apart: 36, of which 11 were waited for; matrix products, arithmetic and copies ran while one was open for 5% of the time, Pallas kernels for 37%

profile of v3, /device:TPU:0, one launch (start us, length us, event | category | flops | bytes accessed | tf_op | source)
XLA Modules:
  0.0 406.0 jit_solution(3812432208086343187)
XLA Ops:
  16.0 32.5 %collective-permute-done.refs_1_ = bf16[1024,768]{1,0:T(8,128)(2,1)S(1)} collective-permute-done((bf16[1024,768]{1,0:T(8,128)(2,1)S(1)}, bf16[1024,768]{1,0:T(8,128)(2,1)S(1)}, u32[]{:S(2)}, u32[]{:S(2)}) %collective-permute-start) | collective-permute-done | bytes 1572896 | tf_op jit(solution)/shard_map/ppermute | solution.py:319
  48.5 32.2 %collective-permute-done.1.refs_1_.refs_11_ = bf16[1024,768]{1,0:T(8,128)(2,1)S(1)} collective-permute-done((bf16[1024,768]{1,0:T(8,128)(2,1)}, bf16[1024,768]{1,0:T(8,128)(2,1)S(1)}, u32[]{:S(2)}, u32[]{:S(2)}) %collective-permute-start.1) | collective-permute-done | bytes 1572896 | tf_op jit(solution)/shard_map/ppermute | solution.py:319
  84.9 8.1 %collective-permute-done.5.refs_2_ = bf16[384,3072]{1,0:T(8,128)(2,1)} collective-permute-done((bf16[384,3072]{1,0:T(8,128)(2,1)}, bf16[384,3072]{1,0:T(8,128)(2,1)}, u32[]{:S(2)}, u32[]{:S(2)}) %collective-permute-start.5) | collective-permute-done | bytes 2359328 | tf_op jit(solution)/shard_map/ppermute | solution.py:365
  95.8 9.9 %collective-permute-done.7.refs_4_ = bf16[384,3072]{1,0:T(8,128)(2,1)} collective-permute-done((bf16[384,3072]{1,0:T(8,128)(2,1)}, bf16[384,3072]{1,0:T(8,128)(2,1)}, u32[]{:S(2)}, u32[]{:S(2)}) %collective-permute-start.7) | collective-permute-done | bytes 2359328 | tf_op jit(solution)/shard_map/ppermute | solution.py:365
  107.1 47.0 %collective-permute-done.9.refs_6_ = bf16[192,3072]{1,0:T(8,128)(2,1)S(1)} collective-permute-done((bf16[192,3072]{1,0:T(8,128)(2,1)S(1)}, bf16[192,3072]{1,0:T(8,128)(2,1)S(1)}, u32[]{:S(2)}, u32[]{:S(2)}) %collective-permute-start.9) | collective-permute-done | bytes 1179680 | tf_op jit(solution)/shard_map/ppermute | solution.py:365
  154.7 3.6 collective-permute-done.11.refs_8_
  163.4 5.5 %split_cores.2 = (bf16[1536,1024]{1,0:T(8,128)(2,1)}, bf16[1536,1024]{1,0:T(8,128)(2,1)}) custom-call(s32[1]{0:T(128)} %bitcast.2.core, s32[3]{0:T(128)} %slice_bitcast_fusion.at, bf16[1024,768]{1,0:T(8,128)(2,1)} %refs_10_.1, bf16[1024,768]{1,0:T(8,128)(2,1)} %copy-done.5, bf16[1024,768]{1,0:T(8,128)(2,1)} %collective-permute-done.3.refs_2_.refs_12_), custom_call_target="tpu_custom_call" | custom-call | bytes 1024 | tf_op jit(solution)/shard_map/split_cores/pallas_call | solution.py:58
  168.9 27.1 %partial_tangent.1 = (f32[1024,3072]{1,0:T(8,128)}, bf16[768,3072]{1,0:T(8,128)(2,1)}) custom-call(s32[4]{0:T(128)} %get-tuple-element.169.at, s32[10]{0:T(128)} %stack.64.slots, bf16[384,3072]{1,0:T(8,128)(2,1)} %refs_0_.7, bf16[384,3072]{1,0:T(8,128)(2,1)} %copy-done.14, bf16[384,3072]{1,0:T(8,128)(2,1)} %collective-permute-done.5.refs_2_, ...), custom_call_target="tpu_custom_call" | custom-call | bytes 1024 | tf_op jit(solution)/shard_map/partial_tangent/pallas_call | solution.py:186
  196.1 10.3 %bent.7 = f32[1024,512]{1,0:T(8,128)} custom-call(s32[4]{0:T(128)} %get-tuple-element.169.at, f32[1024,1]{1,0:T(8,128)} %copy.10.scale, s32[1024,3072]{1,0:T(8,128)} %codes.7, bf16[3072,3072]{1,0:T(8,128)(2,1)} %all-gather.2.cloned.1.call-done.down, bf16[1024,768]{1,0:T(8,128)(2,1)} %refs_0_.11, bf16[1024,768]{1,0:T(8,128)(2,1)} %copy-done.2, ...), custom_call_target="tpu_custom_call" | custom-call | bytes 1024 | tf_op jit(solution)/shard_map/bent/pallas_call | solution.py:122
  206.3 14.2 %bent.6 = f32[1024,1024]{1,0:T(8,128)} custom-call(s32[4]{0:T(128)} %get-tuple-element.169.at, f32[1024,1]{1,0:T(8,128)} %copy.10.scale, s32[1024,3072]{1,0:T(8,128)} %codes.7, bf16[3072,3072]{1,0:T(8,128)(2,1)} %all-gather.2.cloned.1.call-done.down, bf16[1024,768]{1,0:T(8,128)(2,1)} %refs_0_.11, bf16[1024,768]{1,0:T(8,128)(2,1)} %copy-done.2, ...), custom_call_target="tpu_custom_call" | custom-call | bytes 1024 | tf_op jit(solution)/shard_map/bent/pallas_call | solution.py:122
  220.5 14.3 %bent.5 = f32[1024,1024]{1,0:T(8,128)} custom-call(s32[4]{0:T(128)} %get-tuple-element.169.at, f32[1024,1]{1,0:T(8,128)} %copy.10.scale, s32[1024,3072]{1,0:T(8,128)} %codes.7, bf16[3072,3072]{1,0:T(8,128)(2,1)} %all-gather.2.cloned.1.call-done.down, bf16[1024,768]{1,0:T(8,128)(2,1)} %refs_0_.11, bf16[1024,768]{1,0:T(8,128)(2,1)} %copy-done.2, ...), custom_call_target="tpu_custom_call" | custom-call | bytes 1024 | tf_op jit(solution)/shard_map/bent/pallas_call | solution.py:122
  234.8 10.2 %bent.4 = f32[1024,512]{1,0:T(8,128)} custom-call(s32[4]{0:T(128)} %get-tuple-element.169.at, f32[1024,1]{1,0:T(8,128)} %copy.10.scale, s32[1024,3072]{1,0:T(8,128)} %codes.7, bf16[3072,3072]{1,0:T(8,128)(2,1)} %all-gather.2.cloned.1.call-done.down, bf16[1024,768]{1,0:T(8,128)(2,1)} %refs_0_.11, bf16[1024,768]{1,0:T(8,128)(2,1)} %copy-done.2, ...), custom_call_target="tpu_custom_call" | custom-call | bytes 1024 | tf_op jit(solution)/shard_map/bent/pallas_call | solution.py:122
  246.2 3.6 split_cores.3
  249.8 8.9 %front.4 = (bf16[1024,512]{1,0:T(8,128)(2,1)}, bf16[1536,512]{1,0:T(8,128)(2,1)}) custom-call(bf16[1024,768]{1,0:T(8,128)(2,1)} %copy-done, bf16[768,3072]{1,0:T(8,128)(2,1)} %get-tuple-element.99.probe, f32[1024,3072]{1,0:T(8,128)} %get-tuple-element.100.begun, f32[1024,512]{1,0:T(8,128)} %bent.4, bf16[1536,1024]{1,0:T(8,128)(2,1)} %get-tuple-element.102.other), custom_call_target="tpu_custom_call" | custom-call | bytes 1024 | tf_op jit(solution)/shard_map/front/pallas_call | solution.py:226
  258.7 13.3 %front.5 = (bf16[1024,1024]{1,0:T(8,128)(2,1)}, bf16[1536,1024]{1,0:T(8,128)(2,1)}) custom-call(bf16[1024,768]{1,0:T(8,128)(2,1)} %copy-done, bf16[768,3072]{1,0:T(8,128)(2,1)} %get-tuple-element.99.probe, f32[1024,3072]{1,0:T(8,128)} %get-tuple-element.100.begun, f32[1024,1024]{1,0:T(8,128)} %bent.5, bf16[1536,1024]{1,0:T(8,128)(2,1)} %get-tuple-element.102.other), custom_call_target="tpu_custom_call" | custom-call | bytes 1024 | tf_op jit(solution)/shard_map/front/pallas_call | solution.py:226
  273.3 6.4 %back.4 = (f32[2,1,384,256]{3,2,1,0:T(8,128)}, f32[1,2,384,256]{3,2,1,0:T(8,128)}, bf16[2,1,384,256]{3,2,1,0:T(8,128)(2,1)}, bf16[1,2,384,256]{3,2,1,0:T(8,128)(2,1)}) custom-call(s32[2]{0:T(128)} %pad_add_fusion.me, bf16[1536,1024]{1,0:T(8,128)(2,1)} %get-tuple-element.98.mine, bf16[1024,512]{1,0:T(8,128)(2,1)} %get-tuple-element.110.mixed, ...), custom_call_target="tpu_custom_call" | custom-call | bytes 1024 | tf_op jit(solution)/shard_map/back/pallas_call | solution.py:287
  282.4 13.3 %front.6 = (bf16[1024,1024]{1,0:T(8,128)(2,1)}, bf16[1536,1024]{1,0:T(8,128)(2,1)}) custom-call(bf16[1024,768]{1,0:T(8,128)(2,1)} %copy-done, bf16[768,3072]{1,0:T(8,128)(2,1)} %get-tuple-element.99.probe, f32[1024,3072]{1,0:T(8,128)} %get-tuple-element.100.begun, f32[1024,1024]{1,0:T(8,128)} %bent.6, bf16[1536,1024]{1,0:T(8,128)(2,1)} %get-tuple-element.102.other), custom_call_target="tpu_custom_call" | custom-call | bytes 1024 | tf_op jit(solution)/shard_map/front/pallas_call | solution.py:226
  302.8 9.3 %back.5 = (f32[2,1,384,512]{3,2,1,0:T(8,128)}, f32[1,2,384,512]{3,2,1,0:T(8,128)}, bf16[2,1,384,512]{3,2,1,0:T(8,128)(2,1)}, bf16[1,2,384,512]{3,2,1,0:T(8,128)(2,1)}) custom-call(s32[2]{0:T(128)} %pad_add_fusion.me, bf16[1536,1024]{1,0:T(8,128)(2,1)} %get-tuple-element.98.mine, bf16[1024,1024]{1,0:T(8,128)(2,1)} %get-tuple-element.124.mixed, ...), custom_call_target="tpu_custom_call" | custom-call | bytes 1024 | tf_op jit(solution)/shard_map/back/pallas_call | solution.py:287
  314.4 8.7 %front.7 = (bf16[1024,512]{1,0:T(8,128)(2,1)}, bf16[1536,512]{1,0:T(8,128)(2,1)}) custom-call(bf16[1024,768]{1,0:T(8,128)(2,1)} %copy-done, bf16[768,3072]{1,0:T(8,128)(2,1)} %get-tuple-element.99.probe, f32[1024,3072]{1,0:T(8,128)} %get-tuple-element.100.begun, f32[1024,512]{1,0:T(8,128)} %bent.7, bf16[1536,1024]{1,0:T(8,128)(2,1)} %get-tuple-element.102.other), custom_call_target="tpu_custom_call" | custom-call | bytes 1024 | tf_op jit(solution)/shard_map/front/pallas_call | solution.py:226
  323.1 9.7 %collective-permute-done.21 = bf16[2,1,384,512]{3,2,1,0:T(8,128)(2,1)S(1)} collective-permute-done((bf16[2,1,384,512]{3,2,1,0:T(8,128)(2,1)}, bf16[2,1,384,512]{3,2,1,0:T(8,128)(2,1)S(1)}, u32[]{:S(2)}, u32[]{:S(2)}) %collective-permute-start.21) | collective-permute-done | bytes 786464 | tf_op jit(solution)/shard_map/ppermute | solution.py:365
  338.8 9.3 %back.6 = (f32[2,1,384,512]{3,2,1,0:T(8,128)}, f32[1,2,384,512]{3,2,1,0:T(8,128)}, bf16[2,1,384,512]{3,2,1,0:T(8,128)(2,1)}, bf16[1,2,384,512]{3,2,1,0:T(8,128)(2,1)}) custom-call(s32[2]{0:T(128)} %pad_add_fusion.me, bf16[1536,1024]{1,0:T(8,128)(2,1)} %get-tuple-element.98.mine, bf16[1024,1024]{1,0:T(8,128)(2,1)} %get-tuple-element.144.mixed, ...), custom_call_target="tpu_custom_call" | custom-call | bytes 1024 | tf_op jit(solution)/shard_map/back/pallas_call | solution.py:287
  352.1 14.1 %collective-permute-done.27 = bf16[1,2,384,512]{3,2,1,0:T(8,128)(2,1)} collective-permute-done((bf16[1,2,384,512]{3,2,1,0:T(8,128)(2,1)}, bf16[1,2,384,512]{3,2,1,0:T(8,128)(2,1)}, u32[]{:S(2)}, u32[]{:S(2)}) %collective-permute-start.27) | collective-permute-done | bytes 786464 | tf_op jit(solution)/shard_map/ppermute | solution.py:365
  375.1 6.5 %back.7 = (f32[2,1,384,256]{3,2,1,0:T(8,128)}, f32[1,2,384,256]{3,2,1,0:T(8,128)}, bf16[2,1,384,256]{3,2,1,0:T(8,128)(2,1)}, bf16[1,2,384,256]{3,2,1,0:T(8,128)(2,1)}) custom-call(s32[2]{0:T(128)} %pad_add_fusion.me, bf16[1536,1024]{1,0:T(8,128)(2,1)} %get-tuple-element.98.mine, bf16[1024,512]{1,0:T(8,128)(2,1)} %get-tuple-element.157.mixed, ...), custom_call_target="tpu_custom_call" | custom-call | bytes 1024 | tf_op jit(solution)/shard_map/back/pallas_call | solution.py:287
  385.9 4.8 %collective-permute-done.31 = bf16[2,1,384,256]{3,2,1,0:T(8,128)(2,1)S(1)} collective-permute-done((bf16[2,1,384,256]{3,2,1,0:T(8,128)(2,1)}, bf16[2,1,384,256]{3,2,1,0:T(8,128)(2,1)S(1)}, u32[]{:S(2)}, u32[]{:S(2)}) %collective-permute-start.31) | collective-permute-done | bytes 393248 | tf_op jit(solution)/shard_map/ppermute | solution.py:365
  (153 shorter events, 69.5 us)
Async XLA Ops:
  6.5 189.5 %all-gather.2.cloned.1.call-start = ((), (), s32[]{:S(2)}) async-start(), calls=%async_computation | async-start | bytes 21233664 | tf_op jit(solution)/shard_map/all_gather | solution.py:383
  7.3 85.7 %collective-permute-start.5 = (bf16[384,3072]{1,0:T(8,128)(2,1)}, bf16[384,3072]{1,0:T(8,128)(2,1)}, u32[]{:S(2)}, u32[]{:S(2)}) collective-permute-start(bf16[384,3072]{1,0:T(8,128)(2,1)} %refs_0_.7), channel_id=1, source_target_pairs={{0,8},{4,12},{8,0},{12,4},{16,24},{20,28},{24,16},{28,20},{1,9},{5... | collective-permute-start | bytes 7077896 | tf_op jit(solution)/shard_map/ppermute | solution.py:365
  10.3 38.2 %collective-permute-start = (bf16[1024,768]{1,0:T(8,128)(2,1)S(1)}, bf16[1024,768]{1,0:T(8,128)(2,1)S(1)}, u32[]{:S(2)}, u32[]{:S(2)}) collective-permute-start(bf16[1024,768]{1,0:T(8,128)(2,1)S(1)} %copy-done.1), channel_id=1, source_target_pairs={{0,1},{1,3},{3,2},{2,0},{4,5},{5,7},{7,6},{6,4},{8,9},{9,11},{11,1... | collective-permute-start | bytes 4718600 | tf_op jit(solution)/shard_map/ppermute | solution.py:319
  11.9 68.9 %collective-permute-start.1 = (bf16[1024,768]{1,0:T(8,128)(2,1)}, bf16[1024,768]{1,0:T(8,128)(2,1)S(1)}, u32[]{:S(2)}, u32[]{:S(2)}) collective-permute-start(bf16[1024,768]{1,0:T(8,128)(2,1)} %refs_10_.1), channel_id=1, source_target_pairs={{0,1},{1,3},{3,2},{2,0},{4,5},{5,7},{7,6},{6,4},{8,9},{9,11},{11,1... | collective-permute-start | bytes 4718600 | tf_op jit(solution)/shard_map/ppermute | solution.py:319
  14.4 91.2 %collective-permute-start.7 = (bf16[384,3072]{1,0:T(8,128)(2,1)}, bf16[384,3072]{1,0:T(8,128)(2,1)}, u32[]{:S(2)}, u32[]{:S(2)}) collective-permute-start(bf16[384,3072]{1,0:T(8,128)(2,1)} %refs_0_.7), channel_id=1, source_target_pairs={{0,16},{4,20},{8,24},{12,28},{16,0},{20,4},{24,8},{28,12},{1,17},{... | collective-permute-start | bytes 7077896 | tf_op jit(solution)/shard_map/ppermute | solution.py:365
  80.7 73.3 %collective-permute-start.2 = (bf16[1024,768]{1,0:T(8,128)(2,1)S(1)}, bf16[1024,768]{1,0:T(8,128)(2,1)S(1)}, u32[]{:S(2)}, u32[]{:S(2)}) collective-permute-start(bf16[1024,768]{1,0:T(8,128)(2,1)S(1)} %collective-permute-done.refs_1_), channel_id=1, source_target_pairs={{0,1},{1,3},{3,2},{2,0},{4,5},{5,7},{7,6},{6,4},{8,9},{9,11},{11,1... | collective-permute-start | bytes 4718600 | tf_op jit(solution)/shard_map/ppermute | solution.py:319
  81.6 72.9 %collective-permute-start.3 = (bf16[1024,768]{1,0:T(8,128)(2,1)S(1)}, bf16[1024,768]{1,0:T(8,128)(2,1)}, u32[]{:S(2)}, u32[]{:S(2)}) collective-permute-start(bf16[1024,768]{1,0:T(8,128)(2,1)S(1)} %collective-permute-done.1.refs_1_.refs_11_), channel_id=1, source_target_pairs={{0,1},{1,3},{3,2},{2,0},{4,5},{5,7},{7,6},{6,4},{8,9},{9,11},{11,1... | collective-permute-start | bytes 4718600 | tf_op jit(solution)/shard_map/ppermute | solution.py:319
  84.9 69.7 %collective-permute-start.4 = (bf16[384,3072]{1,0:T(8,128)(2,1)}, bf16[384,3072]{1,0:T(8,128)(2,1)S(1)}, u32[]{:S(2)}, u32[]{:S(2)}) collective-permute-start(bf16[384,3072]{1,0:T(8,128)(2,1)} %refs_0_.7), channel_id=1, source_target_pairs={{0,4},{4,0},{8,12},{12,8},{16,20},{20,16},{24,28},{28,24},{1,5},{5... | collective-permute-start | bytes 7077896 | tf_op jit(solution)/shard_map/ppermute | solution.py:323
  94.3 59.7 %collective-permute-start.9 = (bf16[192,3072]{1,0:T(8,128)(2,1)S(1)}, bf16[192,3072]{1,0:T(8,128)(2,1)S(1)}, u32[]{:S(2)}, u32[]{:S(2)}) collective-permute-start(bf16[192,3072]{1,0:T(8,128)(2,1)S(1)} %slice.56), channel_id=1, source_target_pairs={{0,16},{4,20},{8,24},{12,28},{16,0},{20,4},{24,8},{28,12},{1,17},{... | collective-permute-start | bytes 3538952 | tf_op jit(solution)/shard_map/ppermute | solution.py:365
  107.0 51.2 %collective-permute-start.11 = (bf16[192,3072]{1,0:T(8,128)(2,1)S(1)}, bf16[192,3072]{1,0:T(8,128)(2,1)}, u32[]{:S(2)}, u32[]{:S(2)}) collective-permute-start(bf16[192,3072]{1,0:T(8,128)(2,1)S(1)} %slice.57), channel_id=1, source_target_pairs={{0,8},{4,12},{8,0},{12,4},{16,24},{20,28},{24,16},{28,20},{1,9},{5... | collective-permute-start | bytes 3538952 | tf_op jit(solution)/shard_map/ppermute | solution.py:365
  154.1 14.9 %collective-permute-start.6 = (bf16[384,3072]{1,0:T(8,128)(2,1)}, bf16[384,3072]{1,0:T(8,128)(2,1)}, u32[]{:S(2)}, u32[]{:S(2)}) collective-permute-start(bf16[384,3072]{1,0:T(8,128)(2,1)} %collective-permute-done.5.refs_2_), channel_id=1, source_target_pairs={{0,4},{4,0},{8,12},{12,8},{16,20},{20,16},{24,28},{28,24},{1,5},{5... | collective-permute-start | bytes 7077896 | tf_op jit(solution)/shard_map/ppermute | solution.py:323
  154.6 14.4 %collective-permute-start.8 = (bf16[384,3072]{1,0:T(8,128)(2,1)}, bf16[384,3072]{1,0:T(8,128)(2,1)}, u32[]{:S(2)}, u32[]{:S(2)}) collective-permute-start(bf16[384,3072]{1,0:T(8,128)(2,1)} %collective-permute-done.7.refs_4_), channel_id=1, source_target_pairs={{0,4},{4,0},{8,12},{12,8},{16,20},{20,16},{24,28},{28,24},{1,5},{5... | collective-permute-start | bytes 7077896 | tf_op jit(solution)/shard_map/ppermute | solution.py:323
  154.7 41.4 %collective-permute-start.13 = (bf16[1024,768]{1,0:T(8,128)(2,1)S(1)}, bf16[1024,768]{1,0:T(8,128)(2,1)}, u32[]{:S(2)}, u32[]{:S(2)}) collective-permute-start(bf16[1024,768]{1,0:T(8,128)(2,1)S(1)} %collective-permute-done.2.refs_2_), channel_id=1, source_target_pairs={{0,1},{1,3},{3,2},{2,0},{4,5},{5,7},{7,6},{6,4},{8,9},{9,11},{11,1... | collective-permute-start | bytes 4718600 | tf_op jit(solution)/shard_map/ppermute | solution.py:319
  158.2 86.8 %collective-permute-start.14 = (bf16[1024,768]{1,0:T(8,128)(2,1)}, bf16[1024,768]{1,0:T(8,128)(2,1)S(1)}, u32[]{:S(2)}, u32[]{:S(2)}) collective-permute-start(bf16[1024,768]{1,0:T(8,128)(2,1)} %collective-permute-done.3.refs_2_.refs_12_), channel_id=1, source_target_pairs={{0,1},{1,3},{3,2},{2,0},{4,5},{5,7},{7,6},{6,4},{8,9},{9,11},{11,1... | collective-permute-start | bytes 4718600 | tf_op jit(solution)/shard_map/ppermute | solution.py:319
  272.1 29.1 %collective-permute-start.18 = (bf16[1536,1024]{1,0:T(8,128)(2,1)}, bf16[1536,1024]{1,0:T(8,128)(2,1)S(1)}, u32[]{:S(2)}, u32[]{:S(2)}) collective-permute-start(bf16[1536,1024]{1,0:T(8,128)(2,1)} %get-tuple-element.125), channel_id=1, source_target_pairs={{0,4},{4,0},{8,12},{12,8},{16,20},{20,16},{24,28},{28,24},{1,5},{5... | collective-permute-start | bytes 9437192 | tf_op jit(solution)/shard_map/ppermute | solution.py:323
  279.7 16.0 %collective-permute-start.16 = (bf16[2,1,384,256]{3,2,1,0:T(8,128)(2,1)}, bf16[2,1,384,256]{3,2,1,0:T(8,128)(2,1)S(1)}, u32[]{:S(2)}, u32[]{:S(2)}) collective-permute-start(bf16[2,1,384,256]{3,2,1,0:T(8,128)(2,1)} %get-tuple-element.116), channel_id=1, source_target_pairs={{0,8},{4,12},{8,0},{12,4},{16,24},{20,28},{24,16},{28,20},{1,9},{5... | collective-permute-start | bytes 1179656 | tf_op jit(solution)/shard_map/ppermute | solution.py:365
  279.9 15.8 %collective-permute-start.17 = (bf16[1,2,384,256]{3,2,1,0:T(8,128)(2,1)}, bf16[1,2,384,256]{3,2,1,0:T(8,128)(2,1)}, u32[]{:S(2)}, u32[]{:S(2)}) collective-permute-start(bf16[1,2,384,256]{3,2,1,0:T(8,128)(2,1)} %get-tuple-element.117), channel_id=1, source_target_pairs={{0,16},{4,20},{8,24},{12,28},{16,0},{20,4},{24,8},{28,12},{1,17},{... | collective-permute-start | bytes 1179656 | tf_op jit(solution)/shard_map/ppermute | solution.py:365
  295.7 43.1 %collective-permute-start.23 = (bf16[1536,1024]{1,0:T(8,128)(2,1)}, bf16[1536,1024]{1,0:T(8,128)(2,1)}, u32[]{:S(2)}, u32[]{:S(2)}) collective-permute-start(bf16[1536,1024]{1,0:T(8,128)(2,1)} %get-tuple-element.145), channel_id=1, source_target_pairs={{0,4},{4,0},{8,12},{12,8},{16,20},{20,16},{24,28},{28,24},{1,5},{5... | collective-permute-start | bytes 9437192 | tf_op jit(solution)/shard_map/ppermute | solution.py:323
  298.5 13.6 %collective-permute-start.19 = (bf16[1,1,384,256]{3,2,1,0:T(8,128)(2,1)S(1)}, bf16[1,1,384,256]{3,2,1,0:T(8,128)(2,1)S(1)}, u32[]{:S(2)}, u32[]{:S(2)}) collective-permute-start(bf16[1,1,384,256]{3,2,1,0:T(8,128)(2,1)S(1)} %get-tuple-element.128), channel_id=1, source_target_pairs={{0,16},{4,20},{8,24},{12,28},{16,0},{20,4},{24,8},{28,12},{1,17},{... | collective-permute-start | bytes 589832 | tf_op jit(solution)/shard_map/ppermute | solution.py:337
  312.9 19.8 %collective-permute-start.21 = (bf16[2,1,384,512]{3,2,1,0:T(8,128)(2,1)}, bf16[2,1,384,512]{3,2,1,0:T(8,128)(2,1)S(1)}, u32[]{:S(2)}, u32[]{:S(2)}) collective-permute-start(bf16[2,1,384,512]{3,2,1,0:T(8,128)(2,1)} %get-tuple-element.136), channel_id=1, source_target_pairs={{0,8},{4,12},{8,0},{12,4},{16,24},{20,28},{24,16},{28,20},{1,9},{5... | collective-permute-start | bytes 2359304 | tf_op jit(solution)/shard_map/ppermute | solution.py:365
  313.1 19.6 %collective-permute-start.22 = (bf16[1,2,384,512]{3,2,1,0:T(8,128)(2,1)}, bf16[1,2,384,512]{3,2,1,0:T(8,128)(2,1)S(1)}, u32[]{:S(2)}, u32[]{:S(2)}) collective-permute-start(bf16[1,2,384,512]{3,2,1,0:T(8,128)(2,1)} %get-tuple-element.137), channel_id=1, source_target_pairs={{0,16},{4,20},{8,24},{12,28},{16,0},{20,4},{24,8},{28,12},{1,17},{... | collective-permute-start | bytes 2359304 | tf_op jit(solution)/shard_map/ppermute | solution.py:365
  348.2 18.0 %collective-permute-start.27 = (bf16[1,2,384,512]{3,2,1,0:T(8,128)(2,1)}, bf16[1,2,384,512]{3,2,1,0:T(8,128)(2,1)}, u32[]{:S(2)}, u32[]{:S(2)}) collective-permute-start(bf16[1,2,384,512]{3,2,1,0:T(8,128)(2,1)} %get-tuple-element.155), channel_id=1, source_target_pairs={{0,16},{4,20},{8,24},{12,28},{16,0},{20,4},{24,8},{28,12},{1,17},{... | collective-permute-start | bytes 2359304 | tf_op jit(solution)/shard_map/ppermute | solution.py:365
  349.3 19.2 %collective-permute-start.26 = (bf16[2,1,384,512]{3,2,1,0:T(8,128)(2,1)}, bf16[2,1,384,512]{3,2,1,0:T(8,128)(2,1)S(1)}, u32[]{:S(2)}, u32[]{:S(2)}) collective-permute-start(bf16[2,1,384,512]{3,2,1,0:T(8,128)(2,1)} %get-tuple-element.153), channel_id=1, source_target_pairs={{0,8},{4,12},{8,0},{12,4},{16,24},{20,28},{24,16},{28,20},{1,9},{5... | collective-permute-start | bytes 2359304 | tf_op jit(solution)/shard_map/ppermute | solution.py:365
  351.0 24.2 %collective-permute-start.28 = (bf16[1536,512]{1,0:T(8,128)(2,1)}, bf16[1536,512]{1,0:T(8,128)(2,1)}, u32[]{:S(2)}, u32[]{:S(2)}) collective-permute-start(bf16[1536,512]{1,0:T(8,128)(2,1)} %get-tuple-element.158), channel_id=1, source_target_pairs={{0,4},{4,0},{8,12},{12,8},{16,20},{20,16},{24,28},{28,24},{1,5},{5... | collective-permute-start | bytes 4718600 | tf_op jit(solution)/shard_map/ppermute | solution.py:323
  (41 other events, 589.6 us)
Sparse Core Ops, SparseCore 0:
  9.2 161.3 all-gather.1

commit v4 on v3

--- a/solution.py
+++ b/solution.py
@@ -12,7 +12,6 @@
 sixths = (1, 2, 2, 1)
 f32 = jnp.float32
 bf16 = jnp.bfloat16
-vmem = 56 * 1024 * 1024
 
 
 def folded(n):
@@ -30,8 +29,8 @@
 light = pl.CostEstimate(flops=0, bytes_accessed=1024, transcendentals=0)
 
 
-def params():
-    return pltpu.CompilerParams(vmem_limit_bytes=vmem)
+def params(mib):
+    return pltpu.CompilerParams(vmem_limit_bytes=mib * 1024 * 1024)
 
 
 def split_body(count, half, core, at, *refs):
@@ -70,7 +69,7 @@
         ),
         out_shape=[shape, shape],
         input_output_aliases={2 + count: 0, 3 + count: 1} if before else {},
-        compiler_params=params(),
+        compiler_params=params(16),
         cost_estimate=light,
         name="split_cores",
     )(core.reshape(1), at, *pieces, *before)
@@ -89,7 +88,9 @@
 
 
 def whole(shape):
-    return pl.BlockSpec(shape, lambda *_: (0,) * len(shape))
+    return pl.BlockSpec(
+        shape, lambda *_: (0,) * len(shape), pipeline_mode=pl.Buffered(buffer_count=1)
+    )
 
 
 def bent_body(count, parts, width, at, scale, codes, down, *refs):
@@ -112,13 +113,12 @@
         out[rows, :] = total * (jnp.exp(-0.5 * square) * inv_root * (2.0 - square))
 
 
-def bent_of(shards, at, row_scale, codes, down_full, first, wide):
+def bent_of(shards, at, row_scale, codes, down_full):
     count, parts = len(shards), len(shards[0])
     tall, width = shards[0][0].shape
     tok = tall * parts
-    feats = down_full.shape[1]
-    tile = math.gcd(wide, math.gcd(first, 512))
-    base = first // tile
+    wide, feats = down_full.shape
+    tile = math.gcd(wide, 512)
     return pl.pallas_call(
         functools.partial(bent_body, count, parts, width),
         grid_spec=pltpu.PrefetchScalarGridSpec(
@@ -126,14 +126,14 @@
             grid=(wide // tile,),
             in_specs=[
                 whole((tok, 1)),
-                pl.BlockSpec((tok, tile), lambda j, at: (0, base + j)),
-                pl.BlockSpec((tile, feats), lambda j, at: (base + j, 0)),
+                pl.BlockSpec((tok, tile), lambda j, at: (0, j)),
+                pl.BlockSpec((tile, feats), lambda j, at: (j, 0)),
             ]
             + [whole((tall, width))] * (count * parts),
             out_specs=pl.BlockSpec((tok, tile), lambda j, at: (0, j)),
         ),
         out_shape=jax.ShapeDtypeStruct((tok, wide), f32),
-        compiler_params=params(),
+        compiler_params=params(32),
         cost_estimate=light,
         name="bent",
     )(at, row_scale[:, None], codes, down_full, *[p for piece in shards for p in piece])
@@ -205,7 +205,7 @@
             jax.ShapeDtypeStruct((tok, hidden), f32),
             jax.ShapeDtypeStruct((width, hidden), bf16),
         ],
-        compiler_params=params(),
+        compiler_params=params(36),
         cost_estimate=light,
         name="partial_tangent",
     )(at, slots, *arrays, *[p for piece in shards for p in piece])
@@ -217,9 +217,8 @@
     away[...] = jnp.dot(other[...], mixed[...], preferred_element_type=f32).astype(bf16)
 
 
-def front_of(shard, last, begun, bent, other, first):
+def front_of(shard, last, begun, bent, other, first, wide):
     tok, width = shard.shape
-    wide = bent.shape[1]
     half = other.shape[0]
     tile = math.gcd(wide, math.gcd(first, 256))
     base = first // tile
@@ -230,7 +229,7 @@
             whole((tok, width)),
             pl.BlockSpec((width, tile), lambda j: (0, base + j)),
             pl.BlockSpec((tok, tile), lambda j: (0, base + j)),
-            pl.BlockSpec((tok, tile), lambda j: (0, j)),
+            pl.BlockSpec((tok, tile), lambda j: (0, base + j)),
             whole(other.shape),
         ],
         out_specs=[
@@ -241,7 +240,7 @@
             jax.ShapeDtypeStruct((tok, wide), bf16),
             jax.ShapeDtypeStruct((half, wide), bf16),
         ],
-        compiler_params=params(),
+        compiler_params=params(20),
         cost_estimate=light,
         name="front",
     )(shard, last, begun, bent, other)
@@ -302,7 +301,7 @@
         out_shape=[
             jax.ShapeDtypeStruct(shape + (side,), kind) for shape, kind in zip(shapes, kinds)
         ],
-        compiler_params=params(),
+        compiler_params=params(18),
         cost_estimate=light,
         name="back",
     )(jnp.stack([x, y]), mine, mixed, came)
@@ -404,13 +403,8 @@
     if not plain:
         early = list(split_cores(tok[:-1], at[:-1], core, tp))
         early[0], cot[-1] = after(early[0], cot[-1])
-    bent = [
-        bent_of(
-            [[c] for c in cot], at, row_scale, codes, down_full, edges[j], edges[j + 1] - edges[j]
-        )
-        for j in range(len(sixths))
-    ]
-    *bent, tok[-1] = lax.optimization_barrier((*bent, tok[-1]))
+    bent = bent_of([[c] for c in cot], at, row_scale, codes, down_full)
+    bent, tok[-1] = lax.optimization_barrier((bent, tok[-1]))
     if plain:
         mine, other = split_plain(tok, at, core)
     else:
@@ -425,15 +419,15 @@
             hessian = summed(keeps[k], arrived[k]).reshape(rows, b - a)
             out[2 * j + k] = probe[:, a:b].astype(f32) * hessian * (1.0 / (tok_rows * dp))
 
-    def front(j):
-        return front_of(tok[-1], last, begun, bent[j], other, edges[j])
-
-    fronts = {0: front(0)}
+    def front(j, ready):
+        return front_of(tok[-1], ready, begun, bent, other, edges[j], edges[j + 1] - edges[j])
+
+    fronts = {0: front(0, last)}
     came = {0: swapped(fronts[0][1], dp, cores)}
     mixed = fronts[0][0]
     if count > 1:
-        mixed, bent[1] = lax.optimization_barrier((mixed, bent[1]))
-        following, away = front(1)
+        mixed, last = lax.optimization_barrier((mixed, last))
+        following, away = front(1, last)
         mixed, following, away, came[0] = lax.optimization_barrier(
             (mixed, following, away, came[0])
         )
@@ -447,11 +441,11 @@
             finish(j - 1, keeps, arrived)
         ahead = j + 2 < count
         if ahead:
-            to_x, to_y, bent[j + 2] = lax.optimization_barrier((to_x, to_y, bent[j + 2]))
+            to_x, to_y, last = lax.optimization_barrier((to_x, to_y, last))
         from_x = [over(to_x[:, i - 1 : i], x_way, i) for i in range(1, xs)]
         from_y = [over(to_y[k - 1 : k], y_way, k) for k in range(1, ys)]
         if ahead:
-            beyond, away = front(j + 2)
+            beyond, away = front(j + 2, last)
             from_x, from_y, away = lax.optimization_barrier((from_x, from_y, away))
             came[j + 2] = swapped(away, dp, cores)
         left, left_sends = parted(summed(keep_x, from_x), 0, ys, y)

time: 407 us -> 392 us (0.963)
  Pallas kernels: 161 us -> 116 us
  local copies, waits for them, and re-layouts: 18.5 us -> 51 us
    unnamed x58 -> x116, local copies, waits for them, and re-layouts: 9.84 us -> 46.3 us
    pallas_call x4 -> x1, Pallas kernels: 48.9 us -> 28 us  [bent_of(): pl.pallas_call(functools.partial(bent_body, count, parts, width), grid_sp...]
    pallas_call x4, Pallas kernels: 31.5 us -> 19 us  [back_of(): pl.pallas_call(functools.partial(back_body, xs, ys, rows, steps), grid_sp...]
    pallas_call x4, Pallas kernels: 44.3 us -> 37.1 us  [front_of(): pl.pallas_call(front_body, grid=(wide // tile,), in_specs=[whole((tok, wi...]
    ppermute x12, waiting for transfers between devices: 97 us -> 91.8 us  [over(): return lax.ppermute(block, 'dp', shift(way[0], way[1], dp, by))]
    ppermute x8, waiting for transfers between devices: 3.01 us -> 7.72 us  [sent(): lax.ppermute(send, 'dp', shift(n, stride, total, by + 1))]
  transfers between devices with their start and end apart: 36 -> 36, of which waited for: 11 -> 14; matrix products, arithmetic and copies ran while one was open for 5% -> 4% of each run, Pallas kernels for 37% -> 27%
where the time goes in v4:
time: 392 us; the launch traced here: 391 us
  waiting for transfers between devices  165 us (42%)
  Pallas kernels  116 us (30%)
  local copies, waits for them, and re-layouts  51 us (13%)
  starting transfers between devices  35 us (9%)
  between operations  14 us (4%)
  other arithmetic  10.3 us (3%)
    ppermute x12, waiting for transfers between devices, over(): return lax.ppermute(block, 'dp', shift(way[0], way[1], dp, by))  91.8 us
    ppermute x6, waiting for transfers between devices, ring_step(): return lax.ppermute(block, 'tensor', pairs)  65 us
    unnamed x116, local copies, waits for them, and re-layouts  46.3 us
    pallas_call x4, Pallas kernels, front_of(): pl.pallas_call(front_body, grid=(wide // tile,), in_specs=[whole((tok, wi...  37.1 us
    pallas_call x1, Pallas kernels, bent_of(): pl.pallas_call(functools.partial(bent_body, count, parts, width), grid_sp...  28 us
    pallas_call x1, Pallas kernels, partial_tangent(): pl.pallas_call(functools.partial(partial_body, count, parts, width, spots...  24.4 us
    pallas_call x4, Pallas kernels, back_of(): pl.pallas_call(functools.partial(back_body, xs, ys, rows, steps), grid_sp...  19 us
    ppermute x12, starting transfers between devices, over(): return lax.ppermute(block, 'dp', shift(way[0], way[1], dp, by))  14.4 us
  transfers between devices with their start and end apart: 36, of which 14 were waited for; matrix products, arithmetic and copies ran while one was open for 4% of the time, Pallas kernels for 27%

profile of v4, /device:TPU:0, one launch (start us, length us, event | category | flops | bytes accessed | tf_op | source)
XLA Modules:
  0.0 391.3 jit_solution(12279869672696705534)
XLA Ops:
  8.2 2.9 collective-permute-start.5
  16.8 32.7 %collective-permute-done.refs_1_ = bf16[1024,768]{1,0:T(8,128)(2,1)S(1)} collective-permute-done((bf16[1024,768]{1,0:T(8,128)(2,1)}, bf16[1024,768]{1,0:T(8,128)(2,1)S(1)}, u32[]{:S(2)}, u32[]{:S(2)}) %collective-permute-start) | collective-permute-done | bytes 1572896 | tf_op jit(solution)/shard_map/ppermute | solution.py:318
  49.6 32.2 %collective-permute-done.1.refs_1_.refs_11_ = bf16[1024,768]{1,0:T(8,128)(2,1)S(1)} collective-permute-done((bf16[1024,768]{1,0:T(8,128)(2,1)}, bf16[1024,768]{1,0:T(8,128)(2,1)S(1)}, u32[]{:S(2)}, u32[]{:S(2)}) %collective-permute-start.1) | collective-permute-done | bytes 1572896 | tf_op jit(solution)/shard_map/ppermute | solution.py:318
  82.7 3.3 collective-permute-start.2
  86.0 8.2 %collective-permute-done.5.refs_2_ = bf16[384,3072]{1,0:T(8,128)(2,1)} collective-permute-done((bf16[384,3072]{1,0:T(8,128)(2,1)S(1)}, bf16[384,3072]{1,0:T(8,128)(2,1)}, u32[]{:S(2)}, u32[]{:S(2)}) %collective-permute-start.5) | collective-permute-done | bytes 2359328 | tf_op jit(solution)/shard_map/ppermute | solution.py:364
  97.1 9.7 %collective-permute-done.7.refs_4_ = bf16[384,3072]{1,0:T(8,128)(2,1)} collective-permute-done((bf16[384,3072]{1,0:T(8,128)(2,1)S(1)}, bf16[384,3072]{1,0:T(8,128)(2,1)}, u32[]{:S(2)}, u32[]{:S(2)}) %collective-permute-start.7) | collective-permute-done | bytes 2359328 | tf_op jit(solution)/shard_map/ppermute | solution.py:364
  108.3 47.1 %collective-permute-done.9.refs_6_ = bf16[192,3072]{1,0:T(8,128)(2,1)S(1)} collective-permute-done((bf16[192,3072]{1,0:T(8,128)(2,1)S(1)}, bf16[192,3072]{1,0:T(8,128)(2,1)S(1)}, u32[]{:S(2)}, u32[]{:S(2)}) %collective-permute-start.9) | collective-permute-done | bytes 1179680 | tf_op jit(solution)/shard_map/ppermute | solution.py:364
  165.0 4.2 %split_cores.2 = (bf16[1536,1024]{1,0:T(8,128)(2,1)S(1)}, bf16[1536,1024]{1,0:T(8,128)(2,1)S(1)}) custom-call(s32[1]{0:T(128)} %bitcast.2.core, s32[3]{0:T(128)S(1)} %slice_bitcast_fusion.at, bf16[1024,768]{1,0:T(8,128)(2,1)S(1)} %copy-done.18, bf16[1024,768]{1,0:T(8,128)(2,1)S(1)} %copy-done.21, bf16[1024,768]{1,0:T(8,128)(2,1)} %collective-permute-done.3.refs_2_.refs_12_), custom_call_target="tpu_custom_call" | custom-call | bytes 1024 | tf_op jit(solution)/shard_map/split_cores/pallas_call | solution.py:57
  175.5 24.4 %partial_tangent.1 = (f32[1024,3072]{1,0:T(8,128)}, bf16[768,3072]{1,0:T(8,128)(2,1)}) custom-call(s32[4]{0:T(128)S(1)} %get-tuple-element.163.at, s32[10]{0:T(128)S(1)} %stack.64.slots, bf16[384,3072]{1,0:T(8,128)(2,1)S(1)} %copy-done.16, bf16[384,3072]{1,0:T(8,128)(2,1)S(1)} %copy-done.24, bf16[384,3072]{1,0:T(8,128)(2,1)} %collective-permute-done.5.refs_2_, ...), custom_call_target="tpu_custom_call" | custom-call | bytes 1024 | tf_op jit(solution)/shard_map/partial_tangent/pallas_call | solution.py:186
  202.8 28.0 %bent.1 = f32[1024,3072]{1,0:T(8,128)S(1)} custom-call(s32[4]{0:T(128)S(1)} %get-tuple-element.163.at, f32[1024,1]{1,0:T(8,128)S(1)} %copy.10.scale, s32[1024,3072]{1,0:T(8,128)} %codes.1, bf16[3072,3072]{1,0:T(8,128)(2,1)} %all-gather.2.cloned.1.call-done.down, bf16[1024,768]{1,0:T(8,128)(2,1)S(1)} %copy-done.29, bf16[1024,768]{1,0:T(8,128)(2,1)S(1)} %copy-done.31, ...), custom_call_target="tpu_custom_call" | custom-call | bytes 1024 | tf_op jit(solution)/shard_map/bent/pallas_call | solution.py:122
  230.8 4.6 %copy-done = f32[1024,3072]{1,0:T(8,128)} copy-done((f32[1024,3072]{1,0:T(8,128)}, f32[1024,3072]{1,0:T(8,128)S(1)}, u32[]{:S(2)}) %copy-start) | copy-done | bytes 12582936
  239.1 3.0 split_cores.3
  247.3 6.4 %front.4 = (bf16[1024,512]{1,0:T(8,128)(2,1)S(1)}, bf16[1536,512]{1,0:T(8,128)(2,1)S(1)}) custom-call(bf16[1024,768]{1,0:T(8,128)(2,1)} %collective-permute-done.14.refs_0_.shard, bf16[768,3072]{1,0:T(8,128)(2,1)S(1)} %copy-done.14, f32[1024,3072]{1,0:T(8,128)S(1)} %copy-done.1, f32[1024,3072]{1,0:T(8,128)} %copy-done, bf16[1536,1024]{1,0:T(8,128)(2,1)S(1)} %copy-done.6), custom_call_target="tpu_custom_call" | custom-call | bytes 1024 | tf_op jit(solution)/shard_map/front/pallas_call | solution.py:225
  254.4 12.2 %front.5 = (bf16[1024,1024]{1,0:T(8,128)(2,1)S(1)}, bf16[1536,1024]{1,0:T(8,128)(2,1)}) custom-call(bf16[1024,768]{1,0:T(8,128)(2,1)} %collective-permute-done.14.refs_0_.shard, bf16[768,3072]{1,0:T(8,128)(2,1)S(1)} %copy-done.14, f32[1024,3072]{1,0:T(8,128)S(1)} %copy-done.1, f32[1024,3072]{1,0:T(8,128)} %copy-done, bf16[1536,1024]{1,0:T(8,128)(2,1)S(1)} %copy-done.6), custom_call_target="tpu_custom_call" | custom-call | bytes 1024 | tf_op jit(solution)/shard_map/front/pallas_call | solution.py:225
  270.5 3.1 collective-permute-start.17
  273.6 12.1 %front.6 = (bf16[1024,1024]{1,0:T(8,128)(2,1)S(1)}, bf16[1536,1024]{1,0:T(8,128)(2,1)}) custom-call(bf16[1024,768]{1,0:T(8,128)(2,1)} %collective-permute-done.14.refs_0_.shard, bf16[768,3072]{1,0:T(8,128)(2,1)S(1)} %copy-done.14, f32[1024,3072]{1,0:T(8,128)S(1)} %copy-done.1, f32[1024,3072]{1,0:T(8,128)} %copy-done, bf16[1536,1024]{1,0:T(8,128)(2,1)S(1)} %copy-done.7), custom_call_target="tpu_custom_call" | custom-call | bytes 1024 | tf_op jit(solution)/shard_map/front/pallas_call | solution.py:225
  294.6 6.4 %back.5 = (f32[2,1,384,512]{3,2,1,0:T(8,128)S(1)}, f32[1,2,384,512]{3,2,1,0:T(8,128)S(1)}, bf16[2,1,384,512]{3,2,1,0:T(8,128)(2,1)S(1)}, bf16[1,2,384,512]{3,2,1,0:T(8,128)(2,1)S(1)}) custom-call(s32[2]{0:T(128)S(1)} %pad_add_fusion.me, bf16[1536,1024]{1,0:T(8,128)(2,1)S(1)} %copy-done.13, bf16[1024,1024]{1,0:T(8,128)(2,1)S(1)} %copy-done.28, ...), custom_call_target="tpu_custom_call" | custom-call | bytes 1024 | tf_op jit(solution)/shard_map/back/pallas_call | solution.py:286
  303.6 4.6 %copy-done.2 = f32[1024,3072]{1,0:T(8,128)S(1)} copy-done((f32[1024,3072]{1,0:T(8,128)S(1)}, f32[1024,3072]{1,0:T(8,128)}, u32[]{:S(2)}) %copy-start.2) | copy-done | bytes 12582936
  310.5 6.4 %front.7 = (bf16[1024,512]{1,0:T(8,128)(2,1)S(1)}, bf16[1536,512]{1,0:T(8,128)(2,1)S(1)}) custom-call(bf16[1024,768]{1,0:T(8,128)(2,1)} %collective-permute-done.14.refs_0_.shard, bf16[768,3072]{1,0:T(8,128)(2,1)S(1)} %copy-done.15, f32[1024,3072]{1,0:T(8,128)S(1)} %copy-done.2, f32[1024,3072]{1,0:T(8,128)} %copy-done, bf16[1536,1024]{1,0:T(8,128)(2,1)S(1)} %copy-done.8), custom_call_target="tpu_custom_call" | custom-call | bytes 1024 | tf_op jit(solution)/shard_map/front/pallas_call | solution.py:225
  317.0 4.3 %collective-permute-done.21 = bf16[2,1,384,512]{3,2,1,0:T(8,128)(2,1)S(1)} collective-permute-done((bf16[2,1,384,512]{3,2,1,0:T(8,128)(2,1)S(1)}, bf16[2,1,384,512]{3,2,1,0:T(8,128)(2,1)S(1)}, u32[]{:S(2)}, u32[]{:S(2)}) %collective-permute-start.21) | collective-permute-done | bytes 786464 | tf_op jit(solution)/shard_map/ppermute | solution.py:364
  326.3 7.1 %back.6 = (f32[2,1,384,512]{3,2,1,0:T(8,128)S(1)}, f32[1,2,384,512]{3,2,1,0:T(8,128)S(1)}, bf16[2,1,384,512]{3,2,1,0:T(8,128)(2,1)S(1)}, bf16[1,2,384,512]{3,2,1,0:T(8,128)(2,1)}) custom-call(s32[2]{0:T(128)S(1)} %pad_add_fusion.me, bf16[1536,1024]{1,0:T(8,128)(2,1)S(1)} %copy-done.13, bf16[1024,1024]{1,0:T(8,128)(2,1)S(1)} %copy-done.26, ...), custom_call_target="tpu_custom_call" | custom-call | bytes 1024 | tf_op jit(solution)/shard_map/back/pallas_call | solution.py:286
  340.8 13.8 %collective-permute-done.27 = bf16[1,2,384,512]{3,2,1,0:T(8,128)(2,1)} collective-permute-done((bf16[1,2,384,512]{3,2,1,0:T(8,128)(2,1)}, bf16[1,2,384,512]{3,2,1,0:T(8,128)(2,1)}, u32[]{:S(2)}, u32[]{:S(2)}) %collective-permute-start.27) | collective-permute-done | bytes 786464 | tf_op jit(solution)/shard_map/ppermute | solution.py:364
  360.4 2.8 back.7
  368.6 6.5 %collective-permute-done.31 = bf16[2,1,384,256]{3,2,1,0:T(8,128)(2,1)S(1)} collective-permute-done((bf16[2,1,384,256]{3,2,1,0:T(8,128)(2,1)S(1)}, bf16[2,1,384,256]{3,2,1,0:T(8,128)(2,1)S(1)}, u32[]{:S(2)}, u32[]{:S(2)}) %collective-permute-start.31) | collective-permute-done | bytes 393248 | tf_op jit(solution)/shard_map/ppermute | solution.py:364
  (208 shorter events, 91.1 us)
Async XLA Ops:
  6.5 193.4 %all-gather.2.cloned.1.call-start = ((), (), s32[]{:S(2)}) async-start(), calls=%async_computation | async-start | bytes 21233664 | tf_op jit(solution)/shard_map/all_gather | solution.py:382
  8.2 86.0 %collective-permute-start.5 = (bf16[384,3072]{1,0:T(8,128)(2,1)S(1)}, bf16[384,3072]{1,0:T(8,128)(2,1)}, u32[]{:S(2)}, u32[]{:S(2)}) collective-permute-start(bf16[384,3072]{1,0:T(8,128)(2,1)S(1)} %copy-done.16), channel_id=1, source_target_pairs={{0,8},{4,12},{8,0},{12,4},{16,24},{20,28},{24,16},{28,20},{1,9},{5... | collective-permute-start | bytes 7077896 | tf_op jit(solution)/shard_map/ppermute | solution.py:364
  11.1 38.4 %collective-permute-start = (bf16[1024,768]{1,0:T(8,128)(2,1)}, bf16[1024,768]{1,0:T(8,128)(2,1)S(1)}, u32[]{:S(2)}, u32[]{:S(2)}) collective-permute-start(bf16[1024,768]{1,0:T(8,128)(2,1)} %refs_0_.5), channel_id=1, source_target_pairs={{0,1},{1,3},{3,2},{2,0},{4,5},{5,7},{7,6},{6,4},{8,9},{9,11},{11,1... | collective-permute-start | bytes 4718600 | tf_op jit(solution)/shard_map/ppermute | solution.py:318
  12.7 69.1 %collective-permute-start.1 = (bf16[1024,768]{1,0:T(8,128)(2,1)}, bf16[1024,768]{1,0:T(8,128)(2,1)S(1)}, u32[]{:S(2)}, u32[]{:S(2)}) collective-permute-start(bf16[1024,768]{1,0:T(8,128)(2,1)} %refs_10_.1), channel_id=1, source_target_pairs={{0,1},{1,3},{3,2},{2,0},{4,5},{5,7},{7,6},{6,4},{8,9},{9,11},{11,1... | collective-permute-start | bytes 4718600 | tf_op jit(solution)/shard_map/ppermute | solution.py:318
  15.3 91.5 %collective-permute-start.7 = (bf16[384,3072]{1,0:T(8,128)(2,1)S(1)}, bf16[384,3072]{1,0:T(8,128)(2,1)}, u32[]{:S(2)}, u32[]{:S(2)}) collective-permute-start(bf16[384,3072]{1,0:T(8,128)(2,1)S(1)} %copy-done.16), channel_id=1, source_target_pairs={{0,16},{4,20},{8,24},{12,28},{16,0},{20,4},{24,8},{28,12},{1,17},{... | collective-permute-start | bytes 7077896 | tf_op jit(solution)/shard_map/ppermute | solution.py:364
  81.8 74.6 %collective-permute-start.3 = (bf16[1024,768]{1,0:T(8,128)(2,1)S(1)}, bf16[1024,768]{1,0:T(8,128)(2,1)}, u32[]{:S(2)}, u32[]{:S(2)}) collective-permute-start(bf16[1024,768]{1,0:T(8,128)(2,1)S(1)} %collective-permute-done.1.refs_1_.refs_11_), channel_id=1, source_target_pairs={{0,1},{1,3},{3,2},{2,0},{4,5},{5,7},{7,6},{6,4},{8,9},{9,11},{11,1... | collective-permute-start | bytes 4718600 | tf_op jit(solution)/shard_map/ppermute | solution.py:318
  82.7 74.2 %collective-permute-start.2 = (bf16[1024,768]{1,0:T(8,128)(2,1)S(1)}, bf16[1024,768]{1,0:T(8,128)(2,1)}, u32[]{:S(2)}, u32[]{:S(2)}) collective-permute-start(bf16[1024,768]{1,0:T(8,128)(2,1)S(1)} %collective-permute-done.refs_1_), channel_id=1, source_target_pairs={{0,1},{1,3},{3,2},{2,0},{4,5},{5,7},{7,6},{6,4},{8,9},{9,11},{11,1... | collective-permute-start | bytes 4718600 | tf_op jit(solution)/shard_map/ppermute | solution.py:318
  86.0 71.0 %collective-permute-start.4 = (bf16[384,3072]{1,0:T(8,128)(2,1)S(1)}, bf16[384,3072]{1,0:T(8,128)(2,1)S(1)}, u32[]{:S(2)}, u32[]{:S(2)}) collective-permute-start(bf16[384,3072]{1,0:T(8,128)(2,1)S(1)} %copy-done.16), channel_id=1, source_target_pairs={{0,4},{4,0},{8,12},{12,8},{16,20},{20,16},{24,28},{28,24},{1,5},{5... | collective-permute-start | bytes 7077896 | tf_op jit(solution)/shard_map/ppermute | solution.py:322
  95.5 59.8 %collective-permute-start.9 = (bf16[192,3072]{1,0:T(8,128)(2,1)S(1)}, bf16[192,3072]{1,0:T(8,128)(2,1)S(1)}, u32[]{:S(2)}, u32[]{:S(2)}) collective-permute-start(bf16[192,3072]{1,0:T(8,128)(2,1)S(1)} %slice.56), channel_id=1, source_target_pairs={{0,16},{4,20},{8,24},{12,28},{16,0},{20,4},{24,8},{28,12},{1,17},{... | collective-permute-start | bytes 3538952 | tf_op jit(solution)/shard_map/ppermute | solution.py:364
  108.2 51.2 %collective-permute-start.11 = (bf16[192,3072]{1,0:T(8,128)(2,1)S(1)}, bf16[192,3072]{1,0:T(8,128)(2,1)}, u32[]{:S(2)}, u32[]{:S(2)}) collective-permute-start(bf16[192,3072]{1,0:T(8,128)(2,1)S(1)} %slice.57), channel_id=1, source_target_pairs={{0,8},{4,12},{8,0},{12,4},{16,24},{20,28},{24,16},{28,20},{1,9},{5... | collective-permute-start | bytes 3538952 | tf_op jit(solution)/shard_map/ppermute | solution.py:364
  156.4 16.2 %collective-permute-start.6 = (bf16[384,3072]{1,0:T(8,128)(2,1)}, bf16[384,3072]{1,0:T(8,128)(2,1)}, u32[]{:S(2)}, u32[]{:S(2)}) collective-permute-start(bf16[384,3072]{1,0:T(8,128)(2,1)} %collective-permute-done.5.refs_2_), channel_id=1, source_target_pairs={{0,4},{4,0},{8,12},{12,8},{16,20},{20,16},{24,28},{28,24},{1,5},{5... | collective-permute-start | bytes 7077896 | tf_op jit(solution)/shard_map/ppermute | solution.py:322
  156.9 15.7 %collective-permute-start.8 = (bf16[384,3072]{1,0:T(8,128)(2,1)}, bf16[384,3072]{1,0:T(8,128)(2,1)}, u32[]{:S(2)}, u32[]{:S(2)}) collective-permute-start(bf16[384,3072]{1,0:T(8,128)(2,1)} %collective-permute-done.7.refs_4_), channel_id=1, source_target_pairs={{0,4},{4,0},{8,12},{12,8},{16,20},{20,16},{24,28},{28,24},{1,5},{5... | collective-permute-start | bytes 7077896 | tf_op jit(solution)/shard_map/ppermute | solution.py:322
  158.4 41.6 %collective-permute-start.13 = (bf16[1024,768]{1,0:T(8,128)(2,1)}, bf16[1024,768]{1,0:T(8,128)(2,1)}, u32[]{:S(2)}, u32[]{:S(2)}) collective-permute-start(bf16[1024,768]{1,0:T(8,128)(2,1)} %collective-permute-done.2.refs_2_), channel_id=1, source_target_pairs={{0,1},{1,3},{3,2},{2,0},{4,5},{5,7},{7,6},{6,4},{8,9},{9,11},{11,1... | collective-permute-start | bytes 4718600 | tf_op jit(solution)/shard_map/ppermute | solution.py:318
  159.4 75.9 %collective-permute-start.14 = (bf16[1024,768]{1,0:T(8,128)(2,1)}, bf16[1024,768]{1,0:T(8,128)(2,1)}, u32[]{:S(2)}, u32[]{:S(2)}) collective-permute-start(bf16[1024,768]{1,0:T(8,128)(2,1)} %collective-permute-done.3.refs_2_.refs_12_), channel_id=1, source_target_pairs={{0,1},{1,3},{3,2},{2,0},{4,5},{5,7},{7,6},{6,4},{8,9},{9,11},{11,1... | collective-permute-start | bytes 4718600 | tf_op jit(solution)/shard_map/ppermute | solution.py:318
  253.8 12.9 %collective-permute-start.15 = (bf16[1536,512]{1,0:T(8,128)(2,1)S(1)}, bf16[1536,512]{1,0:T(8,128)(2,1)S(1)}, u32[]{:S(2)}, u32[]{:S(2)}) collective-permute-start(bf16[1536,512]{1,0:T(8,128)(2,1)S(1)} %get-tuple-element.105), channel_id=1, source_target_pairs={{0,4},{4,0},{8,12},{12,8},{16,20},{20,16},{24,28},{28,24},{1,5},{5... | collective-permute-start | bytes 4718600 | tf_op jit(solution)/shard_map/ppermute | solution.py:322
  266.6 26.4 %collective-permute-start.18 = (bf16[1536,1024]{1,0:T(8,128)(2,1)}, bf16[1536,1024]{1,0:T(8,128)(2,1)}, u32[]{:S(2)}, u32[]{:S(2)}) collective-permute-start(bf16[1536,1024]{1,0:T(8,128)(2,1)} %get-tuple-element.120), channel_id=1, source_target_pairs={{0,4},{4,0},{8,12},{12,8},{16,20},{20,16},{24,28},{28,24},{1,5},{5... | collective-permute-start | bytes 9437192 | tf_op jit(solution)/shard_map/ppermute | solution.py:322
  270.5 16.6 %collective-permute-start.16 = (bf16[2,1,384,256]{3,2,1,0:T(8,128)(2,1)S(1)}, bf16[2,1,384,256]{3,2,1,0:T(8,128)(2,1)S(1)}, u32[]{:S(2)}, u32[]{:S(2)}) collective-permute-start(bf16[2,1,384,256]{3,2,1,0:T(8,128)(2,1)S(1)} %get-tuple-element.111), channel_id=1, source_target_pairs={{0,8},{4,12},{8,0},{12,4},{16,24},{20,28},{24,16},{28,20},{1,9},{5... | collective-permute-start | bytes 1179656 | tf_op jit(solution)/shard_map/ppermute | solution.py:364
  270.5 16.6 %collective-permute-start.17 = (bf16[1,2,384,256]{3,2,1,0:T(8,128)(2,1)S(1)}, bf16[1,2,384,256]{3,2,1,0:T(8,128)(2,1)S(1)}, u32[]{:S(2)}, u32[]{:S(2)}) collective-permute-start(bf16[1,2,384,256]{3,2,1,0:T(8,128)(2,1)S(1)} %get-tuple-element.112), channel_id=1, source_target_pairs={{0,16},{4,20},{8,24},{12,28},{16,0},{20,4},{24,8},{28,12},{1,17},{... | collective-permute-start | bytes 1179656 | tf_op jit(solution)/shard_map/ppermute | solution.py:364
  287.8 38.5 %collective-permute-start.23 = (bf16[1536,1024]{1,0:T(8,128)(2,1)}, bf16[1536,1024]{1,0:T(8,128)(2,1)}, u32[]{:S(2)}, u32[]{:S(2)}) collective-permute-start(bf16[1536,1024]{1,0:T(8,128)(2,1)} %get-tuple-element.139), channel_id=1, source_target_pairs={{0,4},{4,0},{8,12},{12,8},{16,20},{20,16},{24,28},{28,24},{1,5},{5... | collective-permute-start | bytes 9437192 | tf_op jit(solution)/shard_map/ppermute | solution.py:322
  301.8 19.5 %collective-permute-start.21 = (bf16[2,1,384,512]{3,2,1,0:T(8,128)(2,1)S(1)}, bf16[2,1,384,512]{3,2,1,0:T(8,128)(2,1)S(1)}, u32[]{:S(2)}, u32[]{:S(2)}) collective-permute-start(bf16[2,1,384,512]{3,2,1,0:T(8,128)(2,1)S(1)} %get-tuple-element.130), channel_id=1, source_target_pairs={{0,8},{4,12},{8,0},{12,4},{16,24},{20,28},{24,16},{28,20},{1,9},{5... | collective-permute-start | bytes 2359304 | tf_op jit(solution)/shard_map/ppermute | solution.py:364
  302.7 19.7 %collective-permute-start.22 = (bf16[1,2,384,512]{3,2,1,0:T(8,128)(2,1)S(1)}, bf16[1,2,384,512]{3,2,1,0:T(8,128)(2,1)S(1)}, u32[]{:S(2)}, u32[]{:S(2)}) collective-permute-start(bf16[1,2,384,512]{3,2,1,0:T(8,128)(2,1)S(1)} %get-tuple-element.131), channel_id=1, source_target_pairs={{0,16},{4,20},{8,24},{12,28},{16,0},{20,4},{24,8},{28,12},{1,17},{... | collective-permute-start | bytes 2359304 | tf_op jit(solution)/shard_map/ppermute | solution.py:364
  336.7 18.0 %collective-permute-start.27 = (bf16[1,2,384,512]{3,2,1,0:T(8,128)(2,1)}, bf16[1,2,384,512]{3,2,1,0:T(8,128)(2,1)}, u32[]{:S(2)}, u32[]{:S(2)}) collective-permute-start(bf16[1,2,384,512]{3,2,1,0:T(8,128)(2,1)} %get-tuple-element.149), channel_id=1, source_target_pairs={{0,16},{4,20},{8,24},{12,28},{16,0},{20,4},{24,8},{28,12},{1,17},{... | collective-permute-start | bytes 2359304 | tf_op jit(solution)/shard_map/ppermute | solution.py:364
  337.0 19.2 %collective-permute-start.26 = (bf16[2,1,384,512]{3,2,1,0:T(8,128)(2,1)}, bf16[2,1,384,512]{3,2,1,0:T(8,128)(2,1)S(1)}, u32[]{:S(2)}, u32[]{:S(2)}) collective-permute-start(bf16[2,1,384,512]{3,2,1,0:T(8,128)(2,1)} %copy-done.46), channel_id=1, source_target_pairs={{0,8},{4,12},{8,0},{12,4},{16,24},{20,28},{24,16},{28,20},{1,9},{5... | collective-permute-start | bytes 2359304 | tf_op jit(solution)/shard_map/ppermute | solution.py:364
  339.5 20.8 %collective-permute-start.28 = (bf16[1536,512]{1,0:T(8,128)(2,1)}, bf16[1536,512]{1,0:T(8,128)(2,1)S(1)}, u32[]{:S(2)}, u32[]{:S(2)}) collective-permute-start(bf16[1536,512]{1,0:T(8,128)(2,1)} %copy-done.45), channel_id=1, source_target_pairs={{0,4},{4,0},{8,12},{12,8},{16,20},{20,16},{24,28},{28,24},{1,5},{5... | collective-permute-start | bytes 4718600 | tf_op jit(solution)/shard_map/ppermute | solution.py:322
  (70 other events, 679.4 us)
Sparse Core Ops, SparseCore 0:
  9.2 162.0 all-gather.1

commit v5 on v4

--- a/solution.py
+++ b/solution.py
@@ -69,7 +69,7 @@
         ),
         out_shape=[shape, shape],
         input_output_aliases={2 + count: 0, 3 + count: 1} if before else {},
-        compiler_params=params(16),
+        compiler_params=params(52),
         cost_estimate=light,
         name="split_cores",
     )(core.reshape(1), at, *pieces, *before)
@@ -113,12 +113,11 @@
         out[rows, :] = total * (jnp.exp(-0.5 * square) * inv_root * (2.0 - square))
 
 
-def bent_of(shards, at, row_scale, codes, down_full):
+def bent_of(shards, at, scale, codes, down_full, tile):
     count, parts = len(shards), len(shards[0])
     tall, width = shards[0][0].shape
     tok = tall * parts
     wide, feats = down_full.shape
-    tile = math.gcd(wide, 512)
     return pl.pallas_call(
         functools.partial(bent_body, count, parts, width),
         grid_spec=pltpu.PrefetchScalarGridSpec(
@@ -130,13 +129,13 @@
                 pl.BlockSpec((tile, feats), lambda j, at: (j, 0)),
             ]
             + [whole((tall, width))] * (count * parts),
-            out_specs=pl.BlockSpec((tok, tile), lambda j, at: (0, j)),
+            out_specs=pl.BlockSpec((None, tok, tile), lambda j, at: (j, 0, 0)),
         ),
-        out_shape=jax.ShapeDtypeStruct((tok, wide), f32),
-        compiler_params=params(32),
+        out_shape=jax.ShapeDtypeStruct((wide // tile, tok, tile), f32),
+        compiler_params=params(52),
         cost_estimate=light,
         name="bent",
-    )(at, row_scale[:, None], codes, down_full, *[p for piece in shards for p in piece])
+    )(at, scale, codes, down_full, *[p for piece in shards for p in piece])
 
 
 def partial_body(count, parts, width, spots, plan, arrays, tile, at, slots, *refs):
@@ -145,17 +144,23 @@
     out, last, held, sems = refs[count * parts :]
     step = pl.program_id(0)
 
+    def copies(t):
+        cols = pl.ds(t * tile if isinstance(t, int) else pl.multiple_of(t * tile, tile), tile)
+        made = []
+        for i, (which, first, size) in enumerate(plan):
+            into = held.at[pl.ds(pl.multiple_of(slots[i] * spots, spots), size), cols]
+            source = pieces[which].at[pl.ds(first, size), cols]
+            made.append(pltpu.make_async_copy(source, into, sems.at[t, i]))
+        return made
+
     @pl.when(step == 0)
     def _():
-        copies = []
-        for i, (which, first, size) in enumerate(plan):
-            into = held.at[pl.ds(pl.multiple_of(slots[i] * spots, spots), size)]
-            source = pieces[which].at[pl.ds(first, size)]
-            copies.append(pltpu.make_async_copy(source, into, sems.at[i]))
-        for c in copies:
-            c.start()
-        for c in copies:
-            c.wait()
+        for t in range(held.shape[1] // tile):
+            for c in copies(t):
+                c.start()
+
+    for c in copies(step):
+        c.wait()
 
     cols = pl.ds(pl.multiple_of(step * tile, tile), tile)
     for h in range(parts):
@@ -171,12 +176,11 @@
     last[...] = held[pl.ds(pl.multiple_of(at[count] * width, width), width), cols]
 
 
-def partial_tangent(shards, at, pieces, slots, spots, feats):
+def partial_tangent(shards, at, pieces, slots, spots, feats, tile):
     count, parts = len(shards), len(shards[0])
     tall, width = shards[0][0].shape
     tok = tall * parts
     hidden = pieces[0][0].shape[1]
-    tile = 512
     arrays, plan = [], []
     for piece, first, size in pieces:
         which = [i for i, a in enumerate(arrays) if a is piece]
@@ -193,19 +197,19 @@
             in_specs=[pl.BlockSpec(memory_space=pl.ANY)] * len(arrays)
             + [whole((tall, width))] * (count * parts),
             out_specs=[
-                pl.BlockSpec((tok, tile), lambda j, *_: (0, j)),
-                pl.BlockSpec((width, tile), lambda j, *_: (0, j)),
+                pl.BlockSpec((None, tok, tile), lambda j, *_: (j, 0, 0)),
+                pl.BlockSpec((None, width, tile), lambda j, *_: (j, 0, 0)),
             ],
             scratch_shapes=[
                 pltpu.VMEM((feats, hidden), bf16),
-                pltpu.SemaphoreType.DMA((len(pieces),)),
+                pltpu.SemaphoreType.DMA((hidden // tile, len(pieces))),
             ],
         ),
         out_shape=[
-            jax.ShapeDtypeStruct((tok, hidden), f32),
-            jax.ShapeDtypeStruct((width, hidden), bf16),
+            jax.ShapeDtypeStruct((hidden // tile, tok, tile), f32),
+            jax.ShapeDtypeStruct((hidden // tile, width, tile), bf16),
         ],
-        compiler_params=params(36),
+        compiler_params=params(52),
         cost_estimate=light,
         name="partial_tangent",
     )(at, slots, *arrays, *[p for piece in shards for p in piece])
@@ -220,16 +224,16 @@
 def front_of(shard, last, begun, bent, other, first, wide):
     tok, width = shard.shape
     half = other.shape[0]
-    tile = math.gcd(wide, math.gcd(first, 256))
+    tile = begun.shape[2]
     base = first // tile
     return pl.pallas_call(
         front_body,
         grid=(wide // tile,),
         in_specs=[
             whole((tok, width)),
-            pl.BlockSpec((width, tile), lambda j: (0, base + j)),
-            pl.BlockSpec((tok, tile), lambda j: (0, base + j)),
-            pl.BlockSpec((tok, tile), lambda j: (0, base + j)),
+            pl.BlockSpec((None, width, tile), lambda j: (base + j, 0, 0)),
+            pl.BlockSpec((None, tok, tile), lambda j: (base + j, 0, 0)),
+            pl.BlockSpec((None, tok, tile), lambda j: (base + j, 0, 0)),
             whole(other.shape),
         ],
         out_specs=[
@@ -240,7 +244,7 @@
             jax.ShapeDtypeStruct((tok, wide), bf16),
             jax.ShapeDtypeStruct((half, wide), bf16),
         ],
-        compiler_params=params(20),
+        compiler_params=params(52),
         cost_estimate=light,
         name="front",
     )(shard, last, begun, bent, other)
@@ -272,7 +276,7 @@
 def back_of(mine, mixed, came, x, y, xs, ys, rows):
     tok, wide = mixed.shape
     side = wide // 2
-    tile = math.gcd(side, 256)
+    tile = math.gcd(side, 512)
     steps = side // tile
 
     def left(j, me):
@@ -301,7 +305,7 @@
         out_shape=[
             jax.ShapeDtypeStruct(shape + (side,), kind) for shape, kind in zip(shapes, kinds)
         ],
-        compiler_params=params(18),
+        compiler_params=params(52),
         cost_estimate=light,
         name="back",
     )(jnp.stack([x, y]), mine, mixed, came)
@@ -358,7 +362,15 @@
     )
 
     edges = [hidden * sum(sixths[:j]) // sum(sixths) for j in range(len(sixths) + 1)]
+    unit = hidden // sum(sixths)
     x_way, y_way = (xs, cores), (ys, cores * xs)
+    spots = [(0, 0, 0)] + [(0, i, 0) for i in range(1, xs)] + [(0, 0, k) for k in range(1, ys)]
+    spots += [(half, i, k) for i in range(1, xs) for k in range(1, ys) for half in range(2)]
+    slots = []
+    for half, i, k in spots:
+        chip = (lax.rem(y + ys - k, ys) * xs + lax.rem(x + xs - i, xs)) * cores
+        slots += [(chip + whose) * 2 + half for whose in (core, 1 - core)]
+    slots = jnp.stack(slots)
 
     def over(block, way, by):
         return lax.ppermute(block, "dp", shift(way[0], way[1], dp, by))
@@ -376,34 +388,27 @@
                     far.append(over(across[i - 1][: rows // 2], y_way, k))
                     far.append(over(above[k - 1][rows // 2 :], x_way, i))
             near = [(p, swapped(p, dp, cores)) for p in (probe, *across, *above)]
-        if s < tp - 1:
+        if s == 1:
             cot[s], tok[s] = lax.optimization_barrier((cot[s], tok[s]))
+        if s == 2:
+            near_too = [pair[1] for pair in near]
+            cot[s], tok[s], near_too, at, scale, slots = lax.optimization_barrier(
+                (cot[s], tok[s], near_too, at, row_scale[:, None], slots)
+            )
+            near = [(pair[0], other) for pair, other in zip(near, near_too)]
     far = [(p, swapped(p, dp, cores)) for p in far]
     down_full = lax.all_gather(down_weight, "dp", axis=0, tiled=True)
 
-    pieces, slots = [], []
-
-    def hold(pair, half, i, k):
-        chip = (lax.rem(y + ys - k, ys) * xs + lax.rem(x + xs - i, xs)) * cores
-        for piece, whose in zip(pair, (core, 1 - core)):
-            pieces.append((piece, 0, piece.shape[0]))
-            slots.append((chip + whose) * 2 + half)
-
-    spots = [(0, 0)] + [(i, 0) for i in range(1, xs)] + [(0, k) for k in range(1, ys)]
-    for pair, (i, k) in zip(near, spots):
-        hold(pair, 0, i, k)
-    spots = [(half, i, k) for i in range(1, xs) for k in range(1, ys) for half in range(2)]
-    for pair, spot in zip(far, spots):
-        hold(pair, *spot)
+    pieces = [(p, 0, p.shape[0]) for pair in near + far for p in pair]
     begun, last = partial_tangent(
-        [[t] for t in tok[:-1]], at, pieces, jnp.stack(slots), rows // 2, rows * dp
+        [[t] for t in tok[:-1]], at, pieces, slots, rows // 2, rows * dp, unit
     )
     begun, cot[-1] = after(begun, cot[-1])
     plain = rows % 128 != 0
     if not plain:
         early = list(split_cores(tok[:-1], at[:-1], core, tp))
         early[0], cot[-1] = after(early[0], cot[-1])
-    bent = bent_of([[c] for c in cot], at, row_scale, codes, down_full)
+    bent = bent_of([[c] for c in cot], at, scale, codes, down_full, unit)
     bent, tok[-1] = lax.optimization_barrier((bent, tok[-1]))
     if plain:
         mine, other = split_plain(tok, at, core)

time: 392 us -> 364 us (0.929)
  local copies, waits for them, and re-layouts: 51 us -> 16 us
  Pallas kernels: 116 us -> 124 us
    ppermute x6, waiting for transfers between devices: 65 us -> 113 us  [ring_step(): return lax.ppermute(block, 'tensor', pairs)]
    ppermute x12, waiting for transfers between devices: 91.8 us -> 45.9 us  [over(): return lax.ppermute(block, 'dp', shift(way[0], way[1], dp, by))]
    unnamed x116 -> x52, local copies, waits for them, and re-layouts: 46.3 us -> 8.46 us
    pallas_call x4, Pallas kernels: 19 us -> 28.9 us  [back_of(): pl.pallas_call(functools.partial(back_body, xs, ys, rows, steps), grid_sp...]
    ppermute x8, waiting for transfers between devices: 7.72 us -> 3.44 us  [sent(): lax.ppermute(send, 'dp', shift(n, stride, total, by + 1))]
  transfers between devices with their start and end apart: 36 -> 36, of which waited for: 14 -> 12; matrix products, arithmetic and copies ran while one was open for 4% -> 4% of each run, Pallas kernels for 27% -> 32%
where the time goes in v5:
time: 364 us; the launch traced here: 363 us
  waiting for transfers between devices  163 us (45%)
  Pallas kernels  124 us (34%)
  starting transfers between devices  37.1 us (10%)
  local copies, waits for them, and re-layouts  16 us (4%)
  between operations  13.8 us (4%)
  other arithmetic  9.02 us (2%)
    ppermute x6, waiting for transfers between devices, ring_step(): return lax.ppermute(block, 'tensor', pairs)  113 us
    ppermute x12, waiting for transfers between devices, over(): return lax.ppermute(block, 'dp', shift(way[0], way[1], dp, by))  45.9 us
    pallas_call x4, Pallas kernels, front_of(): pl.pallas_call(front_body, grid=(wide // tile,), in_specs=[whole((tok, wi...  36.3 us
    pallas_call x1, Pallas kernels, bent_of(): pl.pallas_call(functools.partial(bent_body, count, parts, width), grid_sp...  29.2 us
    pallas_call x4, Pallas kernels, back_of(): pl.pallas_call(functools.partial(back_body, xs, ys, rows, steps), grid_sp...  28.9 us
    pallas_call x1, Pallas kernels, partial_tangent(): pl.pallas_call(functools.partial(partial_body, count, parts, width, spots...  23 us
    ppermute x12, starting transfers between devices, over(): return lax.ppermute(block, 'dp', shift(way[0], way[1], dp, by))  18.3 us
    ppermute x6, starting transfers between devices, ring_step(): return lax.ppermute(block, 'tensor', pairs)  10.6 us
  transfers between devices with their start and end apart: 36, of which 12 were waited for; matrix products, arithmetic and copies ran while one was open for 4% of the time, Pallas kernels for 32%

profile of v5, /device:TPU:0, one launch (start us, length us, event | category | flops | bytes accessed | tf_op | source)
XLA Modules:
  0.0 363.5 jit_solution(5609110538652710976)
XLA Ops:
  7.3 3.0 collective-permute-start.5
  16.0 34.3 %collective-permute-done.refs_1_ = bf16[1024,768]{1,0:T(8,128)(2,1)S(1)} collective-permute-done((bf16[1024,768]{1,0:T(8,128)(2,1)}, bf16[1024,768]{1,0:T(8,128)(2,1)S(1)}, u32[]{:S(2)}, u32[]{:S(2)}) %collective-permute-start) | collective-permute-done | bytes 1572896 | tf_op jit(solution)/shard_map/ppermute | solution.py:322
  50.2 31.9 %collective-permute-done.1.refs_1_.refs_11_ = bf16[1024,768]{1,0:T(8,128)(2,1)S(1)} collective-permute-done((bf16[1024,768]{1,0:T(8,128)(2,1)S(1)}, bf16[1024,768]{1,0:T(8,128)(2,1)S(1)}, u32[]{:S(2)}, u32[]{:S(2)}) %collective-permute-start.1) | collective-permute-done | bytes 1572896 | tf_op jit(solution)/shard_map/ppermute | solution.py:322
  84.1 8.8 %collective-permute-done.5.refs_2_ = bf16[384,3072]{1,0:T(8,128)(2,1)} collective-permute-done((bf16[384,3072]{1,0:T(8,128)(2,1)}, bf16[384,3072]{1,0:T(8,128)(2,1)}, u32[]{:S(2)}, u32[]{:S(2)}) %collective-permute-start.5) | collective-permute-done | bytes 2359328 | tf_op jit(solution)/shard_map/ppermute | solution.py:376
  93.0 2.8 collective-permute-done.7.refs_4_
  104.5 17.2 %collective-permute-done.3.refs_2_.refs_12_ = bf16[1024,768]{1,0:T(8,128)(2,1)} collective-permute-done((bf16[1024,768]{1,0:T(8,128)(2,1)S(1)}, bf16[1024,768]{1,0:T(8,128)(2,1)}, u32[]{:S(2)}, u32[]{:S(2)}) %collective-permute-start.3) | collective-permute-done | bytes 1572896 | tf_op jit(solution)/shard_map/ppermute | solution.py:322
  123.0 29.7 %collective-permute-done.2.refs_2_ = bf16[1024,768]{1,0:T(8,128)(2,1)} collective-permute-done((bf16[1024,768]{1,0:T(8,128)(2,1)S(1)}, bf16[1024,768]{1,0:T(8,128)(2,1)}, u32[]{:S(2)}, u32[]{:S(2)}) %collective-permute-start.2) | collective-permute-done | bytes 1572896 | tf_op jit(solution)/shard_map/ppermute | solution.py:322
  153.5 3.5 collective-permute-start.14
  156.9 6.0 %collective-permute-done.11.refs_8_ = bf16[192,3072]{1,0:T(8,128)(2,1)} collective-permute-done((bf16[192,3072]{1,0:T(8,128)(2,1)}, bf16[192,3072]{1,0:T(8,128)(2,1)}, u32[]{:S(2)}, u32[]{:S(2)}) %collective-permute-start.11) | collective-permute-done | bytes 1179680 | tf_op jit(solution)/shard_map/ppermute | solution.py:376
  164.6 4.9 %split_cores.2 = (bf16[1536,1024]{1,0:T(8,128)(2,1)}, bf16[1536,1024]{1,0:T(8,128)(2,1)}) custom-call(s32[1]{0:T(128)} %bitcast.2.core, s32[3]{0:T(128)S(1)} %bitcast.65, bf16[1024,768]{1,0:T(8,128)(2,1)S(1)} %copy-done.2, bf16[1024,768]{1,0:T(8,128)(2,1)} %copy-done.7, bf16[1024,768]{1,0:T(8,128)(2,1)} %collective-permute-done.3.refs_2_.refs_12_), custom_call_target="tpu_custom_call" | custom-call | bytes 1024 | tf_op jit(solution)/shard_map/split_cores/pallas_call | solution.py:57
  169.5 23.0 %partial_tangent.1 = (f32[6,1024,512]{2,1,0:T(8,128)}, bf16[6,768,512]{2,1,0:T(8,128)(2,1)}) custom-call(s32[4]{0:T(128)S(1)} %fusion.16.at, s32[10]{0:T(128)S(1)} %stack.64.slots, bf16[384,3072]{1,0:T(8,128)(2,1)} %refs_0_.4, bf16[384,3072]{1,0:T(8,128)(2,1)} %copy-done.13, bf16[384,3072]{1,0:T(8,128)(2,1)} %collective-permute-done.5.refs_2_, ...), custom_call_target="tpu_custom_call" | custom-call | bytes 1024 | tf_op jit(solution)/shard_map/partial_tangent/pallas_call | solution.py:190
  192.6 29.2 %bent.1 = f32[6,1024,512]{2,1,0:T(8,128)} custom-call(s32[4]{0:T(128)S(1)} %fusion.16.at, f32[1024,1]{1,0:T(8,128)S(1)} %copy-done.3, s32[1024,3072]{1,0:T(8,128)} %codes.1, bf16[3072,3072]{1,0:T(8,128)(2,1)} %all-gather.2.cloned.1.call-done.down, bf16[1024,768]{1,0:T(8,128)(2,1)} %refs_0_.5, bf16[1024,768]{1,0:T(8,128)(2,1)} %copy-done.14, ...), custom_call_target="tpu_custom_call" | custom-call | bytes 1024 | tf_op jit(solution)/shard_map/bent/pallas_call | solution.py:121
  223.8 7.7 %front.4 = (bf16[1024,512]{1,0:T(8,128)(2,1)S(1)}, bf16[1536,512]{1,0:T(8,128)(2,1)}) custom-call(bf16[1024,768]{1,0:T(8,128)(2,1)} %copy-done, bf16[6,768,512]{2,1,0:T(8,128)(2,1)} %get-tuple-element.144.probe, f32[6,1024,512]{2,1,0:T(8,128)} %get-tuple-element.109.begun, f32[6,1024,512]{2,1,0:T(8,128)} %bent.1, bf16[1536,1024]{1,0:T(8,128)(2,1)} %get-tuple-element.111.other), custom_call_target="tpu_custom_call" | custom-call | bytes 1024 | tf_op jit(solution)/shard_map/front/pallas_call | solution.py:229
  232.0 10.5 %front.5 = (bf16[1024,1024]{1,0:T(8,128)(2,1)}, bf16[1536,1024]{1,0:T(8,128)(2,1)}) custom-call(bf16[1024,768]{1,0:T(8,128)(2,1)S(1)} %copy-done.1, bf16[6,768,512]{2,1,0:T(8,128)(2,1)} %get-tuple-element.144.probe, f32[6,1024,512]{2,1,0:T(8,128)} %get-tuple-element.109.begun, f32[6,1024,512]{2,1,0:T(8,128)} %bent.1, bf16[1536,1024]{1,0:T(8,128)(2,1)} %get-tuple-element.111.other), custom_call_target="tpu_custom_call" | custom-call | bytes 1024 | tf_op jit(solution)/shard_map/front/pallas_call | solution.py:229
  243.7 5.9 %back.4 = (f32[2,1,384,256]{3,2,1,0:T(8,128)S(1)}, f32[1,2,384,256]{3,2,1,0:T(8,128)}, bf16[2,1,384,256]{3,2,1,0:T(8,128)(2,1)S(1)}, bf16[1,2,384,256]{3,2,1,0:T(8,128)(2,1)S(1)}) custom-call(s32[2]{0:T(128)S(1)} %pad_add_fusion.me, bf16[1536,1024]{1,0:T(8,128)(2,1)} %get-tuple-element.107.mine, bf16[1024,512]{1,0:T(8,128)(2,1)} %copy-done.5, ...), custom_call_target="tpu_custom_call" | custom-call | bytes 1024 | tf_op jit(solution)/shard_map/back/pallas_call | solution.py:290
  252.8 10.5 %front.6 = (bf16[1024,1024]{1,0:T(8,128)(2,1)}, bf16[1536,1024]{1,0:T(8,128)(2,1)}) custom-call(bf16[1024,768]{1,0:T(8,128)(2,1)S(1)} %copy-done.1, bf16[6,768,512]{2,1,0:T(8,128)(2,1)} %get-tuple-element.144.probe, f32[6,1024,512]{2,1,0:T(8,128)} %get-tuple-element.109.begun, f32[6,1024,512]{2,1,0:T(8,128)} %bent.1, bf16[1536,1024]{1,0:T(8,128)(2,1)} %get-tuple-element.111.other), custom_call_target="tpu_custom_call" | custom-call | bytes 1024 | tf_op jit(solution)/shard_map/front/pallas_call | solution.py:229
  265.4 8.7 %back.5 = (f32[2,1,384,512]{3,2,1,0:T(8,128)}, f32[1,2,384,512]{3,2,1,0:T(8,128)}, bf16[2,1,384,512]{3,2,1,0:T(8,128)(2,1)S(1)}, bf16[1,2,384,512]{3,2,1,0:T(8,128)(2,1)S(1)}) custom-call(s32[2]{0:T(128)S(1)} %pad_add_fusion.me, bf16[1536,1024]{1,0:T(8,128)(2,1)} %get-tuple-element.107.mine, bf16[1024,1024]{1,0:T(8,128)(2,1)} %get-tuple-element.131.mixed, ...), custom_call_target="tpu_custom_call" | custom-call | bytes 1024 | tf_op jit(solution)/shard_map/back/pallas_call | solution.py:290
  278.0 7.7 %front.7 = (bf16[1024,512]{1,0:T(8,128)(2,1)S(1)}, bf16[1536,512]{1,0:T(8,128)(2,1)}) custom-call(bf16[1024,768]{1,0:T(8,128)(2,1)} %copy-done, bf16[6,768,512]{2,1,0:T(8,128)(2,1)} %get-tuple-element.144.probe, f32[6,1024,512]{2,1,0:T(8,128)} %get-tuple-element.109.begun, f32[6,1024,512]{2,1,0:T(8,128)} %bent.1, bf16[1536,1024]{1,0:T(8,128)(2,1)} %get-tuple-element.111.other), custom_call_target="tpu_custom_call" | custom-call | bytes 1024 | tf_op jit(solution)/shard_map/front/pallas_call | solution.py:229
  285.7 7.9 %collective-permute-done.21 = bf16[2,1,384,512]{3,2,1,0:T(8,128)(2,1)S(1)} collective-permute-done((bf16[2,1,384,512]{3,2,1,0:T(8,128)(2,1)S(1)}, bf16[2,1,384,512]{3,2,1,0:T(8,128)(2,1)S(1)}, u32[]{:S(2)}, u32[]{:S(2)}) %collective-permute-start.21) | collective-permute-done | bytes 786464 | tf_op jit(solution)/shard_map/ppermute | solution.py:376
  299.3 8.6 %back.6 = (f32[2,1,384,512]{3,2,1,0:T(8,128)}, f32[1,2,384,512]{3,2,1,0:T(8,128)}, bf16[2,1,384,512]{3,2,1,0:T(8,128)(2,1)S(1)}, bf16[1,2,384,512]{3,2,1,0:T(8,128)(2,1)S(1)}) custom-call(s32[2]{0:T(128)S(1)} %pad_add_fusion.me, bf16[1536,1024]{1,0:T(8,128)(2,1)} %get-tuple-element.107.mine, bf16[1024,1024]{1,0:T(8,128)(2,1)} %get-tuple-element.150.mixed, ...), custom_call_target="tpu_custom_call" | custom-call | bytes 1024 | tf_op jit(solution)/shard_map/back/pallas_call | solution.py:290
  312.3 12.6 %collective-permute-done.27 = bf16[1,2,384,512]{3,2,1,0:T(8,128)(2,1)} collective-permute-done((bf16[1,2,384,512]{3,2,1,0:T(8,128)(2,1)S(1)}, bf16[1,2,384,512]{3,2,1,0:T(8,128)(2,1)}, u32[]{:S(2)}, u32[]{:S(2)}) %collective-permute-start.27) | collective-permute-done | bytes 786464 | tf_op jit(solution)/shard_map/ppermute | solution.py:376
  332.8 5.8 %back.7 = (f32[2,1,384,256]{3,2,1,0:T(8,128)S(1)}, f32[1,2,384,256]{3,2,1,0:T(8,128)}, bf16[2,1,384,256]{3,2,1,0:T(8,128)(2,1)S(1)}, bf16[1,2,384,256]{3,2,1,0:T(8,128)(2,1)S(1)}) custom-call(s32[2]{0:T(128)S(1)} %pad_add_fusion.me, bf16[1536,1024]{1,0:T(8,128)(2,1)} %get-tuple-element.107.mine, bf16[1024,512]{1,0:T(8,128)(2,1)} %copy-done.4, ...), custom_call_target="tpu_custom_call" | custom-call | bytes 1024 | tf_op jit(solution)/shard_map/back/pallas_call | solution.py:290
  342.7 6.4 %collective-permute-done.31 = bf16[2,1,384,256]{3,2,1,0:T(8,128)(2,1)S(1)} collective-permute-done((bf16[2,1,384,256]{3,2,1,0:T(8,128)(2,1)S(1)}, bf16[2,1,384,256]{3,2,1,0:T(8,128)(2,1)S(1)}, u32[]{:S(2)}, u32[]{:S(2)}) %collective-permute-start.31) | collective-permute-done | bytes 393248 | tf_op jit(solution)/shard_map/ppermute | solution.py:376
  351.6 3.4 collective-permute-done.32
  (143 shorter events, 59.7 us)
Async XLA Ops:
  6.5 186.0 %all-gather.2.cloned.1.call-start = ((), (), s32[]{:S(2)}) async-start(), calls=%async_computation | async-start | bytes 21233664 | tf_op jit(solution)/shard_map/all_gather | solution.py:400
  7.3 85.7 %collective-permute-start.5 = (bf16[384,3072]{1,0:T(8,128)(2,1)}, bf16[384,3072]{1,0:T(8,128)(2,1)}, u32[]{:S(2)}, u32[]{:S(2)}) collective-permute-start(bf16[384,3072]{1,0:T(8,128)(2,1)} %refs_0_.4), channel_id=1, source_target_pairs={{0,8},{4,12},{8,0},{12,4},{16,24},{20,28},{24,16},{28,20},{1,9},{5... | collective-permute-start | bytes 7077896 | tf_op jit(solution)/shard_map/ppermute | solution.py:376
  10.3 85.5 %collective-permute-start.7 = (bf16[384,3072]{1,0:T(8,128)(2,1)}, bf16[384,3072]{1,0:T(8,128)(2,1)}, u32[]{:S(2)}, u32[]{:S(2)}) collective-permute-start(bf16[384,3072]{1,0:T(8,128)(2,1)} %refs_0_.4), channel_id=1, source_target_pairs={{0,16},{4,20},{8,24},{12,28},{16,0},{20,4},{24,8},{28,12},{1,17},{... | collective-permute-start | bytes 7077896 | tf_op jit(solution)/shard_map/ppermute | solution.py:376
  11.8 38.4 %collective-permute-start = (bf16[1024,768]{1,0:T(8,128)(2,1)}, bf16[1024,768]{1,0:T(8,128)(2,1)S(1)}, u32[]{:S(2)}, u32[]{:S(2)}) collective-permute-start(bf16[1024,768]{1,0:T(8,128)(2,1)} %refs_0_.5), channel_id=1, source_target_pairs={{0,1},{1,3},{3,2},{2,0},{4,5},{5,7},{7,6},{6,4},{8,9},{9,11},{11,1... | collective-permute-start | bytes 4718600 | tf_op jit(solution)/shard_map/ppermute | solution.py:322
  13.4 68.8 %collective-permute-start.1 = (bf16[1024,768]{1,0:T(8,128)(2,1)S(1)}, bf16[1024,768]{1,0:T(8,128)(2,1)S(1)}, u32[]{:S(2)}, u32[]{:S(2)}) collective-permute-start(bf16[1024,768]{1,0:T(8,128)(2,1)S(1)} %copy-done.2), channel_id=1, source_target_pairs={{0,1},{1,3},{3,2},{2,0},{4,5},{5,7},{7,6},{6,4},{8,9},{9,11},{11,1... | collective-permute-start | bytes 4718600 | tf_op jit(solution)/shard_map/ppermute | solution.py:322
  16.0 86.0 %collective-permute-start.4 = (bf16[384,3072]{1,0:T(8,128)(2,1)}, bf16[384,3072]{1,0:T(8,128)(2,1)S(1)}, u32[]{:S(2)}, u32[]{:S(2)}) collective-permute-start(bf16[384,3072]{1,0:T(8,128)(2,1)} %refs_0_.4), channel_id=1, source_target_pairs={{0,4},{4,0},{8,12},{12,8},{16,20},{20,16},{24,28},{28,24},{1,5},{5... | collective-permute-start | bytes 7077896 | tf_op jit(solution)/shard_map/ppermute | solution.py:326
  83.3 38.3 %collective-permute-start.3 = (bf16[1024,768]{1,0:T(8,128)(2,1)S(1)}, bf16[1024,768]{1,0:T(8,128)(2,1)}, u32[]{:S(2)}, u32[]{:S(2)}) collective-permute-start(bf16[1024,768]{1,0:T(8,128)(2,1)S(1)} %collective-permute-done.1.refs_1_.refs_11_), channel_id=1, source_target_pairs={{0,1},{1,3},{3,2},{2,0},{4,5},{5,7},{7,6},{6,4},{8,9},{9,11},{11,1... | collective-permute-start | bytes 4718600 | tf_op jit(solution)/shard_map/ppermute | solution.py:322
  93.0 59.7 %collective-permute-start.6 = (bf16[384,3072]{1,0:T(8,128)(2,1)}, bf16[384,3072]{1,0:T(8,128)(2,1)}, u32[]{:S(2)}, u32[]{:S(2)}) collective-permute-start(bf16[384,3072]{1,0:T(8,128)(2,1)} %collective-permute-done.5.refs_2_), channel_id=1, source_target_pairs={{0,4},{4,0},{8,12},{12,8},{16,20},{20,16},{24,28},{28,24},{1,5},{5... | collective-permute-start | bytes 7077896 | tf_op jit(solution)/shard_map/ppermute | solution.py:326
  95.8 56.9 %collective-permute-start.8 = (bf16[384,3072]{1,0:T(8,128)(2,1)}, bf16[384,3072]{1,0:T(8,128)(2,1)}, u32[]{:S(2)}, u32[]{:S(2)}) collective-permute-start(bf16[384,3072]{1,0:T(8,128)(2,1)} %collective-permute-done.7.refs_4_), channel_id=1, source_target_pairs={{0,4},{4,0},{8,12},{12,8},{16,20},{20,16},{24,28},{28,24},{1,5},{5... | collective-permute-start | bytes 7077896 | tf_op jit(solution)/shard_map/ppermute | solution.py:326
  95.8 56.9 %collective-permute-start.2 = (bf16[1024,768]{1,0:T(8,128)(2,1)S(1)}, bf16[1024,768]{1,0:T(8,128)(2,1)}, u32[]{:S(2)}, u32[]{:S(2)}) collective-permute-start(bf16[1024,768]{1,0:T(8,128)(2,1)S(1)} %collective-permute-done.refs_1_), channel_id=1, source_target_pairs={{0,1},{1,3},{3,2},{2,0},{4,5},{5,7},{7,6},{6,4},{8,9},{9,11},{11,1... | collective-permute-start | bytes 4718600 | tf_op jit(solution)/shard_map/ppermute | solution.py:322
  102.0 55.0 %collective-permute-start.9 = (bf16[192,3072]{1,0:T(8,128)(2,1)}, bf16[192,3072]{1,0:T(8,128)(2,1)}, u32[]{:S(2)}, u32[]{:S(2)}) collective-permute-start(bf16[192,3072]{1,0:T(8,128)(2,1)} %slice.48), channel_id=1, source_target_pairs={{0,16},{4,20},{8,24},{12,28},{16,0},{20,4},{24,8},{28,12},{1,17},{... | collective-permute-start | bytes 3538952 | tf_op jit(solution)/shard_map/ppermute | solution.py:376
  121.7 41.3 %collective-permute-start.11 = (bf16[192,3072]{1,0:T(8,128)(2,1)}, bf16[192,3072]{1,0:T(8,128)(2,1)}, u32[]{:S(2)}, u32[]{:S(2)}) collective-permute-start(bf16[192,3072]{1,0:T(8,128)(2,1)} %slice.49), channel_id=1, source_target_pairs={{0,8},{4,12},{8,0},{12,4},{16,24},{20,28},{24,16},{28,20},{1,9},{5... | collective-permute-start | bytes 3538952 | tf_op jit(solution)/shard_map/ppermute | solution.py:376
  152.7 39.8 %collective-permute-start.13 = (bf16[1024,768]{1,0:T(8,128)(2,1)}, bf16[1024,768]{1,0:T(8,128)(2,1)}, u32[]{:S(2)}, u32[]{:S(2)}) collective-permute-start(bf16[1024,768]{1,0:T(8,128)(2,1)} %collective-permute-done.2.refs_2_), channel_id=1, source_target_pairs={{0,1},{1,3},{3,2},{2,0},{4,5},{5,7},{7,6},{6,4},{8,9},{9,11},{11,1... | collective-permute-start | bytes 4718600 | tf_op jit(solution)/shard_map/ppermute | solution.py:322
  153.5 68.3 %collective-permute-start.14 = (bf16[1024,768]{1,0:T(8,128)(2,1)}, bf16[1024,768]{1,0:T(8,128)(2,1)S(1)}, u32[]{:S(2)}, u32[]{:S(2)}) collective-permute-start(bf16[1024,768]{1,0:T(8,128)(2,1)} %collective-permute-done.3.refs_2_.refs_12_), channel_id=1, source_target_pairs={{0,1},{1,3},{3,2},{2,0},{4,5},{5,7},{7,6},{6,4},{8,9},{9,11},{11,1... | collective-permute-start | bytes 4718600 | tf_op jit(solution)/shard_map/ppermute | solution.py:322
  156.9 12.6 %collective-permute-start.10 = (bf16[192,3072]{1,0:T(8,128)(2,1)}, bf16[192,3072]{1,0:T(8,128)(2,1)}, u32[]{:S(2)}, u32[]{:S(2)}) collective-permute-start(bf16[192,3072]{1,0:T(8,128)(2,1)} %collective-permute-done.9.refs_6_), channel_id=1, source_target_pairs={{0,4},{4,0},{8,12},{12,8},{16,20},{20,16},{24,28},{28,24},{1,5},{5... | collective-permute-start | bytes 3538952 | tf_op jit(solution)/shard_map/ppermute | solution.py:326
  242.5 22.9 %collective-permute-start.18 = (bf16[1536,1024]{1,0:T(8,128)(2,1)}, bf16[1536,1024]{1,0:T(8,128)(2,1)}, u32[]{:S(2)}, u32[]{:S(2)}) collective-permute-start(bf16[1536,1024]{1,0:T(8,128)(2,1)} %get-tuple-element.132), channel_id=1, source_target_pairs={{0,4},{4,0},{8,12},{12,8},{16,20},{20,16},{24,28},{28,24},{1,5},{5... | collective-permute-start | bytes 9437192 | tf_op jit(solution)/shard_map/ppermute | solution.py:326
  249.5 13.7 %collective-permute-start.16 = (bf16[2,1,384,256]{3,2,1,0:T(8,128)(2,1)S(1)}, bf16[2,1,384,256]{3,2,1,0:T(8,128)(2,1)S(1)}, u32[]{:S(2)}, u32[]{:S(2)}) collective-permute-start(bf16[2,1,384,256]{3,2,1,0:T(8,128)(2,1)S(1)} %get-tuple-element.123), channel_id=1, source_target_pairs={{0,8},{4,12},{8,0},{12,4},{16,24},{20,28},{24,16},{28,20},{1,9},{5... | collective-permute-start | bytes 1179656 | tf_op jit(solution)/shard_map/ppermute | solution.py:376
  251.3 12.0 %collective-permute-start.17 = (bf16[1,2,384,256]{3,2,1,0:T(8,128)(2,1)S(1)}, bf16[1,2,384,256]{3,2,1,0:T(8,128)(2,1)S(1)}, u32[]{:S(2)}, u32[]{:S(2)}) collective-permute-start(bf16[1,2,384,256]{3,2,1,0:T(8,128)(2,1)S(1)} %get-tuple-element.124), channel_id=1, source_target_pairs={{0,16},{4,20},{8,24},{12,28},{16,0},{20,4},{24,8},{28,12},{1,17},{... | collective-permute-start | bytes 1179656 | tf_op jit(solution)/shard_map/ppermute | solution.py:376
  263.3 36.0 %collective-permute-start.23 = (bf16[1536,1024]{1,0:T(8,128)(2,1)}, bf16[1536,1024]{1,0:T(8,128)(2,1)}, u32[]{:S(2)}, u32[]{:S(2)}) collective-permute-start(bf16[1536,1024]{1,0:T(8,128)(2,1)} %get-tuple-element.151), channel_id=1, source_target_pairs={{0,4},{4,0},{8,12},{12,8},{16,20},{20,16},{24,28},{28,24},{1,5},{5... | collective-permute-start | bytes 9437192 | tf_op jit(solution)/shard_map/ppermute | solution.py:326
  274.8 18.8 %collective-permute-start.21 = (bf16[2,1,384,512]{3,2,1,0:T(8,128)(2,1)S(1)}, bf16[2,1,384,512]{3,2,1,0:T(8,128)(2,1)S(1)}, u32[]{:S(2)}, u32[]{:S(2)}) collective-permute-start(bf16[2,1,384,512]{3,2,1,0:T(8,128)(2,1)S(1)} %get-tuple-element.142), channel_id=1, source_target_pairs={{0,8},{4,12},{8,0},{12,4},{16,24},{20,28},{24,16},{28,20},{1,9},{5... | collective-permute-start | bytes 2359304 | tf_op jit(solution)/shard_map/ppermute | solution.py:376
  276.5 18.4 %collective-permute-start.22 = (bf16[1,2,384,512]{3,2,1,0:T(8,128)(2,1)S(1)}, bf16[1,2,384,512]{3,2,1,0:T(8,128)(2,1)S(1)}, u32[]{:S(2)}, u32[]{:S(2)}) collective-permute-start(bf16[1,2,384,512]{3,2,1,0:T(8,128)(2,1)S(1)} %get-tuple-element.143), channel_id=1, source_target_pairs={{0,16},{4,20},{8,24},{12,28},{16,0},{20,4},{24,8},{28,12},{1,17},{... | collective-permute-start | bytes 2359304 | tf_op jit(solution)/shard_map/ppermute | solution.py:376
  307.8 17.1 %collective-permute-start.27 = (bf16[1,2,384,512]{3,2,1,0:T(8,128)(2,1)S(1)}, bf16[1,2,384,512]{3,2,1,0:T(8,128)(2,1)}, u32[]{:S(2)}, u32[]{:S(2)}) collective-permute-start(bf16[1,2,384,512]{3,2,1,0:T(8,128)(2,1)S(1)} %get-tuple-element.161), channel_id=1, source_target_pairs={{0,16},{4,20},{8,24},{12,28},{16,0},{20,4},{24,8},{28,12},{1,17},{... | collective-permute-start | bytes 2359304 | tf_op jit(solution)/shard_map/ppermute | solution.py:376
  308.4 18.1 %collective-permute-start.26 = (bf16[2,1,384,512]{3,2,1,0:T(8,128)(2,1)S(1)}, bf16[2,1,384,512]{3,2,1,0:T(8,128)(2,1)S(1)}, u32[]{:S(2)}, u32[]{:S(2)}) collective-permute-start(bf16[2,1,384,512]{3,2,1,0:T(8,128)(2,1)S(1)} %get-tuple-element.159), channel_id=1, source_target_pairs={{0,8},{4,12},{8,0},{12,4},{16,24},{20,28},{24,16},{28,20},{1,9},{5... | collective-permute-start | bytes 2359304 | tf_op jit(solution)/shard_map/ppermute | solution.py:376
  311.2 20.4 %collective-permute-start.28 = (bf16[1536,512]{1,0:T(8,128)(2,1)}, bf16[1536,512]{1,0:T(8,128)(2,1)S(1)}, u32[]{:S(2)}, u32[]{:S(2)}) collective-permute-start(bf16[1536,512]{1,0:T(8,128)(2,1)} %get-tuple-element.164), channel_id=1, source_target_pairs={{0,4},{4,0},{8,12},{12,8},{16,20},{20,16},{24,28},{28,24},{1,5},{5... | collective-permute-start | bytes 4718600 | tf_op jit(solution)/shard_map/ppermute | solution.py:326
  (38 other events, 517.1 us)
Sparse Core Ops, SparseCore 0:
  9.2 157.9 all-gather.1

commit v6 on v5

--- a/solution.py
+++ b/solution.py
@@ -9,7 +9,7 @@
 from jax.sharding import PartitionSpec as P
 
 inv_root = 1.0 / math.sqrt(2.0 * math.pi)
-sixths = (1, 2, 2, 1)
+sixths = (2, 1, 2, 1)
 f32 = jnp.float32
 bf16 = jnp.bfloat16
 
@@ -326,25 +326,11 @@
     return lax.ppermute(block, "dp", shift(cores, 1, dp, 1))
 
 
-def parted(parts, dim, n, digit):
-    own = lax.dynamic_index_in_dim(parts, digit, dim, keepdims=True)
-    sends = [
-        lax.dynamic_index_in_dim(parts, lax.rem(digit + by, n), dim, keepdims=True).astype(bf16)
-        for by in range(1, n)
-    ]
-    return own, sends
-
-
-def sent(sends, n, stride, total):
-    return [
-        lax.ppermute(send, "dp", shift(n, stride, total, by + 1)) for by, send in enumerate(sends)
-    ]
-
-
-def summed(own, received):
+def block_sum(own, received, dim, at):
+    total = lax.dynamic_index_in_dim(own, at, dim, keepdims=True)
     for r in received:
-        own = own + r.astype(f32)
-    return own
+        total = total + lax.dynamic_index_in_dim(r, at, dim, keepdims=True).astype(f32)
+    return total
 
 
 def shards(tokens, cotangent, codes, row_scale, probe, down_weight):
@@ -396,6 +382,10 @@
                 (cot[s], tok[s], near_too, at, row_scale[:, None], slots)
             )
             near = [(pair[0], other) for pair, other in zip(near, near_too)]
+    plain = rows % 128 != 0
+    if not plain:
+        early = list(split_cores(tok[:-1], at[:-1], core, tp))
+        early[0], far[-1] = lax.optimization_barrier((early[0], far[-1]))
     far = [(p, swapped(p, dp, cores)) for p in far]
     down_full = lax.all_gather(down_weight, "dp", axis=0, tiled=True)
 
@@ -404,10 +394,6 @@
         [[t] for t in tok[:-1]], at, pieces, slots, rows // 2, rows * dp, unit
     )
     begun, cot[-1] = after(begun, cot[-1])
-    plain = rows % 128 != 0
-    if not plain:
-        early = list(split_cores(tok[:-1], at[:-1], core, tp))
-        early[0], cot[-1] = after(early[0], cot[-1])
     bent = bent_of([[c] for c in cot], at, scale, codes, down_full, unit)
     bent, tok[-1] = lax.optimization_barrier((bent, tok[-1]))
     if plain:
@@ -418,50 +404,71 @@
     count = len(sixths)
     out = {}
 
-    def finish(j, keeps, arrived):
-        middle = (edges[j] + edges[j + 1]) // 2
-        for k, (a, b) in enumerate(((edges[j], middle), (middle, edges[j + 1]))):
-            hessian = summed(keeps[k], arrived[k]).reshape(rows, b - a)
-            out[2 * j + k] = probe[:, a:b].astype(f32) * hessian * (1.0 / (tok_rows * dp))
-
     def front(j, ready):
         return front_of(tok[-1], ready, begun, bent, other, edges[j], edges[j + 1] - edges[j])
 
-    fronts = {0: front(0, last)}
-    came = {0: swapped(fronts[0][1], dp, cores)}
-    mixed = fronts[0][0]
+    def back(j):
+        return back_of(mine, mixed.pop(j), came.pop(j), x, y, xs, ys, rows)
+
+    def first_turn(to_x, to_y):
+        return (
+            [over(to_x[:, i - 1 : i], x_way, i) for i in range(1, xs)],
+            [over(to_y[k - 1 : k], y_way, k) for k in range(1, ys)],
+        )
+
+    def finish(j, keeps, first, second):
+        middle = (edges[j] + edges[j + 1]) // 2
+        for n, (a, b) in enumerate(((edges[j], middle), (middle, edges[j + 1]))):
+            total = block_sum(keeps[n], first[n], n, (y, x)[n])
+            for r in second[n]:
+                total = total + r.astype(f32)
+            weight = probe[:, a:b].astype(f32)
+            out[2 * j + n] = weight * total.reshape(rows, b - a) * (1.0 / (tok_rows * dp))
+
+    mixed, came, keeps = {}, {}, {}
+    mixed[0], away = front(0, last)
+    came[0] = swapped(away, dp, cores)
     if count > 1:
-        mixed, last = lax.optimization_barrier((mixed, last))
-        following, away = front(1, last)
-        mixed, following, away, came[0] = lax.optimization_barrier(
-            (mixed, following, away, came[0])
-        )
+        mixed[0], last = lax.optimization_barrier((mixed[0], last))
+        mixed[1], away = front(1, last)
+        mixed[0], away, came[0] = lax.optimization_barrier((mixed[0], away, came[0]))
         came[1] = swapped(away, dp, cores)
+    *keeps[0], to_x, to_y = back(0)
     behind = None
     for j in range(count):
-        keep_x, keep_y, to_x, to_y = back_of(mine, mixed, came[j], x, y, xs, ys, rows)
-        if behind is not None:
-            keeps, arrived = behind
-            to_x, to_y, arrived = lax.optimization_barrier((to_x, to_y, arrived))
-            finish(j - 1, keeps, arrived)
-        ahead = j + 2 < count
-        if ahead:
+        if j + 1 < count:
+            to_x, to_y, mixed[j + 1] = lax.optimization_barrier((to_x, to_y, mixed[j + 1]))
+        first = first_turn(to_x, to_y)
+        if j + 1 < count:
+            *keeps[j + 1], to_x, to_y = back(j + 1)
+        if j + 2 < count:
             to_x, to_y, last = lax.optimization_barrier((to_x, to_y, last))
-        from_x = [over(to_x[:, i - 1 : i], x_way, i) for i in range(1, xs)]
-        from_y = [over(to_y[k - 1 : k], y_way, k) for k in range(1, ys)]
-        if ahead:
-            beyond, away = front(j + 2, last)
-            from_x, from_y, away = lax.optimization_barrier((from_x, from_y, away))
+            mixed[j + 2], away = front(j + 2, last)
+            first, away, to_x, to_y, behind = lax.optimization_barrier(
+                (first, away, to_x, to_y, behind)
+            )
             came[j + 2] = swapped(away, dp, cores)
-        left, left_sends = parted(summed(keep_x, from_x), 0, ys, y)
-        right, right_sends = parted(summed(keep_y, from_y), 1, xs, x)
+        elif j + 1 < count:
+            first, to_x, to_y, behind = lax.optimization_barrier((first, to_x, to_y, behind))
+        if j >= 1:
+            finish(j - 1, *behind)
+        sends_y = [
+            block_sum(keeps[j][0], first[0], 0, lax.rem(y + k, ys)).astype(bf16)
+            for k in range(1, ys)
+        ]
+        sends_x = [
+            block_sum(keeps[j][1], first[1], 1, lax.rem(x + i, xs)).astype(bf16)
+            for i in range(1, xs)
+        ]
         if j + 1 < count:
-            left_sends, right_sends, mixed = lax.optimization_barrier(
-                (left_sends, right_sends, following)
+            sends_y, sends_x, to_x, to_y = lax.optimization_barrier(
+                (sends_y, sends_x, to_x, to_y)
             )
-        if ahead:
-            following = beyond
-        behind = (left, right), (sent(left_sends, *y_way, dp), sent(right_sends, *x_way, dp))
+        second = (
+            [over(p, y_way, k + 1) for k, p in enumerate(sends_y)],
+            [over(p, x_way, i + 1) for i, p in enumerate(sends_x)],
+        )
+        behind = (keeps.pop(j), first, second)
     finish(count - 1, *behind)
     return jnp.concatenate([out[j] for j in range(2 * count)], axis=1)
 

time: 364 us -> 358 us (0.984)
  waiting for transfers between devices: 163 us -> 154 us
  other arithmetic: 9.02 us -> 15.7 us
    ppermute x12 -> x20, waiting for transfers between devices: 45.9 us -> 35.1 us  [over(): return lax.ppermute(block, 'dp', shift(way[0], way[1], dp, by))]
    ppermute x8 -> x0, starting transfers between devices: 7.2 us -> none  [sent(): lax.ppermute(send, 'dp', shift(n, stride, total, by + 1))]
    ppermute x12 -> x20, starting transfers between devices: 18.3 us -> 23.5 us  [over(): return lax.ppermute(block, 'dp', shift(way[0], way[1], dp, by))]
    convert_element_type x0 -> x7, other arithmetic: none -> 5.02 us  [the longest x4 3.05 us: shards(): block_sum(keeps[j][1], first[1], 1, lax.rem(x + i, xs)).astype(bf16)]
    unnamed x7, other arithmetic: 5.46 us -> 9.78 us
  transfers between devices with their start and end apart: 36 -> 36, of which waited for: 12 -> 15; matrix products, arithmetic and copies ran while one was open for 4% -> 6% of each run, Pallas kernels for 32% -> 31%
where the time goes in v6:
time: 358 us
  waiting for transfers between devices  154 us (43%)
  Pallas kernels  125 us (35%)
  starting transfers between devices  34.7 us (10%)
  other arithmetic  15.7 us (4%)
  local copies, waits for them, and re-layouts  14.7 us (4%)
  between operations  13.6 us (4%)
    ppermute x6, waiting for transfers between devices, ring_step(): return lax.ppermute(block, 'tensor', pairs)  116 us
    pallas_call x4, Pallas kernels, front_of(): pl.pallas_call(front_body, grid=(wide // tile,), in_specs=[whole((tok, wi...  36.3 us
    ppermute x20, waiting for transfers between devices, over(): return lax.ppermute(block, 'dp', shift(way[0], way[1], dp, by))  35.1 us
    pallas_call x4, Pallas kernels, back_of(): pl.pallas_call(functools.partial(back_body, xs, ys, rows, steps), grid_sp...  29.3 us
    pallas_call x1, Pallas kernels, bent_of(): pl.pallas_call(functools.partial(bent_body, count, parts, width), grid_sp...  29.2 us
    ppermute x20, starting transfers between devices, over(): return lax.ppermute(block, 'dp', shift(way[0], way[1], dp, by))  23.5 us
    pallas_call x1, Pallas kernels, partial_tangent(): pl.pallas_call(functools.partial(partial_body, count, parts, width, spots...  23 us
    ppermute x6, starting transfers between devices, ring_step(): return lax.ppermute(block, 'tensor', pairs)  10.6 us
  transfers between devices with their start and end apart: 36, of which 15 were waited for; matrix products, arithmetic and copies ran while one was open for 6% of the time, Pallas kernels for 31%

profile of v6, /device:TPU:0, one launch (start us, length us, event | category | flops | bytes accessed | tf_op | source)
XLA Modules:
  0.0 357.8 jit_solution(13569547753920210391)
XLA Ops:
  7.3 3.0 collective-permute-start.5
  13.4 2.6 collective-permute-start.1
  16.0 34.3 %collective-permute-done.refs_1_ = bf16[1024,768]{1,0:T(8,128)(2,1)S(1)} collective-permute-done((bf16[1024,768]{1,0:T(8,128)(2,1)}, bf16[1024,768]{1,0:T(8,128)(2,1)S(1)}, u32[]{:S(2)}, u32[]{:S(2)}) %collective-permute-start) | collective-permute-done | bytes 1572896 | tf_op jit(solution)/shard_map/ppermute | solution.py:322
  50.2 31.9 %collective-permute-done.1.refs_1_.refs_11_ = bf16[1024,768]{1,0:T(8,128)(2,1)S(1)} collective-permute-done((bf16[1024,768]{1,0:T(8,128)(2,1)S(1)}, bf16[1024,768]{1,0:T(8,128)(2,1)S(1)}, u32[]{:S(2)}, u32[]{:S(2)}) %collective-permute-start.1) | collective-permute-done | bytes 1572896 | tf_op jit(solution)/shard_map/ppermute | solution.py:322
  84.1 8.8 %collective-permute-done.5.refs_2_ = bf16[384,3072]{1,0:T(8,128)(2,1)} collective-permute-done((bf16[384,3072]{1,0:T(8,128)(2,1)}, bf16[384,3072]{1,0:T(8,128)(2,1)}, u32[]{:S(2)}, u32[]{:S(2)}) %collective-permute-start.5) | collective-permute-done | bytes 2359328 | tf_op jit(solution)/shard_map/ppermute | solution.py:362
  93.0 2.8 collective-permute-done.7.refs_4_
  99.6 2.5 collective-permute-start.9
  104.5 17.2 %collective-permute-done.3.refs_2_.refs_12_ = bf16[1024,768]{1,0:T(8,128)(2,1)} collective-permute-done((bf16[1024,768]{1,0:T(8,128)(2,1)S(1)}, bf16[1024,768]{1,0:T(8,128)(2,1)}, u32[]{:S(2)}, u32[]{:S(2)}) %collective-permute-start.3) | collective-permute-done | bytes 1572896 | tf_op jit(solution)/shard_map/ppermute | solution.py:322
  123.0 29.7 %collective-permute-done.2.refs_2_ = bf16[1024,768]{1,0:T(8,128)(2,1)} collective-permute-done((bf16[1024,768]{1,0:T(8,128)(2,1)S(1)}, bf16[1024,768]{1,0:T(8,128)(2,1)}, u32[]{:S(2)}, u32[]{:S(2)}) %collective-permute-start.2) | collective-permute-done | bytes 1572896 | tf_op jit(solution)/shard_map/ppermute | solution.py:322
  153.4 3.5 collective-permute-start.14
  156.9 4.9 %split_cores.2 = (bf16[1536,1024]{1,0:T(8,128)(2,1)}, bf16[1536,1024]{1,0:T(8,128)(2,1)}) custom-call(s32[1]{0:T(128)} %bitcast.2.core, s32[3]{0:T(128)S(1)} %bitcast.65, bf16[1024,768]{1,0:T(8,128)(2,1)S(1)} %copy-done.2, bf16[1024,768]{1,0:T(8,128)(2,1)} %copy-done.6, bf16[1024,768]{1,0:T(8,128)(2,1)} %collective-permute-done.3.refs_2_.refs_12_), custom_call_target="tpu_custom_call" | custom-call | bytes 1024 | tf_op jit(solution)/shard_map/split_cores/pallas_call | solution.py:57
  166.1 23.0 %partial_tangent.1 = (f32[6,1024,512]{2,1,0:T(8,128)}, bf16[6,768,512]{2,1,0:T(8,128)(2,1)}) custom-call(s32[4]{0:T(128)S(1)} %fusion.16.at, s32[10]{0:T(128)S(1)} %stack.64.slots, bf16[384,3072]{1,0:T(8,128)(2,1)} %refs_0_.4, bf16[384,3072]{1,0:T(8,128)(2,1)} %copy-done.8, bf16[384,3072]{1,0:T(8,128)(2,1)} %collective-permute-done.5.refs_2_, ...), custom_call_target="tpu_custom_call" | custom-call | bytes 1024 | tf_op jit(solution)/shard_map/partial_tangent/pallas_call | solution.py:190
  191.3 29.2 %bent.1 = f32[6,1024,512]{2,1,0:T(8,128)} custom-call(s32[4]{0:T(128)S(1)} %fusion.16.at, f32[1024,1]{1,0:T(8,128)S(1)} %copy.10.scale, s32[1024,3072]{1,0:T(8,128)} %codes.1, bf16[3072,3072]{1,0:T(8,128)(2,1)} %all-gather.2.cloned.1.call-done.down, bf16[1024,768]{1,0:T(8,128)(2,1)} %refs_0_.5, bf16[1024,768]{1,0:T(8,128)(2,1)} %copy-done.9, ...), custom_call_target="tpu_custom_call" | custom-call | bytes 1024 | tf_op jit(solution)/shard_map/bent/pallas_call | solution.py:121
  223.3 10.6 %front.4 = (bf16[1024,1024]{1,0:T(8,128)(2,1)}, bf16[1536,1024]{1,0:T(8,128)(2,1)}) custom-call(bf16[1024,768]{1,0:T(8,128)(2,1)S(1)} %collective-permute-done.14.refs_0_.shard, bf16[6,768,512]{2,1,0:T(8,128)(2,1)} %get-tuple-element.166.probe, f32[6,1024,512]{2,1,0:T(8,128)} %get-tuple-element.128.begun, f32[6,1024,512]{2,1,0:T(8,128)} %bent.1, ...), custom_call_target="tpu_custom_call" | custom-call | bytes 1024 | tf_op jit(solution)/shard_map/front/pallas_call | solution.py:229
  233.9 7.7 %front.5 = (bf16[1024,512]{1,0:T(8,128)(2,1)S(1)}, bf16[1536,512]{1,0:T(8,128)(2,1)}) custom-call(bf16[1024,768]{1,0:T(8,128)(2,1)} %copy-done, bf16[6,768,512]{2,1,0:T(8,128)(2,1)} %get-tuple-element.166.probe, f32[6,1024,512]{2,1,0:T(8,128)} %get-tuple-element.128.begun, f32[6,1024,512]{2,1,0:T(8,128)} %bent.1, bf16[1536,1024]{1,0:T(8,128)(2,1)} %get-tuple-element.130.other), custom_call_target="tpu_custom_call" | custom-call | bytes 1024 | tf_op jit(solution)/shard_map/front/pallas_call | solution.py:229
  244.2 8.6 %back.4 = (f32[2,1,384,512]{3,2,1,0:T(8,128)}, f32[1,2,384,512]{3,2,1,0:T(8,128)}, bf16[2,1,384,512]{3,2,1,0:T(8,128)(2,1)S(1)}, bf16[1,2,384,512]{3,2,1,0:T(8,128)(2,1)S(1)}) custom-call(s32[2]{0:T(128)S(1)} %pad_add_fusion.me, bf16[1536,1024]{1,0:T(8,128)(2,1)} %get-tuple-element.126.mine, bf16[1024,1024]{1,0:T(8,128)(2,1)} %get-tuple-element.136.mixed, ...), custom_call_target="tpu_custom_call" | custom-call | bytes 1024 | tf_op jit(solution)/shard_map/back/pallas_call | solution.py:290
  255.6 6.0 %back.5 = (f32[2,1,384,256]{3,2,1,0:T(8,128)S(1)}, f32[1,2,384,256]{3,2,1,0:T(8,128)}, bf16[2,1,384,256]{3,2,1,0:T(8,128)(2,1)S(1)}, bf16[1,2,384,256]{3,2,1,0:T(8,128)(2,1)S(1)}) custom-call(s32[2]{0:T(128)S(1)} %pad_add_fusion.me, bf16[1536,1024]{1,0:T(8,128)(2,1)} %get-tuple-element.126.mine, bf16[1024,512]{1,0:T(8,128)(2,1)} %copy-done.4, ...), custom_call_target="tpu_custom_call" | custom-call | bytes 1024 | tf_op jit(solution)/shard_map/back/pallas_call | solution.py:290
  261.6 10.4 %front.6 = (bf16[1024,1024]{1,0:T(8,128)(2,1)}, bf16[1536,1024]{1,0:T(8,128)(2,1)}) custom-call(bf16[1024,768]{1,0:T(8,128)(2,1)S(1)} %copy-done.1, bf16[6,768,512]{2,1,0:T(8,128)(2,1)} %get-tuple-element.166.probe, f32[6,1024,512]{2,1,0:T(8,128)} %get-tuple-element.128.begun, f32[6,1024,512]{2,1,0:T(8,128)} %bent.1, bf16[1536,1024]{1,0:T(8,128)(2,1)} %get-tuple-element.130.other), custom_call_target="tpu_custom_call" | custom-call | bytes 1024 | tf_op jit(solution)/shard_map/front/pallas_call | solution.py:229
  279.1 8.7 %back.6 = (f32[2,1,384,512]{3,2,1,0:T(8,128)}, f32[1,2,384,512]{3,2,1,0:T(8,128)}, bf16[2,1,384,512]{3,2,1,0:T(8,128)(2,1)S(1)}, bf16[1,2,384,512]{3,2,1,0:T(8,128)(2,1)S(1)}) custom-call(s32[2]{0:T(128)S(1)} %pad_add_fusion.me, bf16[1536,1024]{1,0:T(8,128)(2,1)} %get-tuple-element.126.mine, bf16[1024,1024]{1,0:T(8,128)(2,1)} %get-tuple-element.162.mixed, ...), custom_call_target="tpu_custom_call" | custom-call | bytes 1024 | tf_op jit(solution)/shard_map/back/pallas_call | solution.py:290
  287.8 7.7 %front.7 = (bf16[1024,512]{1,0:T(8,128)(2,1)S(1)}, bf16[1536,512]{1,0:T(8,128)(2,1)}) custom-call(bf16[1024,768]{1,0:T(8,128)(2,1)} %copy-done, bf16[6,768,512]{2,1,0:T(8,128)(2,1)} %get-tuple-element.166.probe, f32[6,1024,512]{2,1,0:T(8,128)} %get-tuple-element.128.begun, f32[6,1024,512]{2,1,0:T(8,128)} %bent.1, bf16[1536,1024]{1,0:T(8,128)(2,1)} %get-tuple-element.130.other), custom_call_target="tpu_custom_call" | custom-call | bytes 1024 | tf_op jit(solution)/shard_map/front/pallas_call | solution.py:229
  307.7 6.0 %back.7 = (f32[2,1,384,256]{3,2,1,0:T(8,128)S(1)}, f32[1,2,384,256]{3,2,1,0:T(8,128)}, bf16[2,1,384,256]{3,2,1,0:T(8,128)(2,1)S(1)}, bf16[1,2,384,256]{3,2,1,0:T(8,128)(2,1)S(1)}) custom-call(s32[2]{0:T(128)S(1)} %pad_add_fusion.me, bf16[1536,1024]{1,0:T(8,128)(2,1)} %get-tuple-element.126.mine, bf16[1024,512]{1,0:T(8,128)(2,1)} %copy-done.3, ...), custom_call_target="tpu_custom_call" | custom-call | bytes 1024 | tf_op jit(solution)/shard_map/back/pallas_call | solution.py:290
  313.7 9.7 %collective-permute-done.27 = bf16[1,1,384,256]{3,2,1,0:T(8,128)(2,1)S(1)} collective-permute-done((bf16[1,1,384,256]{3,2,1,0:T(8,128)(2,1)}, bf16[1,1,384,256]{3,2,1,0:T(8,128)(2,1)S(1)}, u32[]{:S(2)}, u32[]{:S(2)}) %collective-permute-start.27) | collective-permute-done | bytes 196640 | tf_op jit(solution)/shard_map/ppermute | solution.py:362
  332.2 5.4 %collective-permute-done.33 = bf16[1,2,384,256]{3,2,1,0:T(8,128)(2,1)S(1)} collective-permute-done((bf16[1,2,384,256]{3,2,1,0:T(8,128)(2,1)S(1)}, bf16[1,2,384,256]{3,2,1,0:T(8,128)(2,1)S(1)}, u32[]{:S(2)}, u32[]{:S(2)}) %collective-permute-start.33) | collective-permute-done | bytes 393248 | tf_op jit(solution)/shard_map/ppermute | solution.py:362
  339.7 6.3 %collective-permute-done.29 = bf16[1,1,384,512]{3,2,1,0:T(8,128)(2,1)S(1)} collective-permute-done((bf16[1,1,384,512]{3,2,1,0:T(8,128)(2,1)S(1)}, bf16[1,1,384,512]{3,2,1,0:T(8,128)(2,1)S(1)}, u32[]{:S(2)}, u32[]{:S(2)}) %collective-permute-start.29) | collective-permute-done | bytes 393248 | tf_op jit(solution)/shard_map/ppermute | solution.py:362
  (135 shorter events, 63.7 us)
Async XLA Ops:
  6.5 184.8 %all-gather.2.cloned.1.call-start = ((), (), s32[]{:S(2)}) async-start(), calls=%async_computation | async-start | bytes 21233664 | tf_op jit(solution)/shard_map/all_gather | solution.py:390
  7.3 85.7 %collective-permute-start.5 = (bf16[384,3072]{1,0:T(8,128)(2,1)}, bf16[384,3072]{1,0:T(8,128)(2,1)}, u32[]{:S(2)}, u32[]{:S(2)}) collective-permute-start(bf16[384,3072]{1,0:T(8,128)(2,1)} %refs_0_.4), channel_id=1, source_target_pairs={{0,8},{4,12},{8,0},{12,4},{16,24},{20,28},{24,16},{28,20},{1,9},{5... | collective-permute-start | bytes 7077896 | tf_op jit(solution)/shard_map/ppermute | solution.py:362
  10.3 85.5 %collective-permute-start.7 = (bf16[384,3072]{1,0:T(8,128)(2,1)}, bf16[384,3072]{1,0:T(8,128)(2,1)}, u32[]{:S(2)}, u32[]{:S(2)}) collective-permute-start(bf16[384,3072]{1,0:T(8,128)(2,1)} %refs_0_.4), channel_id=1, source_target_pairs={{0,16},{4,20},{8,24},{12,28},{16,0},{20,4},{24,8},{28,12},{1,17},{... | collective-permute-start | bytes 7077896 | tf_op jit(solution)/shard_map/ppermute | solution.py:362
  11.8 38.4 %collective-permute-start = (bf16[1024,768]{1,0:T(8,128)(2,1)}, bf16[1024,768]{1,0:T(8,128)(2,1)S(1)}, u32[]{:S(2)}, u32[]{:S(2)}) collective-permute-start(bf16[1024,768]{1,0:T(8,128)(2,1)} %refs_0_.5), channel_id=1, source_target_pairs={{0,1},{1,3},{3,2},{2,0},{4,5},{5,7},{7,6},{6,4},{8,9},{9,11},{11,1... | collective-permute-start | bytes 4718600 | tf_op jit(solution)/shard_map/ppermute | solution.py:322
  13.4 68.8 %collective-permute-start.1 = (bf16[1024,768]{1,0:T(8,128)(2,1)S(1)}, bf16[1024,768]{1,0:T(8,128)(2,1)S(1)}, u32[]{:S(2)}, u32[]{:S(2)}) collective-permute-start(bf16[1024,768]{1,0:T(8,128)(2,1)S(1)} %copy-done.2), channel_id=1, source_target_pairs={{0,1},{1,3},{3,2},{2,0},{4,5},{5,7},{7,6},{6,4},{8,9},{9,11},{11,1... | collective-permute-start | bytes 4718600 | tf_op jit(solution)/shard_map/ppermute | solution.py:322
  16.0 83.6 %collective-permute-start.4 = (bf16[384,3072]{1,0:T(8,128)(2,1)}, bf16[384,3072]{1,0:T(8,128)(2,1)S(1)}, u32[]{:S(2)}, u32[]{:S(2)}) collective-permute-start(bf16[384,3072]{1,0:T(8,128)(2,1)} %refs_0_.4), channel_id=1, source_target_pairs={{0,4},{4,0},{8,12},{12,8},{16,20},{20,16},{24,28},{28,24},{1,5},{5... | collective-permute-start | bytes 7077896 | tf_op jit(solution)/shard_map/ppermute | solution.py:326
  83.3 38.3 %collective-permute-start.3 = (bf16[1024,768]{1,0:T(8,128)(2,1)S(1)}, bf16[1024,768]{1,0:T(8,128)(2,1)}, u32[]{:S(2)}, u32[]{:S(2)}) collective-permute-start(bf16[1024,768]{1,0:T(8,128)(2,1)S(1)} %collective-permute-done.1.refs_1_.refs_11_), channel_id=1, source_target_pairs={{0,1},{1,3},{3,2},{2,0},{4,5},{5,7},{7,6},{6,4},{8,9},{9,11},{11,1... | collective-permute-start | bytes 4718600 | tf_op jit(solution)/shard_map/ppermute | solution.py:322
  93.0 59.7 %collective-permute-start.6 = (bf16[384,3072]{1,0:T(8,128)(2,1)}, bf16[384,3072]{1,0:T(8,128)(2,1)}, u32[]{:S(2)}, u32[]{:S(2)}) collective-permute-start(bf16[384,3072]{1,0:T(8,128)(2,1)} %collective-permute-done.5.refs_2_), channel_id=1, source_target_pairs={{0,4},{4,0},{8,12},{12,8},{16,20},{20,16},{24,28},{28,24},{1,5},{5... | collective-permute-start | bytes 7077896 | tf_op jit(solution)/shard_map/ppermute | solution.py:326
  95.8 56.9 %collective-permute-start.8 = (bf16[384,3072]{1,0:T(8,128)(2,1)}, bf16[384,3072]{1,0:T(8,128)(2,1)}, u32[]{:S(2)}, u32[]{:S(2)}) collective-permute-start(bf16[384,3072]{1,0:T(8,128)(2,1)} %collective-permute-done.7.refs_4_), channel_id=1, source_target_pairs={{0,4},{4,0},{8,12},{12,8},{16,20},{20,16},{24,28},{28,24},{1,5},{5... | collective-permute-start | bytes 7077896 | tf_op jit(solution)/shard_map/ppermute | solution.py:326
  95.8 56.9 %collective-permute-start.2 = (bf16[1024,768]{1,0:T(8,128)(2,1)S(1)}, bf16[1024,768]{1,0:T(8,128)(2,1)}, u32[]{:S(2)}, u32[]{:S(2)}) collective-permute-start(bf16[1024,768]{1,0:T(8,128)(2,1)S(1)} %collective-permute-done.refs_1_), channel_id=1, source_target_pairs={{0,1},{1,3},{3,2},{2,0},{4,5},{5,7},{7,6},{6,4},{8,9},{9,11},{11,1... | collective-permute-start | bytes 4718600 | tf_op jit(solution)/shard_map/ppermute | solution.py:322
  99.6 57.4 %collective-permute-start.9 = (bf16[192,3072]{1,0:T(8,128)(2,1)}, bf16[192,3072]{1,0:T(8,128)(2,1)}, u32[]{:S(2)}, u32[]{:S(2)}) collective-permute-start(bf16[192,3072]{1,0:T(8,128)(2,1)} %slice.48), channel_id=1, source_target_pairs={{0,16},{4,20},{8,24},{12,28},{16,0},{20,4},{24,8},{28,12},{1,17},{... | collective-permute-start | bytes 3538952 | tf_op jit(solution)/shard_map/ppermute | solution.py:362
  121.7 41.3 %collective-permute-start.11 = (bf16[192,3072]{1,0:T(8,128)(2,1)}, bf16[192,3072]{1,0:T(8,128)(2,1)}, u32[]{:S(2)}, u32[]{:S(2)}) collective-permute-start(bf16[192,3072]{1,0:T(8,128)(2,1)} %slice.49), channel_id=1, source_target_pairs={{0,8},{4,12},{8,0},{12,4},{16,24},{20,28},{24,16},{28,20},{1,9},{5... | collective-permute-start | bytes 3538952 | tf_op jit(solution)/shard_map/ppermute | solution.py:362
  152.7 38.6 %collective-permute-start.13 = (bf16[1024,768]{1,0:T(8,128)(2,1)}, bf16[1024,768]{1,0:T(8,128)(2,1)}, u32[]{:S(2)}, u32[]{:S(2)}) collective-permute-start(bf16[1024,768]{1,0:T(8,128)(2,1)} %collective-permute-done.2.refs_2_), channel_id=1, source_target_pairs={{0,1},{1,3},{3,2},{2,0},{4,5},{5,7},{7,6},{6,4},{8,9},{9,11},{11,1... | collective-permute-start | bytes 4718600 | tf_op jit(solution)/shard_map/ppermute | solution.py:322
  153.4 67.9 %collective-permute-start.14 = (bf16[1024,768]{1,0:T(8,128)(2,1)}, bf16[1024,768]{1,0:T(8,128)(2,1)S(1)}, u32[]{:S(2)}, u32[]{:S(2)}) collective-permute-start(bf16[1024,768]{1,0:T(8,128)(2,1)} %collective-permute-done.3.refs_2_.refs_12_), channel_id=1, source_target_pairs={{0,1},{1,3},{3,2},{2,0},{4,5},{5,7},{7,6},{6,4},{8,9},{9,11},{11,1... | collective-permute-start | bytes 4718600 | tf_op jit(solution)/shard_map/ppermute | solution.py:322
  252.8 19.9 %collective-permute-start.16 = (bf16[2,1,384,512]{3,2,1,0:T(8,128)(2,1)S(1)}, bf16[2,1,384,512]{3,2,1,0:T(8,128)(2,1)S(1)}, u32[]{:S(2)}, u32[]{:S(2)}) collective-permute-start(bf16[2,1,384,512]{3,2,1,0:T(8,128)(2,1)S(1)} %get-tuple-element.142), channel_id=1, source_target_pairs={{0,8},{4,12},{8,0},{12,4},{16,24},{20,28},{24,16},{28,20},{1,9},{5... | collective-permute-start | bytes 2359304 | tf_op jit(solution)/shard_map/ppermute | solution.py:362
  253.3 19.7 %collective-permute-start.17 = (bf16[1,2,384,512]{3,2,1,0:T(8,128)(2,1)S(1)}, bf16[1,2,384,512]{3,2,1,0:T(8,128)(2,1)S(1)}, u32[]{:S(2)}, u32[]{:S(2)}) collective-permute-start(bf16[1,2,384,512]{3,2,1,0:T(8,128)(2,1)S(1)} %get-tuple-element.143), channel_id=1, source_target_pairs={{0,16},{4,20},{8,24},{12,28},{16,0},{20,4},{24,8},{28,12},{1,17},{... | collective-permute-start | bytes 2359304 | tf_op jit(solution)/shard_map/ppermute | solution.py:362
  275.0 21.4 %collective-permute-start.19 = (bf16[2,1,384,256]{3,2,1,0:T(8,128)(2,1)S(1)}, bf16[2,1,384,256]{3,2,1,0:T(8,128)(2,1)S(1)}, u32[]{:S(2)}, u32[]{:S(2)}) collective-permute-start(bf16[2,1,384,256]{3,2,1,0:T(8,128)(2,1)S(1)} %get-tuple-element.160), channel_id=1, source_target_pairs={{0,8},{4,12},{8,0},{12,4},{16,24},{20,28},{24,16},{28,20},{1,9},{5... | collective-permute-start | bytes 1179656 | tf_op jit(solution)/shard_map/ppermute | solution.py:362
  276.5 19.9 %collective-permute-start.20 = (bf16[1,2,384,256]{3,2,1,0:T(8,128)(2,1)S(1)}, bf16[1,2,384,256]{3,2,1,0:T(8,128)(2,1)S(1)}, u32[]{:S(2)}, u32[]{:S(2)}) collective-permute-start(bf16[1,2,384,256]{3,2,1,0:T(8,128)(2,1)S(1)} %get-tuple-element.161), channel_id=1, source_target_pairs={{0,16},{4,20},{8,24},{12,28},{16,0},{20,4},{24,8},{28,12},{1,17},{... | collective-permute-start | bytes 1179656 | tf_op jit(solution)/shard_map/ppermute | solution.py:362
  277.0 19.4 %collective-permute-start.22 = (bf16[1,1,384,512]{3,2,1,0:T(8,128)(2,1)S(1)}, bf16[1,1,384,512]{3,2,1,0:T(8,128)(2,1)S(1)}, u32[]{:S(2)}, u32[]{:S(2)}) collective-permute-start(bf16[1,1,384,512]{3,2,1,0:T(8,128)(2,1)S(1)} %get-tuple-element.170), channel_id=1, source_target_pairs={{0,16},{4,20},{8,24},{12,28},{16,0},{20,4},{24,8},{28,12},{1,17},{... | collective-permute-start | bytes 1179656 | tf_op jit(solution)/shard_map/ppermute | solution.py:362
  298.2 25.2 %collective-permute-start.24 = (bf16[2,1,384,512]{3,2,1,0:T(8,128)(2,1)S(1)}, bf16[2,1,384,512]{3,2,1,0:T(8,128)(2,1)}, u32[]{:S(2)}, u32[]{:S(2)}) collective-permute-start(bf16[2,1,384,512]{3,2,1,0:T(8,128)(2,1)S(1)} %get-tuple-element.187), channel_id=1, source_target_pairs={{0,8},{4,12},{8,0},{12,4},{16,24},{20,28},{24,16},{28,20},{1,9},{5... | collective-permute-start | bytes 2359304 | tf_op jit(solution)/shard_map/ppermute | solution.py:362
  299.7 23.8 %collective-permute-start.25 = (bf16[1,2,384,512]{3,2,1,0:T(8,128)(2,1)S(1)}, bf16[1,2,384,512]{3,2,1,0:T(8,128)(2,1)S(1)}, u32[]{:S(2)}, u32[]{:S(2)}) collective-permute-start(bf16[1,2,384,512]{3,2,1,0:T(8,128)(2,1)S(1)} %get-tuple-element.188), channel_id=1, source_target_pairs={{0,16},{4,20},{8,24},{12,28},{16,0},{20,4},{24,8},{28,12},{1,17},{... | collective-permute-start | bytes 2359304 | tf_op jit(solution)/shard_map/ppermute | solution.py:362
  300.3 23.2 %collective-permute-start.27 = (bf16[1,1,384,256]{3,2,1,0:T(8,128)(2,1)}, bf16[1,1,384,256]{3,2,1,0:T(8,128)(2,1)S(1)}, u32[]{:S(2)}, u32[]{:S(2)}) collective-permute-start(bf16[1,1,384,256]{3,2,1,0:T(8,128)(2,1)} %add_convert_fusion.7), channel_id=1, source_target_pairs={{0,16},{4,20},{8,24},{12,28},{16,0},{20,4},{24,8},{28,12},{1,17},{... | collective-permute-start | bytes 589832 | tf_op jit(solution)/shard_map/ppermute | solution.py:362
  301.8 21.7 %collective-permute-start.28 = (bf16[1,1,384,256]{3,2,1,0:T(8,128)(2,1)}, bf16[1,1,384,256]{3,2,1,0:T(8,128)(2,1)S(1)}, u32[]{:S(2)}, u32[]{:S(2)}) collective-permute-start(bf16[1,1,384,256]{3,2,1,0:T(8,128)(2,1)} %add_convert_fusion.6), channel_id=1, source_target_pairs={{0,8},{4,12},{8,0},{12,4},{16,24},{20,28},{24,16},{28,20},{1,9},{5... | collective-permute-start | bytes 589832 | tf_op jit(solution)/shard_map/ppermute | solution.py:362
  328.1 20.0 %collective-permute-start.30 = (bf16[1,1,384,512]{3,2,1,0:T(8,128)(2,1)S(1)}, bf16[1,1,384,512]{3,2,1,0:T(8,128)(2,1)S(1)}, u32[]{:S(2)}, u32[]{:S(2)}) collective-permute-start(bf16[1,1,384,512]{3,2,1,0:T(8,128)(2,1)S(1)} %add_convert_fusion), channel_id=1, source_target_pairs={{0,8},{4,12},{8,0},{12,4},{16,24},{20,28},{24,16},{28,20},{1,9},{5... | collective-permute-start | bytes 1179656 | tf_op jit(solution)/shard_map/ppermute | solution.py:362
  (38 other events, 408.4 us)
Sparse Core Ops, SparseCore 0:
  9.2 157.9 all-gather.1

commit v7 on v6

--- a/solution.py
+++ b/solution.py
@@ -215,9 +215,21 @@
     )(at, slots, *arrays, *[p for piece in shards for p in piece])
 
 
-def front_body(shard, probe, begun, bent, other, mixed, away):
+def front_body(shard, probe, begun, bent, source, mixed, away, other, sem):
+    copy = pltpu.make_async_copy(source, other, sem)
+    starting = pl.program_id(0) == 0
+
+    @pl.when(starting)
+    def _():
+        copy.start()
+
     tangent = begun[...] + jnp.dot(shard[...], probe[...], preferred_element_type=f32)
     mixed[...] = (bent[...] * tangent).astype(bf16)
+
+    @pl.when(starting)
+    def _():
+        copy.wait()
+
     away[...] = jnp.dot(other[...], mixed[...], preferred_element_type=f32).astype(bf16)
 
 
@@ -234,12 +246,13 @@
             pl.BlockSpec((None, width, tile), lambda j: (base + j, 0, 0)),
             pl.BlockSpec((None, tok, tile), lambda j: (base + j, 0, 0)),
             pl.BlockSpec((None, tok, tile), lambda j: (base + j, 0, 0)),
-            whole(other.shape),
+            pl.BlockSpec(memory_space=pl.ANY),
         ],
         out_specs=[
             pl.BlockSpec((tok, tile), lambda j: (0, j)),
             pl.BlockSpec((half, tile), lambda j: (0, j)),
         ],
+        scratch_shapes=[pltpu.VMEM(other.shape, bf16), pltpu.SemaphoreType.DMA(())],
         out_shape=[
             jax.ShapeDtypeStruct((tok, wide), bf16),
             jax.ShapeDtypeStruct((half, wide), bf16),
@@ -250,20 +263,42 @@
     )(shard, last, begun, bent, other)
 
 
-def back_body(xs, ys, rows, steps, me, mine, mixed, came, keep_x, keep_y, to_x, to_y):
+def back_body(xs, ys, rows, steps, me, source, mixed, came, *refs):
+    keep_x, keep_y, to_x, to_y, mine, sems = refs
     x, y = me[0], me[1]
+    order = [(k, lax.rem(x + i, xs)) for k in range(ys) for i in [*range(1, xs), 0]]
+
+    def part(at_y, at_x):
+        return pl.ds(pl.multiple_of((at_y * xs + at_x) * rows, rows), rows)
+
+    copies = [
+        pltpu.make_async_copy(source.at[part(*at)], mine.at[part(*at)], sems.at[n])
+        for n, at in enumerate(order)
+    ]
+    starting = pl.program_id(0) == 0
+
+    @pl.when(starting)
+    def _():
+        for c in copies:
+            c.start()
 
     def block(at_y, at_x):
-        part = pl.ds(pl.multiple_of((at_y * xs + at_x) * rows, rows), rows)
-        total = jnp.dot(mine[part, :], mixed[...], preferred_element_type=f32)
-        return total + came[part, :].astype(f32)
+        total = jnp.dot(mine[part(at_y, at_x), :], mixed[...], preferred_element_type=f32)
+        return total + came[part(at_y, at_x), :].astype(f32)
 
     @pl.when(pl.program_id(0) < steps)
     def _():
-        for k in range(ys):
-            for i in range(1, xs):
-                to_x[k, i - 1] = block(k, lax.rem(x + i, xs)).astype(bf16)
-            keep_x[k, 0] = block(k, x)
+        for n, at in enumerate(order):
+
+            @pl.when(starting)
+            def _():
+                copies[n].wait()
+
+            k, i = n // xs, n % xs
+            if i < xs - 1:
+                to_x[k, i] = block(*at).astype(bf16)
+            else:
+                keep_x[k, 0] = block(*at)
 
     @pl.when(pl.program_id(0) >= steps)
     def _():
@@ -293,13 +328,17 @@
             num_scalar_prefetch=1,
             grid=(2 * steps,),
             in_specs=[
-                whole(mine.shape),
+                pl.BlockSpec(memory_space=pl.ANY),
                 pl.BlockSpec((tok, tile), lambda j, me: (0, j)),
                 pl.BlockSpec((mine.shape[0], tile), lambda j, me: (0, j)),
             ],
             out_specs=[
                 pl.BlockSpec(shape + (tile,), where)
                 for shape, where in zip(shapes, (left, right, left, right))
+            ],
+            scratch_shapes=[
+                pltpu.VMEM(mine.shape, bf16),
+                pltpu.SemaphoreType.DMA((xs * ys,)),
             ],
         ),
         out_shape=[
@@ -460,10 +499,6 @@
             block_sum(keeps[j][1], first[1], 1, lax.rem(x + i, xs)).astype(bf16)
             for i in range(1, xs)
         ]
-        if j + 1 < count:
-            sends_y, sends_x, to_x, to_y = lax.optimization_barrier(
-                (sends_y, sends_x, to_x, to_y)
-            )
         second = (
             [over(p, y_way, k + 1) for k, p in enumerate(sends_y)],
             [over(p, x_way, i + 1) for i, p in enumerate(sends_x)],

time: 358 us -> 361 us (level)
  Pallas kernels: 125 us -> 131 us
  waiting for transfers between devices: 154 us -> 148 us
    ppermute x20, waiting for transfers between devices: 35.1 us -> 28.8 us  [over(): return lax.ppermute(block, 'dp', shift(way[0], way[1], dp, by))]
    pallas_call x4, Pallas kernels: 29.3 us -> 34.2 us  [back_of(): pl.pallas_call(functools.partial(back_body, xs, ys, rows, steps), grid_sp...]
    unnamed x52 -> x54, local copies, waits for them, and re-layouts: 8.31 us -> 8.57 us
  transfers between devices with their start and end apart: 36 -> 36, of which waited for: 15 -> 15; matrix products, arithmetic and copies ran while one was open for 6% -> 6% of each run, Pallas kernels for 31% -> 33%
where the time goes in v7:
time: 361 us; the launch traced here: 360 us
  waiting for transfers between devices  148 us (41%)
  Pallas kernels  131 us (36%)
  starting transfers between devices  35 us (10%)
  other arithmetic  17.7 us (5%)
  local copies, waits for them, and re-layouts  14.9 us (4%)
  between operations  13.8 us (4%)
    ppermute x6, waiting for transfers between devices, ring_step(): return lax.ppermute(block, 'tensor', pairs)  116 us
    pallas_call x4, Pallas kernels, front_of(): pl.pallas_call(front_body, grid=(wide // tile,), in_specs=[whole((tok, wi...  37.5 us
    pallas_call x4, Pallas kernels, back_of(): pl.pallas_call(functools.partial(back_body, xs, ys, rows, steps), grid_sp...  34.2 us
    pallas_call x1, Pallas kernels, bent_of(): pl.pallas_call(functools.partial(bent_body, count, parts, width), grid_sp...  29.2 us
    ppermute x20, waiting for transfers between devices, over(): return lax.ppermute(block, 'dp', shift(way[0], way[1], dp, by))  28.8 us
    ppermute x20, starting transfers between devices, over(): return lax.ppermute(block, 'dp', shift(way[0], way[1], dp, by))  23.8 us
    pallas_call x1, Pallas kernels, partial_tangent(): pl.pallas_call(functools.partial(partial_body, count, parts, width, spots...  23 us
    ppermute x6, starting transfers between devices, ring_step(): return lax.ppermute(block, 'tensor', pairs)  10.6 us
  transfers between devices with their start and end apart: 36, of which 15 were waited for; matrix products, arithmetic and copies ran while one was open for 6% of the time, Pallas kernels for 33%

profile of v7, /device:TPU:0, one launch (start us, length us, event | category | flops | bytes accessed | tf_op | source)
XLA Modules:
  0.0 360.2 jit_solution(3769848611594196452)
XLA Ops:
  7.3 3.0 collective-permute-start.5
  13.4 2.6 collective-permute-start.1
  16.0 34.3 %collective-permute-done.refs_1_ = bf16[1024,768]{1,0:T(8,128)(2,1)S(1)} collective-permute-done((bf16[1024,768]{1,0:T(8,128)(2,1)}, bf16[1024,768]{1,0:T(8,128)(2,1)S(1)}, u32[]{:S(2)}, u32[]{:S(2)}) %collective-permute-start) | collective-permute-done | bytes 1572896 | tf_op jit(solution)/shard_map/ppermute | solution.py:361
  50.2 31.9 %collective-permute-done.1.refs_1_.refs_11_ = bf16[1024,768]{1,0:T(8,128)(2,1)S(1)} collective-permute-done((bf16[1024,768]{1,0:T(8,128)(2,1)S(1)}, bf16[1024,768]{1,0:T(8,128)(2,1)S(1)}, u32[]{:S(2)}, u32[]{:S(2)}) %collective-permute-start.1) | collective-permute-done | bytes 1572896 | tf_op jit(solution)/shard_map/ppermute | solution.py:361
  84.1 8.8 %collective-permute-done.5.refs_2_ = bf16[384,3072]{1,0:T(8,128)(2,1)} collective-permute-done((bf16[384,3072]{1,0:T(8,128)(2,1)}, bf16[384,3072]{1,0:T(8,128)(2,1)}, u32[]{:S(2)}, u32[]{:S(2)}) %collective-permute-start.5) | collective-permute-done | bytes 2359328 | tf_op jit(solution)/shard_map/ppermute | solution.py:401
  93.0 2.8 collective-permute-done.7.refs_4_
  99.6 2.5 collective-permute-start.9
  104.5 17.2 %collective-permute-done.3.refs_2_.refs_12_ = bf16[1024,768]{1,0:T(8,128)(2,1)} collective-permute-done((bf16[1024,768]{1,0:T(8,128)(2,1)S(1)}, bf16[1024,768]{1,0:T(8,128)(2,1)}, u32[]{:S(2)}, u32[]{:S(2)}) %collective-permute-start.3) | collective-permute-done | bytes 1572896 | tf_op jit(solution)/shard_map/ppermute | solution.py:361
  123.0 29.7 %collective-permute-done.2.refs_2_ = bf16[1024,768]{1,0:T(8,128)(2,1)} collective-permute-done((bf16[1024,768]{1,0:T(8,128)(2,1)S(1)}, bf16[1024,768]{1,0:T(8,128)(2,1)}, u32[]{:S(2)}, u32[]{:S(2)}) %collective-permute-start.2) | collective-permute-done | bytes 1572896 | tf_op jit(solution)/shard_map/ppermute | solution.py:361
  153.4 3.5 collective-permute-start.14
  156.9 4.9 %split_cores.2 = (bf16[1536,1024]{1,0:T(8,128)(2,1)}, bf16[1536,1024]{1,0:T(8,128)(2,1)}) custom-call(s32[1]{0:T(128)} %bitcast.2.core, s32[3]{0:T(128)S(1)} %bitcast.65, bf16[1024,768]{1,0:T(8,128)(2,1)S(1)} %copy-done.2, bf16[1024,768]{1,0:T(8,128)(2,1)} %copy-done.6, bf16[1024,768]{1,0:T(8,128)(2,1)} %collective-permute-done.3.refs_2_.refs_12_), custom_call_target="tpu_custom_call" | custom-call | bytes 1024 | tf_op jit(solution)/shard_map/split_cores/pallas_call | solution.py:57
  166.1 23.0 %partial_tangent.1 = (f32[6,1024,512]{2,1,0:T(8,128)}, bf16[6,768,512]{2,1,0:T(8,128)(2,1)}) custom-call(s32[4]{0:T(128)S(1)} %fusion.16.at, s32[10]{0:T(128)S(1)} %stack.64.slots, bf16[384,3072]{1,0:T(8,128)(2,1)} %refs_0_.4, bf16[384,3072]{1,0:T(8,128)(2,1)} %copy-done.8, bf16[384,3072]{1,0:T(8,128)(2,1)} %collective-permute-done.5.refs_2_, ...), custom_call_target="tpu_custom_call" | custom-call | bytes 1024 | tf_op jit(solution)/shard_map/partial_tangent/pallas_call | solution.py:190
  191.3 29.2 %bent.1 = f32[6,1024,512]{2,1,0:T(8,128)} custom-call(s32[4]{0:T(128)S(1)} %fusion.16.at, f32[1024,1]{1,0:T(8,128)S(1)} %copy.10.scale, s32[1024,3072]{1,0:T(8,128)} %codes.1, bf16[3072,3072]{1,0:T(8,128)(2,1)} %all-gather.2.cloned.1.call-done.down, bf16[1024,768]{1,0:T(8,128)(2,1)} %refs_0_.5, bf16[1024,768]{1,0:T(8,128)(2,1)} %copy-done.9, ...), custom_call_target="tpu_custom_call" | custom-call | bytes 1024 | tf_op jit(solution)/shard_map/bent/pallas_call | solution.py:121
  223.3 10.9 %front.4 = (bf16[1024,1024]{1,0:T(8,128)(2,1)}, bf16[1536,1024]{1,0:T(8,128)(2,1)}) custom-call(bf16[1024,768]{1,0:T(8,128)(2,1)S(1)} %collective-permute-done.14.refs_0_.shard, bf16[6,768,512]{2,1,0:T(8,128)(2,1)} %get-tuple-element.148.probe, f32[6,1024,512]{2,1,0:T(8,128)} %get-tuple-element.116.begun, f32[6,1024,512]{2,1,0:T(8,128)} %bent.1, ...), custom_call_target="tpu_custom_call" | custom-call | bytes 1024 | tf_op jit(solution)/shard_map/front/pallas_call | solution.py:241
  234.3 7.9 %front.5 = (bf16[1024,512]{1,0:T(8,128)(2,1)S(1)}, bf16[1536,512]{1,0:T(8,128)(2,1)}) custom-call(bf16[1024,768]{1,0:T(8,128)(2,1)} %copy-done, bf16[6,768,512]{2,1,0:T(8,128)(2,1)} %get-tuple-element.148.probe, f32[6,1024,512]{2,1,0:T(8,128)} %get-tuple-element.116.begun, f32[6,1024,512]{2,1,0:T(8,128)} %bent.1, bf16[1536,1024]{1,0:T(8,128)(2,1)} %get-tuple-element.118.source), custom_call_target="tpu_custom_call" | custom-call | bytes 1024 | tf_op jit(solution)/shard_map/front/pallas_call | solution.py:241
  244.8 9.6 %back.4 = (f32[2,1,384,512]{3,2,1,0:T(8,128)}, f32[1,2,384,512]{3,2,1,0:T(8,128)}, bf16[2,1,384,512]{3,2,1,0:T(8,128)(2,1)S(1)}, bf16[1,2,384,512]{3,2,1,0:T(8,128)(2,1)S(1)}) custom-call(s32[2]{0:T(128)S(1)} %pad_add_fusion.me, bf16[1536,1024]{1,0:T(8,128)(2,1)} %get-tuple-element.114.source, bf16[1024,1024]{1,0:T(8,128)(2,1)} %get-tuple-element.124.mixed, ...), custom_call_target="tpu_custom_call" | custom-call | bytes 1024 | tf_op jit(solution)/shard_map/back/pallas_call | solution.py:325
  257.3 7.5 %back.5 = (f32[2,1,384,256]{3,2,1,0:T(8,128)S(1)}, f32[1,2,384,256]{3,2,1,0:T(8,128)}, bf16[2,1,384,256]{3,2,1,0:T(8,128)(2,1)S(1)}, bf16[1,2,384,256]{3,2,1,0:T(8,128)(2,1)S(1)}) custom-call(s32[2]{0:T(128)S(1)} %pad_add_fusion.me, bf16[1536,1024]{1,0:T(8,128)(2,1)} %get-tuple-element.114.source, bf16[1024,512]{1,0:T(8,128)(2,1)} %copy-done.4, ...), custom_call_target="tpu_custom_call" | custom-call | bytes 1024 | tf_op jit(solution)/shard_map/back/pallas_call | solution.py:325
  264.8 10.9 %front.6 = (bf16[1024,1024]{1,0:T(8,128)(2,1)}, bf16[1536,1024]{1,0:T(8,128)(2,1)}) custom-call(bf16[1024,768]{1,0:T(8,128)(2,1)S(1)} %copy-done.1, bf16[6,768,512]{2,1,0:T(8,128)(2,1)} %get-tuple-element.148.probe, f32[6,1024,512]{2,1,0:T(8,128)} %get-tuple-element.116.begun, f32[6,1024,512]{2,1,0:T(8,128)} %bent.1, ...), custom_call_target="tpu_custom_call" | custom-call | bytes 1024 | tf_op jit(solution)/shard_map/front/pallas_call | solution.py:241
  283.5 9.6 %back.6 = (f32[2,1,384,512]{3,2,1,0:T(8,128)}, f32[1,2,384,512]{3,2,1,0:T(8,128)}, bf16[2,1,384,512]{3,2,1,0:T(8,128)(2,1)S(1)}, bf16[1,2,384,512]{3,2,1,0:T(8,128)(2,1)S(1)}) custom-call(s32[2]{0:T(128)S(1)} %pad_add_fusion.me, bf16[1536,1024]{1,0:T(8,128)(2,1)} %get-tuple-element.114.source, bf16[1024,1024]{1,0:T(8,128)(2,1)} %get-tuple-element.144.mixed, ...), custom_call_target="tpu_custom_call" | custom-call | bytes 1024 | tf_op jit(solution)/shard_map/back/pallas_call | solution.py:325
  293.0 7.8 %front.7 = (bf16[1024,512]{1,0:T(8,128)(2,1)S(1)}, bf16[1536,512]{1,0:T(8,128)(2,1)}) custom-call(bf16[1024,768]{1,0:T(8,128)(2,1)} %copy-done, bf16[6,768,512]{2,1,0:T(8,128)(2,1)} %get-tuple-element.148.probe, f32[6,1024,512]{2,1,0:T(8,128)} %get-tuple-element.116.begun, f32[6,1024,512]{2,1,0:T(8,128)} %bent.1, bf16[1536,1024]{1,0:T(8,128)(2,1)} %get-tuple-element.118.source), custom_call_target="tpu_custom_call" | custom-call | bytes 1024 | tf_op jit(solution)/shard_map/front/pallas_call | solution.py:241
  313.6 7.6 %back.7 = (f32[2,1,384,256]{3,2,1,0:T(8,128)S(1)}, f32[1,2,384,256]{3,2,1,0:T(8,128)}, bf16[2,1,384,256]{3,2,1,0:T(8,128)(2,1)S(1)}, bf16[1,2,384,256]{3,2,1,0:T(8,128)(2,1)S(1)}) custom-call(s32[2]{0:T(128)S(1)} %pad_add_fusion.me, bf16[1536,1024]{1,0:T(8,128)(2,1)} %get-tuple-element.114.source, bf16[1024,512]{1,0:T(8,128)(2,1)} %copy-done.3, ...), custom_call_target="tpu_custom_call" | custom-call | bytes 1024 | tf_op jit(solution)/shard_map/back/pallas_call | solution.py:325
  321.2 4.9 %collective-permute-done.28 = bf16[1,1,384,256]{3,2,1,0:T(8,128)(2,1)S(1)} collective-permute-done((bf16[1,1,384,256]{3,2,1,0:T(8,128)(2,1)S(1)}, bf16[1,1,384,256]{3,2,1,0:T(8,128)(2,1)S(1)}, u32[]{:S(2)}, u32[]{:S(2)}) %collective-permute-start.28) | collective-permute-done | bytes 196640 | tf_op jit(solution)/shard_map/ppermute | solution.py:401
  335.2 3.9 %collective-permute-done.33 = bf16[1,2,384,256]{3,2,1,0:T(8,128)(2,1)S(1)} collective-permute-done((bf16[1,2,384,256]{3,2,1,0:T(8,128)(2,1)S(1)}, bf16[1,2,384,256]{3,2,1,0:T(8,128)(2,1)S(1)}, u32[]{:S(2)}, u32[]{:S(2)}) %collective-permute-start.33) | collective-permute-done | bytes 393248 | tf_op jit(solution)/shard_map/ppermute | solution.py:401
  341.3 6.1 %collective-permute-done.29 = bf16[1,1,384,512]{3,2,1,0:T(8,128)(2,1)S(1)} collective-permute-done((bf16[1,1,384,512]{3,2,1,0:T(8,128)(2,1)S(1)}, bf16[1,1,384,512]{3,2,1,0:T(8,128)(2,1)S(1)}, u32[]{:S(2)}, u32[]{:S(2)}) %collective-permute-start.29) | collective-permute-done | bytes 393248 | tf_op jit(solution)/shard_map/ppermute | solution.py:401
  (138 shorter events, 66.4 us)
Async XLA Ops:
  6.5 184.8 %all-gather.2.cloned.1.call-start = ((), (), s32[]{:S(2)}) async-start(), calls=%async_computation | async-start | bytes 21233664 | tf_op jit(solution)/shard_map/all_gather | solution.py:429
  7.3 85.7 %collective-permute-start.5 = (bf16[384,3072]{1,0:T(8,128)(2,1)}, bf16[384,3072]{1,0:T(8,128)(2,1)}, u32[]{:S(2)}, u32[]{:S(2)}) collective-permute-start(bf16[384,3072]{1,0:T(8,128)(2,1)} %refs_0_.4), channel_id=1, source_target_pairs={{0,8},{4,12},{8,0},{12,4},{16,24},{20,28},{24,16},{28,20},{1,9},{5... | collective-permute-start | bytes 7077896 | tf_op jit(solution)/shard_map/ppermute | solution.py:401
  10.3 85.5 %collective-permute-start.7 = (bf16[384,3072]{1,0:T(8,128)(2,1)}, bf16[384,3072]{1,0:T(8,128)(2,1)}, u32[]{:S(2)}, u32[]{:S(2)}) collective-permute-start(bf16[384,3072]{1,0:T(8,128)(2,1)} %refs_0_.4), channel_id=1, source_target_pairs={{0,16},{4,20},{8,24},{12,28},{16,0},{20,4},{24,8},{28,12},{1,17},{... | collective-permute-start | bytes 7077896 | tf_op jit(solution)/shard_map/ppermute | solution.py:401
  11.8 38.4 %collective-permute-start = (bf16[1024,768]{1,0:T(8,128)(2,1)}, bf16[1024,768]{1,0:T(8,128)(2,1)S(1)}, u32[]{:S(2)}, u32[]{:S(2)}) collective-permute-start(bf16[1024,768]{1,0:T(8,128)(2,1)} %refs_0_.5), channel_id=1, source_target_pairs={{0,1},{1,3},{3,2},{2,0},{4,5},{5,7},{7,6},{6,4},{8,9},{9,11},{11,1... | collective-permute-start | bytes 4718600 | tf_op jit(solution)/shard_map/ppermute | solution.py:361
  13.4 68.8 %collective-permute-start.1 = (bf16[1024,768]{1,0:T(8,128)(2,1)S(1)}, bf16[1024,768]{1,0:T(8,128)(2,1)S(1)}, u32[]{:S(2)}, u32[]{:S(2)}) collective-permute-start(bf16[1024,768]{1,0:T(8,128)(2,1)S(1)} %copy-done.2), channel_id=1, source_target_pairs={{0,1},{1,3},{3,2},{2,0},{4,5},{5,7},{7,6},{6,4},{8,9},{9,11},{11,1... | collective-permute-start | bytes 4718600 | tf_op jit(solution)/shard_map/ppermute | solution.py:361
  16.0 83.6 %collective-permute-start.4 = (bf16[384,3072]{1,0:T(8,128)(2,1)}, bf16[384,3072]{1,0:T(8,128)(2,1)S(1)}, u32[]{:S(2)}, u32[]{:S(2)}) collective-permute-start(bf16[384,3072]{1,0:T(8,128)(2,1)} %refs_0_.4), channel_id=1, source_target_pairs={{0,4},{4,0},{8,12},{12,8},{16,20},{20,16},{24,28},{28,24},{1,5},{5... | collective-permute-start | bytes 7077896 | tf_op jit(solution)/shard_map/ppermute | solution.py:365
  83.3 38.3 %collective-permute-start.3 = (bf16[1024,768]{1,0:T(8,128)(2,1)S(1)}, bf16[1024,768]{1,0:T(8,128)(2,1)}, u32[]{:S(2)}, u32[]{:S(2)}) collective-permute-start(bf16[1024,768]{1,0:T(8,128)(2,1)S(1)} %collective-permute-done.1.refs_1_.refs_11_), channel_id=1, source_target_pairs={{0,1},{1,3},{3,2},{2,0},{4,5},{5,7},{7,6},{6,4},{8,9},{9,11},{11,1... | collective-permute-start | bytes 4718600 | tf_op jit(solution)/shard_map/ppermute | solution.py:361
  93.0 59.7 %collective-permute-start.6 = (bf16[384,3072]{1,0:T(8,128)(2,1)}, bf16[384,3072]{1,0:T(8,128)(2,1)}, u32[]{:S(2)}, u32[]{:S(2)}) collective-permute-start(bf16[384,3072]{1,0:T(8,128)(2,1)} %collective-permute-done.5.refs_2_), channel_id=1, source_target_pairs={{0,4},{4,0},{8,12},{12,8},{16,20},{20,16},{24,28},{28,24},{1,5},{5... | collective-permute-start | bytes 7077896 | tf_op jit(solution)/shard_map/ppermute | solution.py:365
  95.8 56.9 %collective-permute-start.8 = (bf16[384,3072]{1,0:T(8,128)(2,1)}, bf16[384,3072]{1,0:T(8,128)(2,1)}, u32[]{:S(2)}, u32[]{:S(2)}) collective-permute-start(bf16[384,3072]{1,0:T(8,128)(2,1)} %collective-permute-done.7.refs_4_), channel_id=1, source_target_pairs={{0,4},{4,0},{8,12},{12,8},{16,20},{20,16},{24,28},{28,24},{1,5},{5... | collective-permute-start | bytes 7077896 | tf_op jit(solution)/shard_map/ppermute | solution.py:365
  95.8 56.9 %collective-permute-start.2 = (bf16[1024,768]{1,0:T(8,128)(2,1)S(1)}, bf16[1024,768]{1,0:T(8,128)(2,1)}, u32[]{:S(2)}, u32[]{:S(2)}) collective-permute-start(bf16[1024,768]{1,0:T(8,128)(2,1)S(1)} %collective-permute-done.refs_1_), channel_id=1, source_target_pairs={{0,1},{1,3},{3,2},{2,0},{4,5},{5,7},{7,6},{6,4},{8,9},{9,11},{11,1... | collective-permute-start | bytes 4718600 | tf_op jit(solution)/shard_map/ppermute | solution.py:361
  99.6 57.4 %collective-permute-start.9 = (bf16[192,3072]{1,0:T(8,128)(2,1)}, bf16[192,3072]{1,0:T(8,128)(2,1)}, u32[]{:S(2)}, u32[]{:S(2)}) collective-permute-start(bf16[192,3072]{1,0:T(8,128)(2,1)} %slice.48), channel_id=1, source_target_pairs={{0,16},{4,20},{8,24},{12,28},{16,0},{20,4},{24,8},{28,12},{1,17},{... | collective-permute-start | bytes 3538952 | tf_op jit(solution)/shard_map/ppermute | solution.py:401
  121.7 41.3 %collective-permute-start.11 = (bf16[192,3072]{1,0:T(8,128)(2,1)}, bf16[192,3072]{1,0:T(8,128)(2,1)}, u32[]{:S(2)}, u32[]{:S(2)}) collective-permute-start(bf16[192,3072]{1,0:T(8,128)(2,1)} %slice.49), channel_id=1, source_target_pairs={{0,8},{4,12},{8,0},{12,4},{16,24},{20,28},{24,16},{28,20},{1,9},{5... | collective-permute-start | bytes 3538952 | tf_op jit(solution)/shard_map/ppermute | solution.py:401
  152.7 38.6 %collective-permute-start.13 = (bf16[1024,768]{1,0:T(8,128)(2,1)}, bf16[1024,768]{1,0:T(8,128)(2,1)}, u32[]{:S(2)}, u32[]{:S(2)}) collective-permute-start(bf16[1024,768]{1,0:T(8,128)(2,1)} %collective-permute-done.2.refs_2_), channel_id=1, source_target_pairs={{0,1},{1,3},{3,2},{2,0},{4,5},{5,7},{7,6},{6,4},{8,9},{9,11},{11,1... | collective-permute-start | bytes 4718600 | tf_op jit(solution)/shard_map/ppermute | solution.py:361
  153.4 67.9 %collective-permute-start.14 = (bf16[1024,768]{1,0:T(8,128)(2,1)}, bf16[1024,768]{1,0:T(8,128)(2,1)S(1)}, u32[]{:S(2)}, u32[]{:S(2)}) collective-permute-start(bf16[1024,768]{1,0:T(8,128)(2,1)} %collective-permute-done.3.refs_2_.refs_12_), channel_id=1, source_target_pairs={{0,1},{1,3},{3,2},{2,0},{4,5},{5,7},{7,6},{6,4},{8,9},{9,11},{11,1... | collective-permute-start | bytes 4718600 | tf_op jit(solution)/shard_map/ppermute | solution.py:361
  254.5 21.2 %collective-permute-start.16 = (bf16[2,1,384,512]{3,2,1,0:T(8,128)(2,1)S(1)}, bf16[2,1,384,512]{3,2,1,0:T(8,128)(2,1)S(1)}, u32[]{:S(2)}, u32[]{:S(2)}) collective-permute-start(bf16[2,1,384,512]{3,2,1,0:T(8,128)(2,1)S(1)} %get-tuple-element.129), channel_id=1, source_target_pairs={{0,8},{4,12},{8,0},{12,4},{16,24},{20,28},{24,16},{28,20},{1,9},{5... | collective-permute-start | bytes 2359304 | tf_op jit(solution)/shard_map/ppermute | solution.py:401
  255.1 20.7 %collective-permute-start.17 = (bf16[1,2,384,512]{3,2,1,0:T(8,128)(2,1)S(1)}, bf16[1,2,384,512]{3,2,1,0:T(8,128)(2,1)S(1)}, u32[]{:S(2)}, u32[]{:S(2)}) collective-permute-start(bf16[1,2,384,512]{3,2,1,0:T(8,128)(2,1)S(1)} %get-tuple-element.130), channel_id=1, source_target_pairs={{0,16},{4,20},{8,24},{12,28},{16,0},{20,4},{24,8},{28,12},{1,17},{... | collective-permute-start | bytes 2359304 | tf_op jit(solution)/shard_map/ppermute | solution.py:401
  278.0 23.8 %collective-permute-start.23 = (bf16[1,1,384,512]{3,2,1,0:T(8,128)(2,1)S(1)}, bf16[1,1,384,512]{3,2,1,0:T(8,128)(2,1)S(1)}, u32[]{:S(2)}, u32[]{:S(2)}) collective-permute-start(bf16[1,1,384,512]{3,2,1,0:T(8,128)(2,1)S(1)} %add_convert_fusion.2), channel_id=1, source_target_pairs={{0,8},{4,12},{8,0},{12,4},{16,24},{20,28},{24,16},{28,20},{1,9},{5... | collective-permute-start | bytes 1179656 | tf_op jit(solution)/shard_map/ppermute | solution.py:401
  280.3 21.6 %collective-permute-start.22 = (bf16[1,1,384,512]{3,2,1,0:T(8,128)(2,1)S(1)}, bf16[1,1,384,512]{3,2,1,0:T(8,128)(2,1)S(1)}, u32[]{:S(2)}, u32[]{:S(2)}) collective-permute-start(bf16[1,1,384,512]{3,2,1,0:T(8,128)(2,1)S(1)} %add_convert_fusion.3), channel_id=1, source_target_pairs={{0,16},{4,20},{8,24},{12,28},{16,0},{20,4},{24,8},{28,12},{1,17},{... | collective-permute-start | bytes 1179656 | tf_op jit(solution)/shard_map/ppermute | solution.py:401
  281.9 20.0 %collective-permute-start.19 = (bf16[2,1,384,256]{3,2,1,0:T(8,128)(2,1)S(1)}, bf16[2,1,384,256]{3,2,1,0:T(8,128)(2,1)S(1)}, u32[]{:S(2)}, u32[]{:S(2)}) collective-permute-start(bf16[2,1,384,256]{3,2,1,0:T(8,128)(2,1)S(1)} %get-tuple-element.142), channel_id=1, source_target_pairs={{0,8},{4,12},{8,0},{12,4},{16,24},{20,28},{24,16},{28,20},{1,9},{5... | collective-permute-start | bytes 1179656 | tf_op jit(solution)/shard_map/ppermute | solution.py:401
  282.4 19.5 %collective-permute-start.20 = (bf16[1,2,384,256]{3,2,1,0:T(8,128)(2,1)S(1)}, bf16[1,2,384,256]{3,2,1,0:T(8,128)(2,1)S(1)}, u32[]{:S(2)}, u32[]{:S(2)}) collective-permute-start(bf16[1,2,384,256]{3,2,1,0:T(8,128)(2,1)S(1)} %get-tuple-element.143), channel_id=1, source_target_pairs={{0,16},{4,20},{8,24},{12,28},{16,0},{20,4},{24,8},{28,12},{1,17},{... | collective-permute-start | bytes 1179656 | tf_op jit(solution)/shard_map/ppermute | solution.py:401
  302.0 24.9 %collective-permute-start.24 = (bf16[2,1,384,512]{3,2,1,0:T(8,128)(2,1)S(1)}, bf16[2,1,384,512]{3,2,1,0:T(8,128)(2,1)}, u32[]{:S(2)}, u32[]{:S(2)}) collective-permute-start(bf16[2,1,384,512]{3,2,1,0:T(8,128)(2,1)S(1)} %get-tuple-element.165), channel_id=1, source_target_pairs={{0,8},{4,12},{8,0},{12,4},{16,24},{20,28},{24,16},{28,20},{1,9},{5... | collective-permute-start | bytes 2359304 | tf_op jit(solution)/shard_map/ppermute | solution.py:401
  303.0 23.9 %collective-permute-start.25 = (bf16[1,2,384,512]{3,2,1,0:T(8,128)(2,1)S(1)}, bf16[1,2,384,512]{3,2,1,0:T(8,128)(2,1)}, u32[]{:S(2)}, u32[]{:S(2)}) collective-permute-start(bf16[1,2,384,512]{3,2,1,0:T(8,128)(2,1)S(1)} %get-tuple-element.166), channel_id=1, source_target_pairs={{0,16},{4,20},{8,24},{12,28},{16,0},{20,4},{24,8},{28,12},{1,17},{... | collective-permute-start | bytes 2359304 | tf_op jit(solution)/shard_map/ppermute | solution.py:401
  305.8 20.3 %collective-permute-start.28 = (bf16[1,1,384,256]{3,2,1,0:T(8,128)(2,1)S(1)}, bf16[1,1,384,256]{3,2,1,0:T(8,128)(2,1)S(1)}, u32[]{:S(2)}, u32[]{:S(2)}) collective-permute-start(bf16[1,1,384,256]{3,2,1,0:T(8,128)(2,1)S(1)} %add_convert_fusion.6), channel_id=1, source_target_pairs={{0,8},{4,12},{8,0},{12,4},{16,24},{20,28},{24,16},{28,20},{1,9},{5... | collective-permute-start | bytes 589832 | tf_op jit(solution)/shard_map/ppermute | solution.py:401
  307.6 19.3 %collective-permute-start.27 = (bf16[1,1,384,256]{3,2,1,0:T(8,128)(2,1)S(1)}, bf16[1,1,384,256]{3,2,1,0:T(8,128)(2,1)S(1)}, u32[]{:S(2)}, u32[]{:S(2)}) collective-permute-start(bf16[1,1,384,256]{3,2,1,0:T(8,128)(2,1)S(1)} %add_convert_fusion.7), channel_id=1, source_target_pairs={{0,16},{4,20},{8,24},{12,28},{16,0},{20,4},{24,8},{28,12},{1,17},{... | collective-permute-start | bytes 589832 | tf_op jit(solution)/shard_map/ppermute | solution.py:401
  (39 other events, 394.7 us)
Sparse Core Ops, SparseCore 0:
  9.2 157.9 all-gather.1

commit v8 on v6

--- a/solution.py
+++ b/solution.py
@@ -87,14 +87,39 @@
     ]
 
 
+def chunk_specs(shape, tile, edges):
+    def spec(lo, hi):
+        def where(j, *_):
+            return (jnp.clip(j - lo, 0, hi - lo - 1), 0, 0)
+
+        return pl.BlockSpec((None,) + shape + (tile,), where)
+
+    return [spec(lo // tile, hi // tile) for lo, hi in zip(edges, edges[1:])]
+
+
+def chunk_shapes(shape, tile, edges, kind):
+    return [
+        jax.ShapeDtypeStruct(((hi - lo) // tile,) + shape + (tile,), kind)
+        for lo, hi in zip(edges, edges[1:])
+    ]
+
+
+def chunk_store(step, tile, edges, outs, rows, value):
+    for out, lo, hi in zip(outs, edges, edges[1:]):
+
+        @pl.when((step >= lo // tile) & (step < hi // tile))
+        def _():
+            out[rows, :] = value
+
+
 def whole(shape):
     return pl.BlockSpec(
         shape, lambda *_: (0,) * len(shape), pipeline_mode=pl.Buffered(buffer_count=1)
     )
 
 
-def bent_body(count, parts, width, at, scale, codes, down, *refs):
-    shards, out = refs[: count * parts], refs[count * parts]
+def bent_body(count, parts, width, tile, edges, at, scale, codes, down, *refs):
+    shards, outs = refs[: count * parts], refs[count * parts :]
     for h in range(parts):
         tall = shards[h].shape[0]
         total = None
@@ -110,16 +135,17 @@
         rows = pl.ds(h * tall, tall)
         active = codes[rows, :].astype(f32) * scale[rows, :]
         square = active * active
-        out[rows, :] = total * (jnp.exp(-0.5 * square) * inv_root * (2.0 - square))
-
-
-def bent_of(shards, at, scale, codes, down_full, tile):
+        value = total * (jnp.exp(-0.5 * square) * inv_root * (2.0 - square))
+        chunk_store(pl.program_id(0), tile, edges, outs, rows, value)
+
+
+def bent_of(shards, at, scale, codes, down_full, tile, edges):
     count, parts = len(shards), len(shards[0])
     tall, width = shards[0][0].shape
     tok = tall * parts
     wide, feats = down_full.shape
     return pl.pallas_call(
-        functools.partial(bent_body, count, parts, width),
+        functools.partial(bent_body, count, parts, width, tile, edges),
         grid_spec=pltpu.PrefetchScalarGridSpec(
             num_scalar_prefetch=1,
             grid=(wide // tile,),
@@ -129,19 +155,19 @@
                 pl.BlockSpec((tile, feats), lambda j, at: (j, 0)),
             ]
             + [whole((tall, width))] * (count * parts),
-            out_specs=pl.BlockSpec((None, tok, tile), lambda j, at: (j, 0, 0)),
+            out_specs=chunk_specs((tok,), tile, edges),
         ),
-        out_shape=jax.ShapeDtypeStruct((wide // tile, tok, tile), f32),
+        out_shape=chunk_shapes((tok,), tile, edges, f32),
         compiler_params=params(52),
         cost_estimate=light,
         name="bent",
     )(at, scale, codes, down_full, *[p for piece in shards for p in piece])
 
 
-def partial_body(count, parts, width, spots, plan, arrays, tile, at, slots, *refs):
+def partial_body(count, parts, width, spots, plan, arrays, tile, edges, at, slots, *refs):
     pieces, refs = refs[:arrays], refs[arrays:]
     shards = refs[: count * parts]
-    out, last, held, sems = refs[count * parts :]
+    *outs, last, held, sems = refs[count * parts :]
     step = pl.program_id(0)
 
     def copies(t):
@@ -172,11 +198,11 @@
                 shards[s * parts + h][...], held[rows, cols], preferred_element_type=f32
             )
             total = term if total is None else total + term
-        out[pl.ds(h * tall, tall), :] = total
+        chunk_store(step, tile, edges, outs, pl.ds(h * tall, tall), total)
     last[...] = held[pl.ds(pl.multiple_of(at[count] * width, width), width), cols]
 
 
-def partial_tangent(shards, at, pieces, slots, spots, feats, tile):
+def partial_tangent(shards, at, pieces, slots, spots, feats, tile, edges):
     count, parts = len(shards), len(shards[0])
     tall, width = shards[0][0].shape
     tok = tall * parts
@@ -189,7 +215,7 @@
         plan.append((which[0] if which else len(arrays) - 1, first, size))
     return pl.pallas_call(
         functools.partial(
-            partial_body, count, parts, width, spots, plan, len(arrays), tile
+            partial_body, count, parts, width, spots, plan, len(arrays), tile, edges
         ),
         grid_spec=pltpu.PrefetchScalarGridSpec(
             num_scalar_prefetch=2,
@@ -197,7 +223,7 @@
             in_specs=[pl.BlockSpec(memory_space=pl.ANY)] * len(arrays)
             + [whole((tall, width))] * (count * parts),
             out_specs=[
-                pl.BlockSpec((None, tok, tile), lambda j, *_: (j, 0, 0)),
+                *chunk_specs((tok,), tile, edges),
                 pl.BlockSpec((None, width, tile), lambda j, *_: (j, 0, 0)),
             ],
             scratch_shapes=[
@@ -206,7 +232,7 @@
             ],
         ),
         out_shape=[
-            jax.ShapeDtypeStruct((hidden // tile, tok, tile), f32),
+            *chunk_shapes((tok,), tile, edges, f32),
             jax.ShapeDtypeStruct((hidden // tile, width, tile), bf16),
         ],
         compiler_params=params(52),
@@ -232,8 +258,8 @@
         in_specs=[
             whole((tok, width)),
             pl.BlockSpec((None, width, tile), lambda j: (base + j, 0, 0)),
-            pl.BlockSpec((None, tok, tile), lambda j: (base + j, 0, 0)),
-            pl.BlockSpec((None, tok, tile), lambda j: (base + j, 0, 0)),
+            pl.BlockSpec((None, tok, tile), lambda j: (j, 0, 0)),
+            pl.BlockSpec((None, tok, tile), lambda j: (j, 0, 0)),
             whole(other.shape),
         ],
         out_specs=[
@@ -244,7 +270,7 @@
             jax.ShapeDtypeStruct((tok, wide), bf16),
             jax.ShapeDtypeStruct((half, wide), bf16),
         ],
-        compiler_params=params(52),
+        compiler_params=params(40),
         cost_estimate=light,
         name="front",
     )(shard, last, begun, bent, other)
@@ -305,7 +331,7 @@
         out_shape=[
             jax.ShapeDtypeStruct(shape + (side,), kind) for shape, kind in zip(shapes, kinds)
         ],
-        compiler_params=params(52),
+        compiler_params=params(30),
         cost_estimate=light,
         name="back",
     )(jnp.stack([x, y]), mine, mixed, came)
@@ -390,11 +416,11 @@
     down_full = lax.all_gather(down_weight, "dp", axis=0, tiled=True)
 
     pieces = [(p, 0, p.shape[0]) for pair in near + far for p in pair]
-    begun, last = partial_tangent(
-        [[t] for t in tok[:-1]], at, pieces, slots, rows // 2, rows * dp, unit
+    *begun, last = partial_tangent(
+        [[t] for t in tok[:-1]], at, pieces, slots, rows // 2, rows * dp, unit, edges
     )
     begun, cot[-1] = after(begun, cot[-1])
-    bent = bent_of([[c] for c in cot], at, scale, codes, down_full, unit)
+    bent = bent_of([[c] for c in cot], at, scale, codes, down_full, unit, edges)
     bent, tok[-1] = lax.optimization_barrier((bent, tok[-1]))
     if plain:
         mine, other = split_plain(tok, at, core)
@@ -405,7 +431,7 @@
     out = {}
 
     def front(j, ready):
-        return front_of(tok[-1], ready, begun, bent, other, edges[j], edges[j + 1] - edges[j])
+        return front_of(tok[-1], ready, begun[j], bent[j], other, edges[j], edges[j + 1] - edges[j])
 
     def back(j):
         return back_of(mine, mixed.pop(j), came.pop(j), x, y, xs, ys, rows)
@@ -460,10 +486,6 @@
             block_sum(keeps[j][1], first[1], 1, lax.rem(x + i, xs)).astype(bf16)
             for i in range(1, xs)
         ]
-        if j + 1 < count:
-            sends_y, sends_x, to_x, to_y = lax.optimization_barrier(
-                (sends_y, sends_x, to_x, to_y)
-            )
         second = (
             [over(p, y_way, k + 1) for k, p in enumerate(sends_y)],
             [over(p, x_way, i + 1) for i, p in enumerate(sends_x)],

time: 358 us -> 359 us (level)
  Pallas kernels: 125 us -> 109 us
  local copies, waits for them, and re-layouts: 14.7 us -> 26.6 us
  waiting for transfers between devices: 154 us -> 158 us
    unnamed x52 -> x94, local copies, waits for them, and re-layouts: 8.31 us -> 20.2 us
    pallas_call x4, Pallas kernels: 36.3 us -> 24.9 us  [front_of(): pl.pallas_call(front_body, grid=(wide // tile,), in_specs=[whole((tok, wi...]
    pallas_call x4, Pallas kernels: 29.3 us -> 18.4 us  [back_of(): pl.pallas_call(functools.partial(back_body, xs, ys, rows, steps), grid_sp...]
    ppermute x20, waiting for transfers between devices: 35.1 us -> 41.3 us  [over(): return lax.ppermute(block, 'dp', shift(way[0], way[1], dp, by))]
    unnamed x7, other arithmetic: 9.78 us -> 5.61 us
  transfers between devices with their start and end apart: 36 -> 36, of which waited for: 15 -> 18; matrix products, arithmetic and copies ran while one was open for 6% -> 5% of each run, Pallas kernels for 31% -> 28%
where the time goes in v8:
time: 359 us; the launch traced here: 358 us
  waiting for transfers between devices  158 us (44%)
  Pallas kernels  109 us (30%)
  starting transfers between devices  37.1 us (10%)
  local copies, waits for them, and re-layouts  26.6 us (7%)
  other arithmetic  14.2 us (4%)
  between operations  13.8 us (4%)
    ppermute x6, waiting for transfers between devices, ring_step(): return lax.ppermute(block, 'tensor', pairs)  113 us
    ppermute x20, waiting for transfers between devices, over(): return lax.ppermute(block, 'dp', shift(way[0], way[1], dp, by))  41.3 us
    pallas_call x1, Pallas kernels, bent_of(): pl.pallas_call(functools.partial(bent_body, count, parts, width, tile, ed...  32.2 us
    ppermute x20, starting transfers between devices, over(): return lax.ppermute(block, 'dp', shift(way[0], way[1], dp, by))  26.2 us
    pallas_call x1, Pallas kernels, partial_tangent(): pl.pallas_call(functools.partial(partial_body, count, parts, width, spots...  26 us
    pallas_call x4, Pallas kernels, front_of(): pl.pallas_call(front_body, grid=(wide // tile,), in_specs=[whole((tok, wi...  24.9 us
    unnamed x94, local copies, waits for them, and re-layouts  20.2 us
    pallas_call x4, Pallas kernels, back_of(): pl.pallas_call(functools.partial(back_body, xs, ys, rows, steps), grid_sp...  18.4 us
  transfers between devices with their start and end apart: 36, of which 18 were waited for; matrix products, arithmetic and copies ran while one was open for 5% of the time, Pallas kernels for 28%

profile of v8, /device:TPU:0, one launch (start us, length us, event | category | flops | bytes accessed | tf_op | source)
XLA Modules:
  0.0 358.3 jit_solution(4874519622216822613)
XLA Ops:
  7.3 3.0 collective-permute-start.5
  13.4 2.6 collective-permute-start.1
  16.0 34.3 %collective-permute-done.refs_1_ = bf16[1024,768]{1,0:T(8,128)(2,1)S(1)} collective-permute-done((bf16[1024,768]{1,0:T(8,128)(2,1)}, bf16[1024,768]{1,0:T(8,128)(2,1)S(1)}, u32[]{:S(2)}, u32[]{:S(2)}) %collective-permute-start) | collective-permute-done | bytes 1572896 | tf_op jit(solution)/shard_map/ppermute | solution.py:348
  50.2 31.9 %collective-permute-done.1.refs_1_.refs_11_ = bf16[1024,768]{1,0:T(8,128)(2,1)S(1)} collective-permute-done((bf16[1024,768]{1,0:T(8,128)(2,1)S(1)}, bf16[1024,768]{1,0:T(8,128)(2,1)S(1)}, u32[]{:S(2)}, u32[]{:S(2)}) %collective-permute-start.1) | collective-permute-done | bytes 1572896 | tf_op jit(solution)/shard_map/ppermute | solution.py:348
  84.1 8.9 %collective-permute-done.5.refs_2_ = bf16[384,3072]{1,0:T(8,128)(2,1)} collective-permute-done((bf16[384,3072]{1,0:T(8,128)(2,1)}, bf16[384,3072]{1,0:T(8,128)(2,1)}, u32[]{:S(2)}, u32[]{:S(2)}) %collective-permute-start.5) | collective-permute-done | bytes 2359328 | tf_op jit(solution)/shard_map/ppermute | solution.py:388
  93.0 2.8 collective-permute-done.7.refs_4_
  104.4 17.2 %collective-permute-done.3.refs_2_.refs_12_ = bf16[1024,768]{1,0:T(8,128)(2,1)} collective-permute-done((bf16[1024,768]{1,0:T(8,128)(2,1)S(1)}, bf16[1024,768]{1,0:T(8,128)(2,1)}, u32[]{:S(2)}, u32[]{:S(2)}) %collective-permute-start.3) | collective-permute-done | bytes 1572896 | tf_op jit(solution)/shard_map/ppermute | solution.py:348
  123.0 29.7 %collective-permute-done.2.refs_2_ = bf16[1024,768]{1,0:T(8,128)(2,1)} collective-permute-done((bf16[1024,768]{1,0:T(8,128)(2,1)S(1)}, bf16[1024,768]{1,0:T(8,128)(2,1)}, u32[]{:S(2)}, u32[]{:S(2)}) %collective-permute-start.2) | collective-permute-done | bytes 1572896 | tf_op jit(solution)/shard_map/ppermute | solution.py:348
  153.4 3.5 collective-permute-start.14
  156.9 4.9 %split_cores.2 = (bf16[1536,1024]{1,0:T(8,128)(2,1)}, bf16[1536,1024]{1,0:T(8,128)(2,1)}) custom-call(s32[1]{0:T(128)} %bitcast.2.core, s32[3]{0:T(128)S(1)} %bitcast.65, bf16[1024,768]{1,0:T(8,128)(2,1)S(1)} %copy-done.7, bf16[1024,768]{1,0:T(8,128)(2,1)} %copy-done.33, bf16[1024,768]{1,0:T(8,128)(2,1)} %collective-permute-done.3.refs_2_.refs_12_), custom_call_target="tpu_custom_call" | custom-call | bytes 1024 | tf_op jit(solution)/shard_map/split_cores/pallas_call | solution.py:57
  166.1 26.0 %partial_tangent.1 = (f32[2,1024,512]{2,1,0:T(8,128)}, f32[1,1024,512]{2,1,0:T(8,128)}, f32[2,1024,512]{2,1,0:T(8,128)}, f32[1,1024,512]{2,1,0:T(8,128)}, bf16[6,768,512]{2,1,0:T(8,128)(2,1)}) custom-call(s32[4]{0:T(128)S(1)} %fusion.16.at, s32[10]{0:T(128)S(1)} %stack.64.slots, bf16[384,3072]{1,0:T(8,128)(2,1)} %refs_0_.4, bf16[384,3072]{1,0:T(8,128)(2,1)} %copy-done.34, ...), custom_call_target="tpu_custom_call" | custom-call | bytes 1024 | tf_op jit(solution)/shard_map/partial_tangent/pallas_call | solution.py:216
  192.2 32.2 %bent.1 = (f32[2,1024,512]{2,1,0:T(8,128)}, f32[1,1024,512]{2,1,0:T(8,128)}, f32[2,1024,512]{2,1,0:T(8,128)}, f32[1,1024,512]{2,1,0:T(8,128)}) custom-call(s32[4]{0:T(128)S(1)} %fusion.16.at, f32[1024,1]{1,0:T(8,128)S(1)} %copy.10.scale, s32[1024,3072]{1,0:T(8,128)} %codes.1, bf16[3072,3072]{1,0:T(8,128)(2,1)} %all-gather.2.cloned.1.call-done.down, ...), custom_call_target="tpu_custom_call" | custom-call | bytes 1024 | tf_op jit(solution)/shard_map/bent/pallas_call | solution.py:147
  229.6 7.6 %front.4 = (bf16[1024,1024]{1,0:T(8,128)(2,1)S(1)}, bf16[1536,1024]{1,0:T(8,128)(2,1)S(1)}) custom-call(bf16[1024,768]{1,0:T(8,128)(2,1)S(1)} %collective-permute-done.14.refs_0_.shard, bf16[6,768,512]{2,1,0:T(8,128)(2,1)} %get-tuple-element.172.probe, f32[2,1024,512]{2,1,0:T(8,128)S(1)} %copy-done.9, f32[2,1024,512]{2,1,0:T(8,128)} %get-tuple-element.137.bent, ...), custom_call_target="tpu_custom_call" | custom-call | bytes 1024 | tf_op jit(solution)/shard_map/front/pallas_call | solution.py:255
  240.5 3.9 %front.5 = (bf16[1024,512]{1,0:T(8,128)(2,1)S(1)}, bf16[1536,512]{1,0:T(8,128)(2,1)S(1)}) custom-call(bf16[1024,768]{1,0:T(8,128)(2,1)S(1)} %copy-done.5, bf16[6,768,512]{2,1,0:T(8,128)(2,1)} %get-tuple-element.172.probe, f32[1,1024,512]{2,1,0:T(8,128)S(1)} %copy-done.12, f32[1,1024,512]{2,1,0:T(8,128)S(1)} %copy-done.15, bf16[1536,1024]{1,0:T(8,128)(2,1)S(1)} %copy-done.1), custom_call_target="tpu_custom_call" | custom-call | bytes 1024 | tf_op jit(solution)/shard_map/front/pallas_call | solution.py:255
  245.0 4.7 %back.4 = (f32[2,1,384,512]{3,2,1,0:T(8,128)S(1)}, f32[1,2,384,512]{3,2,1,0:T(8,128)S(1)}, bf16[2,1,384,512]{3,2,1,0:T(8,128)(2,1)S(1)}, bf16[1,2,384,512]{3,2,1,0:T(8,128)(2,1)S(1)}) custom-call(s32[2]{0:T(128)S(1)} %pad_add_fusion.me, bf16[1536,1024]{1,0:T(8,128)(2,1)S(1)} %copy-done, bf16[1024,1024]{1,0:T(8,128)(2,1)S(1)} %get-tuple-element.146.mixed, ...), custom_call_target="tpu_custom_call" | custom-call | bytes 1024 | tf_op jit(solution)/shard_map/back/pallas_call | solution.py:316
  252.2 3.0 collective-permute-start.16
  256.0 2.8 back.5
  261.3 8.5 %front.6 = (bf16[1024,1024]{1,0:T(8,128)(2,1)S(1)}, bf16[1536,1024]{1,0:T(8,128)(2,1)}) custom-call(bf16[1024,768]{1,0:T(8,128)(2,1)S(1)} %copy-done.5, bf16[6,768,512]{2,1,0:T(8,128)(2,1)} %get-tuple-element.172.probe, f32[2,1024,512]{2,1,0:T(8,128)S(1)} %copy-done.8, f32[2,1024,512]{2,1,0:T(8,128)} %get-tuple-element.159.bent, bf16[1536,1024]{1,0:T(8,128)(2,1)S(1)} %copy-done.2), custom_call_target="tpu_custom_call" | custom-call | bytes 1024 | tf_op jit(solution)/shard_map/front/pallas_call | solution.py:255
  282.8 6.9 %back.6 = (f32[2,1,384,512]{3,2,1,0:T(8,128)S(1)}, f32[1,2,384,512]{3,2,1,0:T(8,128)S(1)}, bf16[2,1,384,512]{3,2,1,0:T(8,128)(2,1)}, bf16[1,2,384,512]{3,2,1,0:T(8,128)(2,1)}) custom-call(s32[2]{0:T(128)S(1)} %pad_add_fusion.me, bf16[1536,1024]{1,0:T(8,128)(2,1)S(1)} %copy-done, bf16[1024,1024]{1,0:T(8,128)(2,1)S(1)} %copy-done.14, ...), custom_call_target="tpu_custom_call" | custom-call | bytes 1024 | tf_op jit(solution)/shard_map/back/pallas_call | solution.py:316
  292.1 4.9 %front.7 = (bf16[1024,512]{1,0:T(8,128)(2,1)S(1)}, bf16[1536,512]{1,0:T(8,128)(2,1)}) custom-call(bf16[1024,768]{1,0:T(8,128)(2,1)S(1)} %copy-done.6, bf16[6,768,512]{2,1,0:T(8,128)(2,1)} %get-tuple-element.172.probe, f32[1,1024,512]{2,1,0:T(8,128)S(1)} %copy-done.10, f32[1,1024,512]{2,1,0:T(8,128)S(1)} %copy-done.11, bf16[1536,1024]{1,0:T(8,128)(2,1)S(1)} %copy-done.3), custom_call_target="tpu_custom_call" | custom-call | bytes 1024 | tf_op jit(solution)/shard_map/front/pallas_call | solution.py:255
  309.9 4.0 %back.7 = (f32[2,1,384,256]{3,2,1,0:T(8,128)S(1)}, f32[1,2,384,256]{3,2,1,0:T(8,128)S(1)}, bf16[2,1,384,256]{3,2,1,0:T(8,128)(2,1)S(1)}, bf16[1,2,384,256]{3,2,1,0:T(8,128)(2,1)S(1)}) custom-call(s32[2]{0:T(128)S(1)} %pad_add_fusion.me, bf16[1536,1024]{1,0:T(8,128)(2,1)S(1)} %copy-done, bf16[1024,512]{1,0:T(8,128)(2,1)S(1)} %copy-done.24, ...), custom_call_target="tpu_custom_call" | custom-call | bytes 1024 | tf_op jit(solution)/shard_map/back/pallas_call | solution.py:316
  314.0 10.7 %collective-permute-done.28 = bf16[1,1,384,256]{3,2,1,0:T(8,128)(2,1)S(1)} collective-permute-done((bf16[1,1,384,256]{3,2,1,0:T(8,128)(2,1)S(1)}, bf16[1,1,384,256]{3,2,1,0:T(8,128)(2,1)S(1)}, u32[]{:S(2)}, u32[]{:S(2)}) %collective-permute-start.28) | collective-permute-done | bytes 196640 | tf_op jit(solution)/shard_map/ppermute | solution.py:388
  332.0 5.4 %collective-permute-done.33 = bf16[1,2,384,256]{3,2,1,0:T(8,128)(2,1)S(1)} collective-permute-done((bf16[1,2,384,256]{3,2,1,0:T(8,128)(2,1)S(1)}, bf16[1,2,384,256]{3,2,1,0:T(8,128)(2,1)S(1)}, u32[]{:S(2)}, u32[]{:S(2)}) %collective-permute-start.33) | collective-permute-done | bytes 393248 | tf_op jit(solution)/shard_map/ppermute | solution.py:388
  339.6 6.2 %collective-permute-done.29 = bf16[1,1,384,512]{3,2,1,0:T(8,128)(2,1)S(1)} collective-permute-done((bf16[1,1,384,512]{3,2,1,0:T(8,128)(2,1)S(1)}, bf16[1,1,384,512]{3,2,1,0:T(8,128)(2,1)S(1)}, u32[]{:S(2)}, u32[]{:S(2)}) %collective-permute-start.29) | collective-permute-done | bytes 393248 | tf_op jit(solution)/shard_map/ppermute | solution.py:388
  (178 shorter events, 78.8 us)
Async XLA Ops:
  6.5 185.7 %all-gather.2.cloned.1.call-start = ((), (), s32[]{:S(2)}) async-start(), calls=%async_computation | async-start | bytes 21233664 | tf_op jit(solution)/shard_map/all_gather | solution.py:416
  7.3 85.7 %collective-permute-start.5 = (bf16[384,3072]{1,0:T(8,128)(2,1)}, bf16[384,3072]{1,0:T(8,128)(2,1)}, u32[]{:S(2)}, u32[]{:S(2)}) collective-permute-start(bf16[384,3072]{1,0:T(8,128)(2,1)} %refs_0_.4), channel_id=1, source_target_pairs={{0,8},{4,12},{8,0},{12,4},{16,24},{20,28},{24,16},{28,20},{1,9},{5... | collective-permute-start | bytes 7077896 | tf_op jit(solution)/shard_map/ppermute | solution.py:388
  10.3 85.5 %collective-permute-start.7 = (bf16[384,3072]{1,0:T(8,128)(2,1)}, bf16[384,3072]{1,0:T(8,128)(2,1)}, u32[]{:S(2)}, u32[]{:S(2)}) collective-permute-start(bf16[384,3072]{1,0:T(8,128)(2,1)} %refs_0_.4), channel_id=1, source_target_pairs={{0,16},{4,20},{8,24},{12,28},{16,0},{20,4},{24,8},{28,12},{1,17},{... | collective-permute-start | bytes 7077896 | tf_op jit(solution)/shard_map/ppermute | solution.py:388
  11.8 38.4 %collective-permute-start = (bf16[1024,768]{1,0:T(8,128)(2,1)}, bf16[1024,768]{1,0:T(8,128)(2,1)S(1)}, u32[]{:S(2)}, u32[]{:S(2)}) collective-permute-start(bf16[1024,768]{1,0:T(8,128)(2,1)} %refs_0_.5), channel_id=1, source_target_pairs={{0,1},{1,3},{3,2},{2,0},{4,5},{5,7},{7,6},{6,4},{8,9},{9,11},{11,1... | collective-permute-start | bytes 4718600 | tf_op jit(solution)/shard_map/ppermute | solution.py:348
  13.4 68.8 %collective-permute-start.1 = (bf16[1024,768]{1,0:T(8,128)(2,1)S(1)}, bf16[1024,768]{1,0:T(8,128)(2,1)S(1)}, u32[]{:S(2)}, u32[]{:S(2)}) collective-permute-start(bf16[1024,768]{1,0:T(8,128)(2,1)S(1)} %copy-done.7), channel_id=1, source_target_pairs={{0,1},{1,3},{3,2},{2,0},{4,5},{5,7},{7,6},{6,4},{8,9},{9,11},{11,1... | collective-permute-start | bytes 4718600 | tf_op jit(solution)/shard_map/ppermute | solution.py:348
  16.0 83.6 %collective-permute-start.4 = (bf16[384,3072]{1,0:T(8,128)(2,1)}, bf16[384,3072]{1,0:T(8,128)(2,1)S(1)}, u32[]{:S(2)}, u32[]{:S(2)}) collective-permute-start(bf16[384,3072]{1,0:T(8,128)(2,1)} %refs_0_.4), channel_id=1, source_target_pairs={{0,4},{4,0},{8,12},{12,8},{16,20},{20,16},{24,28},{28,24},{1,5},{5... | collective-permute-start | bytes 7077896 | tf_op jit(solution)/shard_map/ppermute | solution.py:352
  83.3 38.3 %collective-permute-start.3 = (bf16[1024,768]{1,0:T(8,128)(2,1)S(1)}, bf16[1024,768]{1,0:T(8,128)(2,1)}, u32[]{:S(2)}, u32[]{:S(2)}) collective-permute-start(bf16[1024,768]{1,0:T(8,128)(2,1)S(1)} %collective-permute-done.1.refs_1_.refs_11_), channel_id=1, source_target_pairs={{0,1},{1,3},{3,2},{2,0},{4,5},{5,7},{7,6},{6,4},{8,9},{9,11},{11,1... | collective-permute-start | bytes 4718600 | tf_op jit(solution)/shard_map/ppermute | solution.py:348
  93.0 59.7 %collective-permute-start.6 = (bf16[384,3072]{1,0:T(8,128)(2,1)}, bf16[384,3072]{1,0:T(8,128)(2,1)}, u32[]{:S(2)}, u32[]{:S(2)}) collective-permute-start(bf16[384,3072]{1,0:T(8,128)(2,1)} %collective-permute-done.5.refs_2_), channel_id=1, source_target_pairs={{0,4},{4,0},{8,12},{12,8},{16,20},{20,16},{24,28},{28,24},{1,5},{5... | collective-permute-start | bytes 7077896 | tf_op jit(solution)/shard_map/ppermute | solution.py:352
  95.8 56.9 %collective-permute-start.8 = (bf16[384,3072]{1,0:T(8,128)(2,1)}, bf16[384,3072]{1,0:T(8,128)(2,1)}, u32[]{:S(2)}, u32[]{:S(2)}) collective-permute-start(bf16[384,3072]{1,0:T(8,128)(2,1)} %collective-permute-done.7.refs_4_), channel_id=1, source_target_pairs={{0,4},{4,0},{8,12},{12,8},{16,20},{20,16},{24,28},{28,24},{1,5},{5... | collective-permute-start | bytes 7077896 | tf_op jit(solution)/shard_map/ppermute | solution.py:352
  95.8 56.9 %collective-permute-start.2 = (bf16[1024,768]{1,0:T(8,128)(2,1)S(1)}, bf16[1024,768]{1,0:T(8,128)(2,1)}, u32[]{:S(2)}, u32[]{:S(2)}) collective-permute-start(bf16[1024,768]{1,0:T(8,128)(2,1)S(1)} %collective-permute-done.refs_1_), channel_id=1, source_target_pairs={{0,1},{1,3},{3,2},{2,0},{4,5},{5,7},{7,6},{6,4},{8,9},{9,11},{11,1... | collective-permute-start | bytes 4718600 | tf_op jit(solution)/shard_map/ppermute | solution.py:348
  99.6 57.3 %collective-permute-start.9 = (bf16[192,3072]{1,0:T(8,128)(2,1)}, bf16[192,3072]{1,0:T(8,128)(2,1)}, u32[]{:S(2)}, u32[]{:S(2)}) collective-permute-start(bf16[192,3072]{1,0:T(8,128)(2,1)} %slice.48), channel_id=1, source_target_pairs={{0,16},{4,20},{8,24},{12,28},{16,0},{20,4},{24,8},{28,12},{1,17},{... | collective-permute-start | bytes 3538952 | tf_op jit(solution)/shard_map/ppermute | solution.py:388
  121.6 41.3 %collective-permute-start.11 = (bf16[192,3072]{1,0:T(8,128)(2,1)}, bf16[192,3072]{1,0:T(8,128)(2,1)}, u32[]{:S(2)}, u32[]{:S(2)}) collective-permute-start(bf16[192,3072]{1,0:T(8,128)(2,1)} %slice.49), channel_id=1, source_target_pairs={{0,8},{4,12},{8,0},{12,4},{16,24},{20,28},{24,16},{28,20},{1,9},{5... | collective-permute-start | bytes 3538952 | tf_op jit(solution)/shard_map/ppermute | solution.py:388
  152.7 39.5 %collective-permute-start.13 = (bf16[1024,768]{1,0:T(8,128)(2,1)}, bf16[1024,768]{1,0:T(8,128)(2,1)}, u32[]{:S(2)}, u32[]{:S(2)}) collective-permute-start(bf16[1024,768]{1,0:T(8,128)(2,1)} %collective-permute-done.2.refs_2_), channel_id=1, source_target_pairs={{0,1},{1,3},{3,2},{2,0},{4,5},{5,7},{7,6},{6,4},{8,9},{9,11},{11,1... | collective-permute-start | bytes 4718600 | tf_op jit(solution)/shard_map/ppermute | solution.py:348
  153.4 71.0 %collective-permute-start.14 = (bf16[1024,768]{1,0:T(8,128)(2,1)}, bf16[1024,768]{1,0:T(8,128)(2,1)S(1)}, u32[]{:S(2)}, u32[]{:S(2)}) collective-permute-start(bf16[1024,768]{1,0:T(8,128)(2,1)} %collective-permute-done.3.refs_2_.refs_12_), channel_id=1, source_target_pairs={{0,1},{1,3},{3,2},{2,0},{4,5},{5,7},{7,6},{6,4},{8,9},{9,11},{11,1... | collective-permute-start | bytes 4718600 | tf_op jit(solution)/shard_map/ppermute | solution.py:348
  252.2 21.0 %collective-permute-start.16 = (bf16[2,1,384,512]{3,2,1,0:T(8,128)(2,1)S(1)}, bf16[2,1,384,512]{3,2,1,0:T(8,128)(2,1)S(1)}, u32[]{:S(2)}, u32[]{:S(2)}) collective-permute-start(bf16[2,1,384,512]{3,2,1,0:T(8,128)(2,1)S(1)} %get-tuple-element.151), channel_id=1, source_target_pairs={{0,8},{4,12},{8,0},{12,4},{16,24},{20,28},{24,16},{28,20},{1,9},{5... | collective-permute-start | bytes 2359304 | tf_op jit(solution)/shard_map/ppermute | solution.py:388
  255.1 19.5 %collective-permute-start.17 = (bf16[1,2,384,512]{3,2,1,0:T(8,128)(2,1)S(1)}, bf16[1,2,384,512]{3,2,1,0:T(8,128)(2,1)S(1)}, u32[]{:S(2)}, u32[]{:S(2)}) collective-permute-start(bf16[1,2,384,512]{3,2,1,0:T(8,128)(2,1)S(1)} %get-tuple-element.152), channel_id=1, source_target_pairs={{0,16},{4,20},{8,24},{12,28},{16,0},{20,4},{24,8},{28,12},{1,17},{... | collective-permute-start | bytes 2359304 | tf_op jit(solution)/shard_map/ppermute | solution.py:388
  277.1 20.9 %collective-permute-start.23 = (bf16[1,1,384,512]{3,2,1,0:T(8,128)(2,1)S(1)}, bf16[1,1,384,512]{3,2,1,0:T(8,128)(2,1)S(1)}, u32[]{:S(2)}, u32[]{:S(2)}) collective-permute-start(bf16[1,1,384,512]{3,2,1,0:T(8,128)(2,1)S(1)} %add_convert_fusion.2), channel_id=1, source_target_pairs={{0,8},{4,12},{8,0},{12,4},{16,24},{20,28},{24,16},{28,20},{1,9},{5... | collective-permute-start | bytes 1179656 | tf_op jit(solution)/shard_map/ppermute | solution.py:388
  279.8 18.2 %collective-permute-start.22 = (bf16[1,1,384,512]{3,2,1,0:T(8,128)(2,1)S(1)}, bf16[1,1,384,512]{3,2,1,0:T(8,128)(2,1)S(1)}, u32[]{:S(2)}, u32[]{:S(2)}) collective-permute-start(bf16[1,1,384,512]{3,2,1,0:T(8,128)(2,1)S(1)} %add_convert_fusion.3), channel_id=1, source_target_pairs={{0,16},{4,20},{8,24},{12,28},{16,0},{20,4},{24,8},{28,12},{1,17},{... | collective-permute-start | bytes 1179656 | tf_op jit(solution)/shard_map/ppermute | solution.py:388
  281.6 17.9 %collective-permute-start.20 = (bf16[1,2,384,256]{3,2,1,0:T(8,128)(2,1)S(1)}, bf16[1,2,384,256]{3,2,1,0:T(8,128)(2,1)S(1)}, u32[]{:S(2)}, u32[]{:S(2)}) collective-permute-start(bf16[1,2,384,256]{3,2,1,0:T(8,128)(2,1)S(1)} %get-tuple-element.167), channel_id=1, source_target_pairs={{0,16},{4,20},{8,24},{12,28},{16,0},{20,4},{24,8},{28,12},{1,17},{... | collective-permute-start | bytes 1179656 | tf_op jit(solution)/shard_map/ppermute | solution.py:388
  300.3 25.0 %collective-permute-start.24 = (bf16[2,1,384,512]{3,2,1,0:T(8,128)(2,1)}, bf16[2,1,384,512]{3,2,1,0:T(8,128)(2,1)}, u32[]{:S(2)}, u32[]{:S(2)}) collective-permute-start(bf16[2,1,384,512]{3,2,1,0:T(8,128)(2,1)} %get-tuple-element.191), channel_id=1, source_target_pairs={{0,8},{4,12},{8,0},{12,4},{16,24},{20,28},{24,16},{28,20},{1,9},{5... | collective-permute-start | bytes 2359304 | tf_op jit(solution)/shard_map/ppermute | solution.py:388
  301.2 24.0 %collective-permute-start.25 = (bf16[1,2,384,512]{3,2,1,0:T(8,128)(2,1)}, bf16[1,2,384,512]{3,2,1,0:T(8,128)(2,1)}, u32[]{:S(2)}, u32[]{:S(2)}) collective-permute-start(bf16[1,2,384,512]{3,2,1,0:T(8,128)(2,1)} %get-tuple-element.192), channel_id=1, source_target_pairs={{0,16},{4,20},{8,24},{12,28},{16,0},{20,4},{24,8},{28,12},{1,17},{... | collective-permute-start | bytes 2359304 | tf_op jit(solution)/shard_map/ppermute | solution.py:388
  303.3 21.4 %collective-permute-start.28 = (bf16[1,1,384,256]{3,2,1,0:T(8,128)(2,1)S(1)}, bf16[1,1,384,256]{3,2,1,0:T(8,128)(2,1)S(1)}, u32[]{:S(2)}, u32[]{:S(2)}) collective-permute-start(bf16[1,1,384,256]{3,2,1,0:T(8,128)(2,1)S(1)} %add_convert_fusion.6), channel_id=1, source_target_pairs={{0,8},{4,12},{8,0},{12,4},{16,24},{20,28},{24,16},{28,20},{1,9},{5... | collective-permute-start | bytes 589832 | tf_op jit(solution)/shard_map/ppermute | solution.py:388
  305.7 19.6 %collective-permute-start.27 = (bf16[1,1,384,256]{3,2,1,0:T(8,128)(2,1)S(1)}, bf16[1,1,384,256]{3,2,1,0:T(8,128)(2,1)S(1)}, u32[]{:S(2)}, u32[]{:S(2)}) collective-permute-start(bf16[1,1,384,256]{3,2,1,0:T(8,128)(2,1)S(1)} %add_convert_fusion.7), channel_id=1, source_target_pairs={{0,16},{4,20},{8,24},{12,28},{16,0},{20,4},{24,8},{28,12},{1,17},{... | collective-permute-start | bytes 589832 | tf_op jit(solution)/shard_map/ppermute | solution.py:388
  328.4 18.6 %collective-permute-start.30 = (bf16[1,1,384,512]{3,2,1,0:T(8,128)(2,1)S(1)}, bf16[1,1,384,512]{3,2,1,0:T(8,128)(2,1)S(1)}, u32[]{:S(2)}, u32[]{:S(2)}) collective-permute-start(bf16[1,1,384,512]{3,2,1,0:T(8,128)(2,1)S(1)} %add_convert_fusion), channel_id=1, source_target_pairs={{0,8},{4,12},{8,0},{12,4},{16,24},{20,28},{24,16},{28,20},{1,9},{5... | collective-permute-start | bytes 1179656 | tf_op jit(solution)/shard_map/ppermute | solution.py:388
  (59 other events, 536.9 us)
Sparse Core Ops, SparseCore 0:
  9.2 157.9 all-gather.1

commit v9 on v6

--- a/solution.py
+++ b/solution.py
@@ -425,33 +425,7 @@
             weight = probe[:, a:b].astype(f32)
             out[2 * j + n] = weight * total.reshape(rows, b - a) * (1.0 / (tok_rows * dp))
 
-    mixed, came, keeps = {}, {}, {}
-    mixed[0], away = front(0, last)
-    came[0] = swapped(away, dp, cores)
-    if count > 1:
-        mixed[0], last = lax.optimization_barrier((mixed[0], last))
-        mixed[1], away = front(1, last)
-        mixed[0], away, came[0] = lax.optimization_barrier((mixed[0], away, came[0]))
-        came[1] = swapped(away, dp, cores)
-    *keeps[0], to_x, to_y = back(0)
-    behind = None
-    for j in range(count):
-        if j + 1 < count:
-            to_x, to_y, mixed[j + 1] = lax.optimization_barrier((to_x, to_y, mixed[j + 1]))
-        first = first_turn(to_x, to_y)
-        if j + 1 < count:
-            *keeps[j + 1], to_x, to_y = back(j + 1)
-        if j + 2 < count:
-            to_x, to_y, last = lax.optimization_barrier((to_x, to_y, last))
-            mixed[j + 2], away = front(j + 2, last)
-            first, away, to_x, to_y, behind = lax.optimization_barrier(
-                (first, away, to_x, to_y, behind)
-            )
-            came[j + 2] = swapped(away, dp, cores)
-        elif j + 1 < count:
-            first, to_x, to_y, behind = lax.optimization_barrier((first, to_x, to_y, behind))
-        if j >= 1:
-            finish(j - 1, *behind)
+    def second_turn(j, first):
         sends_y = [
             block_sum(keeps[j][0], first[0], 0, lax.rem(y + k, ys)).astype(bf16)
             for k in range(1, ys)
@@ -460,16 +434,54 @@
             block_sum(keeps[j][1], first[1], 1, lax.rem(x + i, xs)).astype(bf16)
             for i in range(1, xs)
         ]
-        if j + 1 < count:
-            sends_y, sends_x, to_x, to_y = lax.optimization_barrier(
-                (sends_y, sends_x, to_x, to_y)
-            )
-        second = (
+        return sends_y, sends_x
+
+    def send_second(sends_y, sends_x):
+        return (
             [over(p, y_way, k + 1) for k, p in enumerate(sends_y)],
             [over(p, x_way, i + 1) for i, p in enumerate(sends_x)],
         )
-        behind = (keeps.pop(j), first, second)
-    finish(count - 1, *behind)
+
+    mixed, came, keeps = {}, {}, {}
+    mixed[0], away = front(0, last)
+    came[0] = swapped(away, dp, cores)
+    mixed[0], last = lax.optimization_barrier((mixed[0], last))
+    mixed[1], away = front(1, last)
+    mixed[0], away, came[0] = lax.optimization_barrier((mixed[0], away, came[0]))
+    came[1] = swapped(away, dp, cores)
+    *keeps[0], to_x, to_y = back(0)
+    waiting = None
+    for j in range(0, count, 2):
+        more = j + 2 < count
+        to_x, to_y, mixed[j + 1] = lax.optimization_barrier((to_x, to_y, mixed[j + 1]))
+        first = first_turn(to_x, to_y)
+        *keeps[j + 1], next_x, next_y = back(j + 1)
+        if more:
+            next_x, next_y, last = lax.optimization_barrier((next_x, next_y, last))
+        following = first_turn(next_x, next_y)
+        if waiting is not None:
+            for n, (pair, arrived) in enumerate(waiting):
+                finish(j - 2 + n, keeps[j - 2 + n], pair, arrived)
+        if more:
+            mixed[j + 2], away = front(j + 2, last)
+            mixed[j + 3], later = front(j + 3, last)
+            first, following, away, later = lax.optimization_barrier(
+                (first, following, away, later)
+            )
+            came[j + 2] = swapped(away, dp, cores)
+            came[j + 3] = swapped(later, dp, cores)
+        else:
+            first, following = lax.optimization_barrier((first, following))
+        sends = [second_turn(j, first), second_turn(j + 1, following)]
+        if more:
+            sends, mixed[j + 2] = lax.optimization_barrier((sends, mixed[j + 2]))
+        arrived = [send_second(*pair) for pair in sends]
+        if more:
+            *keeps[j + 2], to_x, to_y = back(j + 2)
+            arrived, to_x, to_y = lax.optimization_barrier((arrived, to_x, to_y))
+        waiting = [(first, arrived[0]), (following, arrived[1])]
+    for n, (pair, arrived) in enumerate(waiting):
+        finish(count - 2 + n, keeps[count - 2 + n], pair, arrived)
     return jnp.concatenate([out[j] for j in range(2 * count)], axis=1)
 
 

time: 358 us -> 357 us (level)
  other arithmetic: 15.7 us -> 9.11 us
  waiting for transfers between devices: 154 us -> 159 us
    unnamed x7, other arithmetic: 9.78 us -> 3.15 us
    ppermute x20, waiting for transfers between devices: 35.1 us -> 39.7 us  [over(): return lax.ppermute(block, 'dp', shift(way[0], way[1], dp, by))]
    unnamed x52 -> x68, local copies, waits for them, and re-layouts: 8.31 us -> 7.42 us
  transfers between devices with their start and end apart: 36 -> 36, of which waited for: 15 -> 18; matrix products, arithmetic and copies ran while one was open for 6% -> 4% of each run, Pallas kernels for 31% -> 32%
where the time goes in v9:
time: 357 us; the launch traced here: 356 us
  waiting for transfers between devices  159 us (45%)
  Pallas kernels  125 us (35%)
  starting transfers between devices  35.8 us (10%)
  local copies, waits for them, and re-layouts  13.7 us (4%)
  between operations  13.7 us (4%)
  other arithmetic  9.11 us (3%)
    ppermute x6, waiting for transfers between devices, ring_step(): return lax.ppermute(block, 'tensor', pairs)  116 us
    ppermute x20, waiting for transfers between devices, over(): return lax.ppermute(block, 'dp', shift(way[0], way[1], dp, by))  39.7 us
    pallas_call x4, Pallas kernels, front_of(): pl.pallas_call(front_body, grid=(wide // tile,), in_specs=[whole((tok, wi...  36.7 us
    pallas_call x4, Pallas kernels, back_of(): pl.pallas_call(functools.partial(back_body, xs, ys, rows, steps), grid_sp...  29.2 us
    pallas_call x1, Pallas kernels, bent_of(): pl.pallas_call(functools.partial(bent_body, count, parts, width), grid_sp...  29.2 us
    ppermute x20, starting transfers between devices, over(): return lax.ppermute(block, 'dp', shift(way[0], way[1], dp, by))  24.2 us
    pallas_call x1, Pallas kernels, partial_tangent(): pl.pallas_call(functools.partial(partial_body, count, parts, width, spots...  23 us
    ppermute x6, starting transfers between devices, ring_step(): return lax.ppermute(block, 'tensor', pairs)  10.6 us
  transfers between devices with their start and end apart: 36, of which 18 were waited for; matrix products, arithmetic and copies ran while one was open for 4% of the time, Pallas kernels for 32%

profile of v9, /device:TPU:0, one launch (start us, length us, event | category | flops | bytes accessed | tf_op | source)
XLA Modules:
  0.0 356.4 jit_solution(18315585062651878236)
XLA Ops:
  7.3 3.0 collective-permute-start.5
  13.4 2.6 collective-permute-start.1
  16.0 34.3 %collective-permute-done.refs_1_ = bf16[1024,768]{1,0:T(8,128)(2,1)S(1)} collective-permute-done((bf16[1024,768]{1,0:T(8,128)(2,1)}, bf16[1024,768]{1,0:T(8,128)(2,1)S(1)}, u32[]{:S(2)}, u32[]{:S(2)}) %collective-permute-start) | collective-permute-done | bytes 1572896 | tf_op jit(solution)/shard_map/ppermute | solution.py:322
  50.2 31.9 %collective-permute-done.1.refs_1_.refs_11_ = bf16[1024,768]{1,0:T(8,128)(2,1)S(1)} collective-permute-done((bf16[1024,768]{1,0:T(8,128)(2,1)S(1)}, bf16[1024,768]{1,0:T(8,128)(2,1)S(1)}, u32[]{:S(2)}, u32[]{:S(2)}) %collective-permute-start.1) | collective-permute-done | bytes 1572896 | tf_op jit(solution)/shard_map/ppermute | solution.py:322
  84.1 8.8 %collective-permute-done.5.refs_2_ = bf16[384,3072]{1,0:T(8,128)(2,1)} collective-permute-done((bf16[384,3072]{1,0:T(8,128)(2,1)}, bf16[384,3072]{1,0:T(8,128)(2,1)}, u32[]{:S(2)}, u32[]{:S(2)}) %collective-permute-start.5) | collective-permute-done | bytes 2359328 | tf_op jit(solution)/shard_map/ppermute | solution.py:362
  93.0 2.8 collective-permute-done.7.refs_4_
  99.6 2.5 collective-permute-start.9
  104.4 17.2 %collective-permute-done.3.refs_2_.refs_12_ = bf16[1024,768]{1,0:T(8,128)(2,1)} collective-permute-done((bf16[1024,768]{1,0:T(8,128)(2,1)S(1)}, bf16[1024,768]{1,0:T(8,128)(2,1)}, u32[]{:S(2)}, u32[]{:S(2)}) %collective-permute-start.3) | collective-permute-done | bytes 1572896 | tf_op jit(solution)/shard_map/ppermute | solution.py:322
  123.0 29.7 %collective-permute-done.2.refs_2_ = bf16[1024,768]{1,0:T(8,128)(2,1)} collective-permute-done((bf16[1024,768]{1,0:T(8,128)(2,1)S(1)}, bf16[1024,768]{1,0:T(8,128)(2,1)}, u32[]{:S(2)}, u32[]{:S(2)}) %collective-permute-start.2) | collective-permute-done | bytes 1572896 | tf_op jit(solution)/shard_map/ppermute | solution.py:322
  153.4 3.5 collective-permute-start.14
  156.9 4.9 %split_cores.2 = (bf16[1536,1024]{1,0:T(8,128)(2,1)}, bf16[1536,1024]{1,0:T(8,128)(2,1)}) custom-call(s32[1]{0:T(128)} %bitcast.2.core, s32[3]{0:T(128)S(1)} %bitcast.65, bf16[1024,768]{1,0:T(8,128)(2,1)S(1)} %copy-done.2, bf16[1024,768]{1,0:T(8,128)(2,1)} %copy-done.6, bf16[1024,768]{1,0:T(8,128)(2,1)} %collective-permute-done.3.refs_2_.refs_12_), custom_call_target="tpu_custom_call" | custom-call | bytes 1024 | tf_op jit(solution)/shard_map/split_cores/pallas_call | solution.py:57
  166.1 23.0 %partial_tangent.1 = (f32[6,1024,512]{2,1,0:T(8,128)}, bf16[6,768,512]{2,1,0:T(8,128)(2,1)}) custom-call(s32[4]{0:T(128)S(1)} %fusion.16.at, s32[10]{0:T(128)S(1)} %stack.64.slots, bf16[384,3072]{1,0:T(8,128)(2,1)} %refs_0_.4, bf16[384,3072]{1,0:T(8,128)(2,1)} %copy-done.8, bf16[384,3072]{1,0:T(8,128)(2,1)} %collective-permute-done.5.refs_2_, ...), custom_call_target="tpu_custom_call" | custom-call | bytes 1024 | tf_op jit(solution)/shard_map/partial_tangent/pallas_call | solution.py:190
  191.3 29.2 %bent.1 = f32[6,1024,512]{2,1,0:T(8,128)} custom-call(s32[4]{0:T(128)S(1)} %fusion.16.at, f32[1024,1]{1,0:T(8,128)S(1)} %copy.10.scale, s32[1024,3072]{1,0:T(8,128)} %codes.1, bf16[3072,3072]{1,0:T(8,128)(2,1)} %all-gather.2.cloned.1.call-done.down, bf16[1024,768]{1,0:T(8,128)(2,1)} %refs_0_.5, bf16[1024,768]{1,0:T(8,128)(2,1)} %copy-done.9, ...), custom_call_target="tpu_custom_call" | custom-call | bytes 1024 | tf_op jit(solution)/shard_map/bent/pallas_call | solution.py:121
  223.3 10.5 %front.4 = (bf16[1024,1024]{1,0:T(8,128)(2,1)}, bf16[1536,1024]{1,0:T(8,128)(2,1)}) custom-call(bf16[1024,768]{1,0:T(8,128)(2,1)S(1)} %collective-permute-done.14.refs_0_.shard, bf16[6,768,512]{2,1,0:T(8,128)(2,1)} %get-tuple-element.127.probe, f32[6,1024,512]{2,1,0:T(8,128)} %get-tuple-element.105.begun, f32[6,1024,512]{2,1,0:T(8,128)} %bent.1, ...), custom_call_target="tpu_custom_call" | custom-call | bytes 1024 | tf_op jit(solution)/shard_map/front/pallas_call | solution.py:229
  233.8 7.7 %front.5 = (bf16[1024,512]{1,0:T(8,128)(2,1)S(1)}, bf16[1536,512]{1,0:T(8,128)(2,1)}) custom-call(bf16[1024,768]{1,0:T(8,128)(2,1)} %copy-done, bf16[6,768,512]{2,1,0:T(8,128)(2,1)} %get-tuple-element.127.probe, f32[6,1024,512]{2,1,0:T(8,128)} %get-tuple-element.105.begun, f32[6,1024,512]{2,1,0:T(8,128)} %bent.1, bf16[1536,1024]{1,0:T(8,128)(2,1)} %get-tuple-element.107.other), custom_call_target="tpu_custom_call" | custom-call | bytes 1024 | tf_op jit(solution)/shard_map/front/pallas_call | solution.py:229
  244.2 8.6 %back.4 = (f32[2,1,384,512]{3,2,1,0:T(8,128)}, f32[1,2,384,512]{3,2,1,0:T(8,128)}, bf16[2,1,384,512]{3,2,1,0:T(8,128)(2,1)S(1)}, bf16[1,2,384,512]{3,2,1,0:T(8,128)(2,1)S(1)}) custom-call(s32[2]{0:T(128)S(1)} %pad_add_fusion.me, bf16[1536,1024]{1,0:T(8,128)(2,1)} %get-tuple-element.103.mine, bf16[1024,1024]{1,0:T(8,128)(2,1)} %get-tuple-element.113.mixed, ...), custom_call_target="tpu_custom_call" | custom-call | bytes 1024 | tf_op jit(solution)/shard_map/back/pallas_call | solution.py:290
  255.6 6.0 %back.5 = (f32[2,1,384,256]{3,2,1,0:T(8,128)S(1)}, f32[1,2,384,256]{3,2,1,0:T(8,128)}, bf16[2,1,384,256]{3,2,1,0:T(8,128)(2,1)S(1)}, bf16[1,2,384,256]{3,2,1,0:T(8,128)(2,1)S(1)}) custom-call(s32[2]{0:T(128)S(1)} %pad_add_fusion.me, bf16[1536,1024]{1,0:T(8,128)(2,1)} %get-tuple-element.103.mine, bf16[1024,512]{1,0:T(8,128)(2,1)} %copy-done.4, ...), custom_call_target="tpu_custom_call" | custom-call | bytes 1024 | tf_op jit(solution)/shard_map/back/pallas_call | solution.py:290
  264.1 7.7 %front.7 = (bf16[1024,512]{1,0:T(8,128)(2,1)S(1)}, bf16[1536,512]{1,0:T(8,128)(2,1)}) custom-call(bf16[1024,768]{1,0:T(8,128)(2,1)} %copy-done, bf16[6,768,512]{2,1,0:T(8,128)(2,1)} %get-tuple-element.127.probe, f32[6,1024,512]{2,1,0:T(8,128)} %get-tuple-element.105.begun, f32[6,1024,512]{2,1,0:T(8,128)} %bent.1, bf16[1536,1024]{1,0:T(8,128)(2,1)} %get-tuple-element.107.other), custom_call_target="tpu_custom_call" | custom-call | bytes 1024 | tf_op jit(solution)/shard_map/front/pallas_call | solution.py:229
  271.8 10.9 %front.6 = (bf16[1024,1024]{1,0:T(8,128)(2,1)}, bf16[1536,1024]{1,0:T(8,128)(2,1)}) custom-call(bf16[1024,768]{1,0:T(8,128)(2,1)S(1)} %copy-done.1, bf16[6,768,512]{2,1,0:T(8,128)(2,1)} %get-tuple-element.127.probe, f32[6,1024,512]{2,1,0:T(8,128)} %get-tuple-element.105.begun, f32[6,1024,512]{2,1,0:T(8,128)} %bent.1, bf16[1536,1024]{1,0:T(8,128)(2,1)} %get-tuple-element.107.other), custom_call_target="tpu_custom_call" | custom-call | bytes 1024 | tf_op jit(solution)/shard_map/front/pallas_call | solution.py:229
  291.3 8.6 %back.6 = (f32[2,1,384,512]{3,2,1,0:T(8,128)}, f32[1,2,384,512]{3,2,1,0:T(8,128)}, bf16[2,1,384,512]{3,2,1,0:T(8,128)(2,1)S(1)}, bf16[1,2,384,512]{3,2,1,0:T(8,128)(2,1)S(1)}) custom-call(s32[2]{0:T(128)S(1)} %pad_add_fusion.me, bf16[1536,1024]{1,0:T(8,128)(2,1)} %get-tuple-element.103.mine, bf16[1024,1024]{1,0:T(8,128)(2,1)} %get-tuple-element.142.mixed, ...), custom_call_target="tpu_custom_call" | custom-call | bytes 1024 | tf_op jit(solution)/shard_map/back/pallas_call | solution.py:290
  299.9 2.6 collective-permute-done.23
  305.2 6.0 %back.7 = (f32[2,1,384,256]{3,2,1,0:T(8,128)S(1)}, f32[1,2,384,256]{3,2,1,0:T(8,128)}, bf16[2,1,384,256]{3,2,1,0:T(8,128)(2,1)S(1)}, bf16[1,2,384,256]{3,2,1,0:T(8,128)(2,1)S(1)}) custom-call(s32[2]{0:T(128)S(1)} %pad_add_fusion.me, bf16[1536,1024]{1,0:T(8,128)(2,1)} %get-tuple-element.103.mine, bf16[1024,512]{1,0:T(8,128)(2,1)} %copy-done.3, ...), custom_call_target="tpu_custom_call" | custom-call | bytes 1024 | tf_op jit(solution)/shard_map/back/pallas_call | solution.py:290
  313.9 15.8 %collective-permute-done.29 = bf16[2,1,384,256]{3,2,1,0:T(8,128)(2,1)S(1)} collective-permute-done((bf16[2,1,384,256]{3,2,1,0:T(8,128)(2,1)S(1)}, bf16[2,1,384,256]{3,2,1,0:T(8,128)(2,1)S(1)}, u32[]{:S(2)}, u32[]{:S(2)}) %collective-permute-start.29) | collective-permute-done | bytes 393248 | tf_op jit(solution)/shard_map/ppermute | solution.py:362
  337.3 5.3 %collective-permute-done.31 = bf16[1,1,384,512]{3,2,1,0:T(8,128)(2,1)S(1)} collective-permute-done((bf16[1,1,384,512]{3,2,1,0:T(8,128)(2,1)S(1)}, bf16[1,1,384,512]{3,2,1,0:T(8,128)(2,1)S(1)}, u32[]{:S(2)}, u32[]{:S(2)}) %collective-permute-start.31) | collective-permute-done | bytes 393248 | tf_op jit(solution)/shard_map/ppermute | solution.py:362
  (150 shorter events, 59.6 us)
Async XLA Ops:
  6.5 184.8 %all-gather.2.cloned.1.call-start = ((), (), s32[]{:S(2)}) async-start(), calls=%async_computation | async-start | bytes 21233664 | tf_op jit(solution)/shard_map/all_gather | solution.py:390
  7.3 85.7 %collective-permute-start.5 = (bf16[384,3072]{1,0:T(8,128)(2,1)}, bf16[384,3072]{1,0:T(8,128)(2,1)}, u32[]{:S(2)}, u32[]{:S(2)}) collective-permute-start(bf16[384,3072]{1,0:T(8,128)(2,1)} %refs_0_.4), channel_id=1, source_target_pairs={{0,8},{4,12},{8,0},{12,4},{16,24},{20,28},{24,16},{28,20},{1,9},{5... | collective-permute-start | bytes 7077896 | tf_op jit(solution)/shard_map/ppermute | solution.py:362
  10.3 85.5 %collective-permute-start.7 = (bf16[384,3072]{1,0:T(8,128)(2,1)}, bf16[384,3072]{1,0:T(8,128)(2,1)}, u32[]{:S(2)}, u32[]{:S(2)}) collective-permute-start(bf16[384,3072]{1,0:T(8,128)(2,1)} %refs_0_.4), channel_id=1, source_target_pairs={{0,16},{4,20},{8,24},{12,28},{16,0},{20,4},{24,8},{28,12},{1,17},{... | collective-permute-start | bytes 7077896 | tf_op jit(solution)/shard_map/ppermute | solution.py:362
  11.8 38.4 %collective-permute-start = (bf16[1024,768]{1,0:T(8,128)(2,1)}, bf16[1024,768]{1,0:T(8,128)(2,1)S(1)}, u32[]{:S(2)}, u32[]{:S(2)}) collective-permute-start(bf16[1024,768]{1,0:T(8,128)(2,1)} %refs_0_.5), channel_id=1, source_target_pairs={{0,1},{1,3},{3,2},{2,0},{4,5},{5,7},{7,6},{6,4},{8,9},{9,11},{11,1... | collective-permute-start | bytes 4718600 | tf_op jit(solution)/shard_map/ppermute | solution.py:322
  13.4 68.8 %collective-permute-start.1 = (bf16[1024,768]{1,0:T(8,128)(2,1)S(1)}, bf16[1024,768]{1,0:T(8,128)(2,1)S(1)}, u32[]{:S(2)}, u32[]{:S(2)}) collective-permute-start(bf16[1024,768]{1,0:T(8,128)(2,1)S(1)} %copy-done.2), channel_id=1, source_target_pairs={{0,1},{1,3},{3,2},{2,0},{4,5},{5,7},{7,6},{6,4},{8,9},{9,11},{11,1... | collective-permute-start | bytes 4718600 | tf_op jit(solution)/shard_map/ppermute | solution.py:322
  16.0 83.6 %collective-permute-start.4 = (bf16[384,3072]{1,0:T(8,128)(2,1)}, bf16[384,3072]{1,0:T(8,128)(2,1)S(1)}, u32[]{:S(2)}, u32[]{:S(2)}) collective-permute-start(bf16[384,3072]{1,0:T(8,128)(2,1)} %refs_0_.4), channel_id=1, source_target_pairs={{0,4},{4,0},{8,12},{12,8},{16,20},{20,16},{24,28},{28,24},{1,5},{5... | collective-permute-start | bytes 7077896 | tf_op jit(solution)/shard_map/ppermute | solution.py:326
  83.3 38.3 %collective-permute-start.3 = (bf16[1024,768]{1,0:T(8,128)(2,1)S(1)}, bf16[1024,768]{1,0:T(8,128)(2,1)}, u32[]{:S(2)}, u32[]{:S(2)}) collective-permute-start(bf16[1024,768]{1,0:T(8,128)(2,1)S(1)} %collective-permute-done.1.refs_1_.refs_11_), channel_id=1, source_target_pairs={{0,1},{1,3},{3,2},{2,0},{4,5},{5,7},{7,6},{6,4},{8,9},{9,11},{11,1... | collective-permute-start | bytes 4718600 | tf_op jit(solution)/shard_map/ppermute | solution.py:322
  93.0 59.7 %collective-permute-start.6 = (bf16[384,3072]{1,0:T(8,128)(2,1)}, bf16[384,3072]{1,0:T(8,128)(2,1)}, u32[]{:S(2)}, u32[]{:S(2)}) collective-permute-start(bf16[384,3072]{1,0:T(8,128)(2,1)} %collective-permute-done.5.refs_2_), channel_id=1, source_target_pairs={{0,4},{4,0},{8,12},{12,8},{16,20},{20,16},{24,28},{28,24},{1,5},{5... | collective-permute-start | bytes 7077896 | tf_op jit(solution)/shard_map/ppermute | solution.py:326
  95.8 56.9 %collective-permute-start.8 = (bf16[384,3072]{1,0:T(8,128)(2,1)}, bf16[384,3072]{1,0:T(8,128)(2,1)}, u32[]{:S(2)}, u32[]{:S(2)}) collective-permute-start(bf16[384,3072]{1,0:T(8,128)(2,1)} %collective-permute-done.7.refs_4_), channel_id=1, source_target_pairs={{0,4},{4,0},{8,12},{12,8},{16,20},{20,16},{24,28},{28,24},{1,5},{5... | collective-permute-start | bytes 7077896 | tf_op jit(solution)/shard_map/ppermute | solution.py:326
  95.8 56.9 %collective-permute-start.2 = (bf16[1024,768]{1,0:T(8,128)(2,1)S(1)}, bf16[1024,768]{1,0:T(8,128)(2,1)}, u32[]{:S(2)}, u32[]{:S(2)}) collective-permute-start(bf16[1024,768]{1,0:T(8,128)(2,1)S(1)} %collective-permute-done.refs_1_), channel_id=1, source_target_pairs={{0,1},{1,3},{3,2},{2,0},{4,5},{5,7},{7,6},{6,4},{8,9},{9,11},{11,1... | collective-permute-start | bytes 4718600 | tf_op jit(solution)/shard_map/ppermute | solution.py:322
  99.6 57.3 %collective-permute-start.9 = (bf16[192,3072]{1,0:T(8,128)(2,1)}, bf16[192,3072]{1,0:T(8,128)(2,1)}, u32[]{:S(2)}, u32[]{:S(2)}) collective-permute-start(bf16[192,3072]{1,0:T(8,128)(2,1)} %slice.48), channel_id=1, source_target_pairs={{0,16},{4,20},{8,24},{12,28},{16,0},{20,4},{24,8},{28,12},{1,17},{... | collective-permute-start | bytes 3538952 | tf_op jit(solution)/shard_map/ppermute | solution.py:362
  121.7 41.3 %collective-permute-start.11 = (bf16[192,3072]{1,0:T(8,128)(2,1)}, bf16[192,3072]{1,0:T(8,128)(2,1)}, u32[]{:S(2)}, u32[]{:S(2)}) collective-permute-start(bf16[192,3072]{1,0:T(8,128)(2,1)} %slice.49), channel_id=1, source_target_pairs={{0,8},{4,12},{8,0},{12,4},{16,24},{20,28},{24,16},{28,20},{1,9},{5... | collective-permute-start | bytes 3538952 | tf_op jit(solution)/shard_map/ppermute | solution.py:362
  152.7 38.6 %collective-permute-start.13 = (bf16[1024,768]{1,0:T(8,128)(2,1)}, bf16[1024,768]{1,0:T(8,128)(2,1)}, u32[]{:S(2)}, u32[]{:S(2)}) collective-permute-start(bf16[1024,768]{1,0:T(8,128)(2,1)} %collective-permute-done.2.refs_2_), channel_id=1, source_target_pairs={{0,1},{1,3},{3,2},{2,0},{4,5},{5,7},{7,6},{6,4},{8,9},{9,11},{11,1... | collective-permute-start | bytes 4718600 | tf_op jit(solution)/shard_map/ppermute | solution.py:322
  153.4 67.9 %collective-permute-start.14 = (bf16[1024,768]{1,0:T(8,128)(2,1)}, bf16[1024,768]{1,0:T(8,128)(2,1)S(1)}, u32[]{:S(2)}, u32[]{:S(2)}) collective-permute-start(bf16[1024,768]{1,0:T(8,128)(2,1)} %collective-permute-done.3.refs_2_.refs_12_), channel_id=1, source_target_pairs={{0,1},{1,3},{3,2},{2,0},{4,5},{5,7},{7,6},{6,4},{8,9},{9,11},{11,1... | collective-permute-start | bytes 4718600 | tf_op jit(solution)/shard_map/ppermute | solution.py:322
  252.9 29.8 %collective-permute-start.16 = (bf16[2,1,384,512]{3,2,1,0:T(8,128)(2,1)S(1)}, bf16[2,1,384,512]{3,2,1,0:T(8,128)(2,1)S(1)}, u32[]{:S(2)}, u32[]{:S(2)}) collective-permute-start(bf16[2,1,384,512]{3,2,1,0:T(8,128)(2,1)S(1)} %get-tuple-element.119), channel_id=1, source_target_pairs={{0,8},{4,12},{8,0},{12,4},{16,24},{20,28},{24,16},{28,20},{1,9},{5... | collective-permute-start | bytes 2359304 | tf_op jit(solution)/shard_map/ppermute | solution.py:362
  253.4 29.3 %collective-permute-start.17 = (bf16[1,2,384,512]{3,2,1,0:T(8,128)(2,1)S(1)}, bf16[1,2,384,512]{3,2,1,0:T(8,128)(2,1)S(1)}, u32[]{:S(2)}, u32[]{:S(2)}) collective-permute-start(bf16[1,2,384,512]{3,2,1,0:T(8,128)(2,1)S(1)} %get-tuple-element.120), channel_id=1, source_target_pairs={{0,16},{4,20},{8,24},{12,28},{16,0},{20,4},{24,8},{28,12},{1,17},{... | collective-permute-start | bytes 2359304 | tf_op jit(solution)/shard_map/ppermute | solution.py:362
  261.6 21.1 %collective-permute-start.19 = (bf16[2,1,384,256]{3,2,1,0:T(8,128)(2,1)S(1)}, bf16[2,1,384,256]{3,2,1,0:T(8,128)(2,1)S(1)}, u32[]{:S(2)}, u32[]{:S(2)}) collective-permute-start(bf16[2,1,384,256]{3,2,1,0:T(8,128)(2,1)S(1)} %get-tuple-element.125), channel_id=1, source_target_pairs={{0,8},{4,12},{8,0},{12,4},{16,24},{20,28},{24,16},{28,20},{1,9},{5... | collective-permute-start | bytes 1179656 | tf_op jit(solution)/shard_map/ppermute | solution.py:362
  262.6 20.2 %collective-permute-start.20 = (bf16[1,2,384,256]{3,2,1,0:T(8,128)(2,1)S(1)}, bf16[1,2,384,256]{3,2,1,0:T(8,128)(2,1)S(1)}, u32[]{:S(2)}, u32[]{:S(2)}) collective-permute-start(bf16[1,2,384,256]{3,2,1,0:T(8,128)(2,1)S(1)} %get-tuple-element.126), channel_id=1, source_target_pairs={{0,16},{4,20},{8,24},{12,28},{16,0},{20,4},{24,8},{28,12},{1,17},{... | collective-permute-start | bytes 1179656 | tf_op jit(solution)/shard_map/ppermute | solution.py:362
  284.0 21.3 %collective-permute-start.28 = (bf16[1536,512]{1,0:T(8,128)(2,1)}, bf16[1536,512]{1,0:T(8,128)(2,1)}, u32[]{:S(2)}, u32[]{:S(2)}) collective-permute-start(bf16[1536,512]{1,0:T(8,128)(2,1)} %get-tuple-element.157), channel_id=1, source_target_pairs={{0,4},{4,0},{8,12},{12,8},{16,20},{20,16},{24,28},{28,24},{1,5},{5... | collective-permute-start | bytes 4718600 | tf_op jit(solution)/shard_map/ppermute | solution.py:326
  287.2 15.5 %collective-permute-start.21 = (bf16[1,1,384,512]{3,2,1,0:T(8,128)(2,1)S(1)}, bf16[1,1,384,512]{3,2,1,0:T(8,128)(2,1)S(1)}, u32[]{:S(2)}, u32[]{:S(2)}) collective-permute-start(bf16[1,1,384,512]{3,2,1,0:T(8,128)(2,1)S(1)} %get-tuple-element.138), channel_id=1, source_target_pairs={{0,16},{4,20},{8,24},{12,28},{16,0},{20,4},{24,8},{28,12},{1,17},{... | collective-permute-start | bytes 1179656 | tf_op jit(solution)/shard_map/ppermute | solution.py:362
  302.8 27.8 %collective-permute-start.26 = (bf16[2,1,384,512]{3,2,1,0:T(8,128)(2,1)S(1)}, bf16[2,1,384,512]{3,2,1,0:T(8,128)(2,1)}, u32[]{:S(2)}, u32[]{:S(2)}) collective-permute-start(bf16[2,1,384,512]{3,2,1,0:T(8,128)(2,1)S(1)} %get-tuple-element.154), channel_id=1, source_target_pairs={{0,8},{4,12},{8,0},{12,4},{16,24},{20,28},{24,16},{28,20},{1,9},{5... | collective-permute-start | bytes 2359304 | tf_op jit(solution)/shard_map/ppermute | solution.py:362
  303.9 26.6 %collective-permute-start.27 = (bf16[1,2,384,512]{3,2,1,0:T(8,128)(2,1)S(1)}, bf16[1,2,384,512]{3,2,1,0:T(8,128)(2,1)}, u32[]{:S(2)}, u32[]{:S(2)}) collective-permute-start(bf16[1,2,384,512]{3,2,1,0:T(8,128)(2,1)S(1)} %get-tuple-element.155), channel_id=1, source_target_pairs={{0,16},{4,20},{8,24},{12,28},{16,0},{20,4},{24,8},{28,12},{1,17},{... | collective-permute-start | bytes 2359304 | tf_op jit(solution)/shard_map/ppermute | solution.py:362
  311.3 18.4 %collective-permute-start.29 = (bf16[2,1,384,256]{3,2,1,0:T(8,128)(2,1)S(1)}, bf16[2,1,384,256]{3,2,1,0:T(8,128)(2,1)S(1)}, u32[]{:S(2)}, u32[]{:S(2)}) collective-permute-start(bf16[2,1,384,256]{3,2,1,0:T(8,128)(2,1)S(1)} %get-tuple-element.158), channel_id=1, source_target_pairs={{0,8},{4,12},{8,0},{12,4},{16,24},{20,28},{24,16},{28,20},{1,9},{5... | collective-permute-start | bytes 1179656 | tf_op jit(solution)/shard_map/ppermute | solution.py:362
  312.6 18.0 %collective-permute-start.30 = (bf16[1,2,384,256]{3,2,1,0:T(8,128)(2,1)S(1)}, bf16[1,2,384,256]{3,2,1,0:T(8,128)(2,1)S(1)}, u32[]{:S(2)}, u32[]{:S(2)}) collective-permute-start(bf16[1,2,384,256]{3,2,1,0:T(8,128)(2,1)S(1)} %get-tuple-element.159), channel_id=1, source_target_pairs={{0,16},{4,20},{8,24},{12,28},{16,0},{20,4},{24,8},{28,12},{1,17},{... | collective-permute-start | bytes 1179656 | tf_op jit(solution)/shard_map/ppermute | solution.py:362
  (46 other events, 442.5 us)
Sparse Core Ops, SparseCore 0:
  9.2 157.9 all-gather.1
